TPU v7x, 32 devices: a whole 2x2x4 slice. The times are simulated.
32 devices in a mesh: grp: 2 (over y), atoms: 4 (over z), feat: 2 (over x), rep: 2 (over core).
Axes of the slice: x: 2, y: 2, z: 4, core: 2. Of those that a mesh axis runs over, the one named last changes fastest.
Arguments:
- atom_coords: bfloat16 [4, 2048, 3, 3072], P(('grp', 'rep'), None, None, 'atoms'), parts along dimension 0, may hold values from -9 to 9
- atom_pairs: int32 [2, 1024], P(None, 'feat'), may hold values from 0 to 3071, as said below
- traj_ids: int32 [4, 2048], P(('grp', 'rep')), parts along dimension 0, may hold values from 0 to 7, never falling along the last dimension, each value on 1 to 512 neighbouring positions
Outputs:
- corr_inst: float32 [2048, 1024], P(('grp', 'atoms', 'rep'), 'feat'), parts along dimension 0
- corr_lag: float32 [2048, 1024], P(('grp', 'atoms', 'rep'), 'feat'), parts along dimension 0
- projections: float32 [4, 2048, 1024], P(('grp', 'rep'), 'atoms', 'feat'), parts along dimension 0
There are 2 independent parts, one for each index of `grp`. A program takes and returns all parts, laid end to end along the dimension named above; an argument that names none is the same for every part. Nothing has to cross between parts.
Inputs may be any that keep to these rules, and one draw needn't show every extreme that they name: `atom_pairs`: the two atoms of a feature differ. `traj_ids`: trajectory numbers never fall along a replica stream; some trajectory holds exactly 512 frames.
All inputs are finite; a program needn't handle non-finite values.
Results may differ from a plain program's by a relative error of at most 0.0003.
Values may be sent and summed in bfloat16 or wider, within the bound.
No kernel may reach another device: no remote copies, remote signals or barrier semaphores. Data moves between devices by JAX's collectives and lax.ppermute only.
A program may use at most 128 MiB of HBM per device.

v0:
```python
import jax
import jax.numpy as jnp
from jax import lax
from jax.sharding import PartitionSpec as P

LAG = 10


def passed_along(block, axis, distance):
    devices = range(lax.axis_size(axis))
    route = [(i - distance, i) for i in devices if i - distance in devices]
    return lax.ppermute(block, axis, route)


def featurize(positions, pairs):
    first = jnp.take(positions, pairs[0], axis=2)
    second = jnp.take(positions, pairs[1], axis=2)
    delta = first - second
    return jnp.sqrt(jnp.sum(delta * delta, axis=1) + 0.01)


def cross_moment(left, right):
    return lax.dot_general(
        left,
        right,
        (((0,), (0,)), ((), ())),
        precision=lax.Precision.HIGHEST,
        preferred_element_type=jnp.float32,
    )


def shards(atom_coords, atom_pairs, traj_ids):
    atom_groups = lax.axis_size("atoms")
    feat_groups = lax.axis_size("feat")
    frames_here = atom_coords.shape[1] // atom_groups
    width_atoms = atom_coords.shape[3]
    atom_index = lax.axis_index("atoms")
    feat_index = lax.axis_index("feat")
    col_width = atom_pairs.shape[1]
    used_pairs = lax.all_gather(atom_pairs, "feat", axis=1, tiled=True)
    quarter = frames_here // feat_groups
    grouped = atom_coords.reshape(1, atom_groups, feat_groups, quarter, 3, width_atoms)
    blocks = lax.dynamic_slice_in_dim(grouped, feat_index, 1, 2).reshape(
        1, atom_groups, quarter, 3, width_atoms
    )
    computed = featurize(
        lax.all_to_all(blocks, "atoms", split_axis=1, concat_axis=4, tiled=True)[0, 0].astype(
            jnp.float32
        ),
        used_pairs,
    )
    every = lax.all_gather(computed, "feat", axis=0, tiled=True)
    own = lax.dynamic_slice_in_dim(every, feat_index * col_width, col_width, 1)
    incoming = passed_along(own[:LAG], "atoms", -1)
    future = jnp.concatenate([own[LAG:], incoming], 0)
    ids = jnp.concatenate([traj_ids[0], jnp.full((LAG,), -1, jnp.int32)])
    offset = atom_index * frames_here
    ids_now = lax.dynamic_slice_in_dim(ids, offset, frames_here)
    ids_later = lax.dynamic_slice_in_dim(ids, offset + LAG, frames_here)
    valid = (ids_now == ids_later).astype(jnp.float32)[:, None]
    count, total_now, total_next = lax.psum(
        (jnp.sum(valid), jnp.sum(valid * every, 0), jnp.sum(valid * future, 0)), ("atoms", "rep")
    )
    mean_now = total_now / count
    mean_next = total_next / count
    centered = every - mean_now
    own_centered = lax.dynamic_slice_in_dim(centered, feat_index * col_width, col_width, 1)
    future_centered = future - mean_next
    right_side = jnp.concatenate([valid * own_centered, valid * future_centered], 1)
    spread_now_part = jnp.sum(valid * centered * centered, 0)
    spread_next_part = jnp.sum(valid * future_centered * future_centered, 0)
    row_count = every.shape[1] // lax.axis_size(("atoms", "rep"))
    row_start = lax.axis_index(("atoms", "rep")) * row_count
    local_moments = cross_moment(centered, right_side)
    summed, spread_now, spread_next = lax.psum(
        (local_moments, spread_now_part, spread_next_part), ("atoms", "rep")
    )
    mine = lax.dynamic_slice_in_dim(summed, row_start, row_count, 0)
    scale_now = 1.0 / jnp.sqrt(spread_now / count + 1e-05)
    scale_next = 1.0 / jnp.sqrt(spread_next / count + 1e-05)
    scale_rows = lax.dynamic_slice_in_dim(scale_now, row_start, row_count)
    scale_cols = lax.dynamic_slice_in_dim(scale_now, feat_index * col_width, col_width)
    corr_inst = mine[:, :col_width] / count * scale_rows[:, None] * scale_cols[None, :]
    corr_lag = mine[:, col_width:] / count * scale_rows[:, None] * scale_next[None, :]
    projections = (own_centered * scale_cols)[None]
    return (corr_inst, corr_lag, projections)


def solution(mesh):
    placed = (P(("grp", "rep"), None, None, "atoms"), P(None, "feat"), P(("grp", "rep"), None))
    return jax.shard_map(
        shards,
        mesh=mesh,
        in_specs=placed,
        out_specs=(
            P(("grp", "atoms", "rep"), "feat"),
            P(("grp", "atoms", "rep"), "feat"),
            P(("grp", "rep"), "atoms", "feat"),
        ),
        check_vma=False,
    )
```

profile of v0, /device:TPU:9, one launch (start us, length us, event | category | flops | bytes accessed | tf_op | source)
XLA Modules:
  0.0 381.9 jit_solution(13211677239903812215)
XLA Ops:
  7.2 4.8 %constant_dynamic-slice_fusion.1 = bf16[1,4,1,256,3,768]{5,3,2,1,4,0:T(8,128)(2,1)} fusion(bf16[1,4,2,256,3,768]{5,3,2,1,4,0:T(8,128)(2,1)} %bitcast.24, s32[]{:T(128)S(6)} %select_n.25), kind=kLoop, calls=%fused_computation.42 | loop fusion | bytes 9437188 | tf_op jit(solution)/shard_map/dynamic_slice | solution.py:43
  12.0 6.6 %copy.14 = bf16[1,4,1,256,3,768]{3,5,4,1,2,0:T(8,128)(2,1)} copy(bf16[1,4,1,256,3,768]{5,3,2,1,4,0:T(8,128)(2,1)} %constant_dynamic-slice_fusion.1) | data formatting | bytes 9437184
  18.6 0.0 copy-start.2
  18.6 5.1 %all-to-all-start = ((bf16[1,4,256,3,768]{2,4,3,0,1:T(8,128)(2,1)}), bf16[1,4,256,3,768]{2,4,3,0,1:T(8,128)(2,1)}, u32[]{:S(2)}, u32[]{:S(2)}) async-start(bf16[1,4,256,3,768]{2,4,3,0,1:T(8,128)(2,1)} %bitcast.23), calls=%async_computation | async-start | bytes 9437184 | tf_op jit(solution)/shard_map/all_to_all | solution.py:47
  23.7 0.0 all-gather.2.cloned.1.call-start
  23.7 0.0 copy-done.2
  23.8 3.5 all_gather.6
  27.3 97.0 %all-to-all-done = bf16[1,4,256,3,768]{2,4,3,0,1:T(8,128)(2,1)} async-done(((bf16[1,4,256,3,768]{2,4,3,0,1:T(8,128)(2,1)}), bf16[1,4,256,3,768]{2,4,3,0,1:T(8,128)(2,1)}, u32[]{:S(2)}, u32[]{:S(2)}) %all-to-all-start) | async-done | bytes 4718624 | tf_op jit(solution)/shard_map/all_to_all | solution.py:47
  124.3 3.3 bitcast_convert_fusion
  127.6 22.2 %copy.11 = f32[256,3,3072]{0,1,2:T(4,128)} copy(f32[256,3,3072]{0,2,1:T(8,128)S(1)} %bitcast.22) | data formatting | bytes 18874368 | tf_op jit(solution)/shard_map/convert_element_type | solution.py:47
  149.8 14.2 %gather_fusion = f32[1024,256,3]{1,2,0:T(4,128)} fusion(f32[256,3,3072]{0,1,2:T(4,128)} %copy.11, s32[1024]{0:T(1024)S(1)} %fusion.11), kind=kCustom, calls=%fused_computation.clone | custom fusion | bytes 6295552 | tf_op jit(solution)/shard_map/jit(_take)/gather | solution.py:16
  164.0 14.2 %gather_fusion.1 = f32[1024,256,3]{1,2,0:T(4,128)} fusion(f32[256,3,3072]{0,1,2:T(4,128)} %copy.11, s32[1024]{0:T(1024)S(1)} %fusion.12), kind=kCustom, calls=%fused_computation.1.clone | custom fusion | bytes 6295552 | tf_op jit(solution)/shard_map/jit(_take)/gather | solution.py:17
  178.2 0.0 copy-start.1
  178.2 9.0 %fusion.1 = f32[256,1024]{0,1:T(8,128)S(1)} fusion(f32[1024,256,3]{1,2,0:T(4,128)} %gather_fusion.1, f32[1024,256,3]{1,2,0:T(4,128)} %gather_fusion, pred[1024]{0:T(1024)(128)(4,1)S(1)} %get-tuple-element.24, pred[1024]{0:T(1024)(128)(4,1)S(1)} %get-tuple-element.25), kind=kLoop, calls=%fused_computation.5 | loop fusion | flops 3670016 | bytes 7342080 | tf_op jit(solution)/shard_map/reduce_sum | solution.py:19
  187.3 1.2 add_sqrt_fusion
  188.5 0.0 all-gather.2.cloned.1.call-update
  188.5 0.0 all-reduce.5.cloned.1.call-start
  188.6 0.0 copy-done.1
  188.6 0.7 fusion.16
  189.3 35.7 %all-gather.2.cloned.1.call-done = f32[512,1024]{0,1:T(8,128)} async-done(((f32[256,1024]{0,1:T(8,128)}), f32[512,1024]{0,1:T(8,128)}) %all-gather.2.cloned.1.call-update) | async-done | bytes 2097168 | tf_op jit(solution)/shard_map/all_gather | solution.py:52
  224.9 1.0 constant_dynamic-slice_fusion
  225.9 2.2 collective-permute-start
  228.1 1.8 multiply_reduce_fusion
  229.9 1.6 dynamic-slice
  231.5 3.5 collective-permute-done
  235.0 0.2 multiply_reduce_fusion.2
  235.2 12.0 %all-reduce.2 = (f32[1024]{0:T(1024)S(1)}, f32[]{:T(128)}, f32[512]{0:T(512)S(1)}) all-reduce(f32[1024]{0:T(1024)S(1)} %multiply_reduce_fusion, f32[]{:T(128)} %get-tuple-element.14, f32[512]{0:T(512)S(1)} %multiply_reduce_fusion.2), channel_id=1, replica_groups=mesh['grp'=2,'atoms'=4,'feat'=2,'rep'=2] {'atoms','rep'}, use_global_device_ids=true, to_apply=%region_2.4 | all-reduce | flops 1537 | bytes 12296 | tf_op jit(solution)/shard_map/psum | solution.py:61
  247.2 0.6 broadcast_divide_fusion.1
  247.8 0.6 broadcast_divide_fusion
  248.4 0.3 multiply_reduce_fusion.1
  248.8 2.1 fusion.2
  250.8 13.8 %all-reduce.1 = (f32[1024]{0:T(1024)S(1)}, f32[512]{0:T(512)S(1)}) all-reduce(f32[1024]{0:T(1024)S(1)} %get-tuple-element.12, f32[512]{0:T(512)S(1)} %get-tuple-element.20), channel_id=1, replica_groups=mesh['grp'=2,'atoms'=4,'feat'=2,'rep'=2] {'atoms','rep'}, use_global_device_ids=true, to_apply=%region_9.11 | all-reduce | flops 1536 | bytes 12288 | tf_op jit(solution)/shard_map/psum | solution.py:75
  264.7 0.6 add_rsqrt_fusion
  265.2 0.1 dynamic_slice.31
  265.3 1.1 multiply_bitcast_fusion
  266.4 8.6 %fusion.3 = f32[1024,1024]{1,0:T(8,128)} fusion(f32[512,1024]{0,1:T(8,128)S(1)} %get-tuple-element.13, f32[512,512]{0,1:T(8,128)S(1)} %get-tuple-element.21, f32[512,512]{0,1:T(8,128)S(1)} %get-tuple-element.19), kind=kOutput, calls=%fused_computation.8 | convolution fusion | flops 6442975232 | bytes 8388608 | tf_op jit(solution)/shard_map/dot_general | solution.py:23
  275.0 0.0 copy-start
  275.0 0.0 all-reduce.5.cloned.1.call-update
  275.1 0.1 dynamic_slice.30
  275.1 1.1 copy-done
  276.3 1.3 copy.13
  277.6 0.6 add_rsqrt_fusion.1
  278.1 94.4 %all-reduce.5.cloned.1.call-done = f32[1024,1024]{1,0:T(8,128)} async-done(((f32[1024,1024]{1,0:T(8,128)}), f32[1024,1024]{1,0:T(8,128)}) %all-reduce.5.cloned.1.call-update) | async-done | bytes 4194320 | tf_op jit(solution)/shard_map/psum | solution.py:75
  372.5 2.5 fusion.8
  (4 shorter events, 0.0 us)
Async XLA Ops:
  18.6 5.1 %copy-start.2 = (s32[2,512]{1,0:T(2,128)S(1)}, s32[2,512]{1,0:T(2,128)}, u32[]{:S(2)}) copy-start(s32[2,512]{1,0:T(2,128)} %param.6) | copy-start | bytes 12292
  18.6 105.7 %all-to-all-start = ((bf16[1,4,256,3,768]{2,4,3,0,1:T(8,128)(2,1)}), bf16[1,4,256,3,768]{2,4,3,0,1:T(8,128)(2,1)}, u32[]{:S(2)}, u32[]{:S(2)}) async-start(bf16[1,4,256,3,768]{2,4,3,0,1:T(8,128)(2,1)} %bitcast.23), calls=%async_computation | async-start | bytes 9437184 | tf_op jit(solution)/shard_map/all_to_all | solution.py:47
  23.7 201.3 %all-gather.2.cloned.1.call-start = ((), (), s32[]{:S(2)}) async-start(), calls=%async_computation.1 | async-start | bytes 3145728 | tf_op jit(solution)/shard_map/all_gather | solution.py:52
  178.2 10.4 %copy-start.1 = (s32[1,2048]{1,0:T(1,128)S(1)}, s32[1,2048]{1,0:T(1,128)}, u32[]{:S(2)}) copy-start(s32[1,2048]{1,0:T(1,128)} %param.7) | copy-start | bytes 24580
  188.5 184.0 %all-reduce.5.cloned.1.call-start = ((), (), s32[]{:S(2)}) async-start(), calls=%async_computation.2 | async-start | bytes 8388608 | tf_op jit(solution)/shard_map/psum | solution.py:75
  225.9 9.1 %collective-permute-start = (f32[10,512]{0,1:T(8,128)S(1)}, f32[10,512]{0,1:T(8,128)S(1)}, u32[]{:S(2)}, u32[]{:S(2)}) collective-permute-start(f32[10,512]{0,1:T(8,128)S(1)} %constant_dynamic-slice_fusion), channel_id=1, source_target_pairs={{4,0},{8,4},{12,8},{5,1},{9,5},{13,9},{6,2},{10,6},{14,10},{7,3},{... | collective-permute-start | bytes 61448 | tf_op jit(solution)/shard_map/ppermute | solution.py:12
  275.0 1.2 copy-start
Sparse Core Ops, SparseCore 0:
  188.6 36.2 all-gather.1
  275.2 97.3 all-reduce.4
where the time goes:
time: 384 us; the launch traced here: 382 us
  waiting for transfers between devices  231 us (60%)
  local copies, waits for them, and re-layouts  67.2 us (18%)
  blocking collectives  29.3 us (8%)
  other arithmetic  24.6 us (6%)
  between operations  14.2 us (4%)
  matrix products  8.6 us (2%)
  starting transfers between devices  7.32 us (2%)
    all_to_all x1, waiting for transfers between devices, shards(): lax.all_to_all(blocks, 'atoms', split_axis=1, concat_axis=4, tiled=True)  97 us
    psum x1, waiting for transfers between devices, shards(): lax.psum((local_moments, spread_now_part, spread_next_part), ('atoms', 'r...  94.4 us
    all_gather x1, waiting for transfers between devices, shards(): every = lax.all_gather(computed, 'feat', axis=0, tiled=True)  35.7 us
    convert_element_type x1, local copies, waits for them, and re-layouts, shards(): lax.all_to_all(blocks, 'atoms', split_axis=1, concat_axis=4, tiled=True)  22.2 us
    gather x1, local copies, waits for them, and re-layouts, featurize(): second = jnp.take(positions, pairs[1], axis=2)  14.2 us
    gather x1, local copies, waits for them, and re-layouts, featurize(): first = jnp.take(positions, pairs[0], axis=2)  14.2 us
    psum x1, blocking collectives, shards(): lax.psum((local_moments, spread_now_part, spread_next_part), ('atoms', 'r...  13.8 us
    psum x1, blocking collectives, shards(): lax.psum((jnp.sum(valid), jnp.sum(valid * every, 0), jnp.sum(valid * futu...  12 us
  transfers between devices with their start and end apart: 4, of which 4 were waited for; matrix products, arithmetic and copies ran while one was open for 2% of the time, Pallas kernels for 0%

commit v1 on v0

v1 whole, which is shorter than its diff:
```python
import functools

import jax
import jax.numpy as jnp
from jax import lax
from jax.experimental import pallas as pl
from jax.experimental.pallas import tpu as pltpu
from jax.sharding import PartitionSpec as P

LAG = 10
HALO = 16
CHUNK = 64
VMEM_LIMIT = 48 * 1024 * 1024
F32 = jnp.float32
BF16 = jnp.bfloat16


def rotated(block, axis, shift):
    size = lax.axis_size(axis)
    return lax.ppermute(block, axis, [(i, (i + shift) % size) for i in range(size)])


def passed_down(block, axis):
    return lax.ppermute(block, axis, [(i + 1, i) for i in range(lax.axis_size(axis) - 1)])


def params():
    return pltpu.CompilerParams(vmem_limit_bytes=VMEM_LIMIT)


def pick_kernel(groups, cap, place_ref, *refs):
    del place_ref
    blocks, rank_ref, outs = refs[:groups], refs[groups], refs[groups + 1 :]
    width = blocks[0].shape[2]
    slots = lax.broadcasted_iota(jnp.int32, (width, cap), 1)
    chosen = (rank_ref[...] == slots).astype(F32).astype(BF16)
    half = CHUNK // 2
    for block, out in zip(blocks, outs):
        rows = block[...].reshape(3 * CHUNK, width)
        picked = jnp.dot(rows, chosen, preferred_element_type=F32).astype(BF16)
        picked = picked.reshape(3, CHUNK, cap)
        out[:, :, 0:cap] = picked[:, :half, :]
        out[:, :, cap : 2 * cap] = picked[:, half:, :]


def pick(coords, rank, cap, place, chunk, groups, sides):
    frames = coords.shape[1] // groups
    per_group = frames // CHUNK

    def at(shift):
        def index(step, where):
            there = lax.rem(where[0] + shift, groups)
            return (0, there * per_group + chunk * sides + where[1], 0)

        return index

    width = coords.shape[2]
    shape = jax.ShapeDtypeStruct((3, CHUNK // 2, 2 * cap), BF16)
    return pl.pallas_call(
        functools.partial(pick_kernel, groups, cap),
        grid_spec=pltpu.PrefetchScalarGridSpec(
            num_scalar_prefetch=1,
            grid=(1,),
            in_specs=[pl.BlockSpec((3, CHUNK, width), at(s)) for s in range(groups)]
            + [pl.BlockSpec((width, 1), lambda step, where: (0, 0))],
            out_specs=[
                pl.BlockSpec((3, CHUNK // 2, 2 * cap), lambda step, where: (0, 0, 0))
                for _ in range(groups)
            ],
        ),
        out_shape=[shape] * groups,
        compiler_params=params(),
        name="pick",
    )(place, *([coords] * groups), rank)


def distance_kernel(groups, cap, *refs):
    blocks, signs_ref, out, joined = refs[:groups], refs[groups], refs[groups + 1], refs[groups + 2]
    half = CHUNK // 2
    for s, block in enumerate(blocks):
        for k in range(3):
            joined[k * CHUNK : k * CHUNK + half, s * cap : (s + 1) * cap] = block[k, :, 0:cap]
            joined[k * CHUNK + half : (k + 1) * CHUNK, s * cap : (s + 1) * cap] = block[
                k, :, cap : 2 * cap
            ]
    delta = jnp.dot(joined[...], signs_ref[...], preferred_element_type=F32)
    square = delta * delta
    total = square[:CHUNK] + square[CHUNK : 2 * CHUNK] + square[2 * CHUNK :]
    out[...] = jnp.sqrt(total + 0.01)


def distances(blocks, signs, cap):
    groups = len(blocks)
    return pl.pallas_call(
        functools.partial(distance_kernel, groups, cap),
        out_shape=jax.ShapeDtypeStruct((CHUNK, signs.shape[1]), F32),
        scratch_shapes=[pltpu.VMEM((3 * CHUNK, groups * cap), BF16)],
        compiler_params=params(),
        name="distances",
    )(*blocks, signs)


def split_in_two(value):
    high = value.astype(BF16)
    return high, (value - high.astype(F32)).astype(BF16)


def moment_kernel(chunks, sides, place_ref, *refs):
    pieces = refs[: chunks * sides]
    halo_ref, valid_ref, shift_ref, out, own_out, sums_out, sums_next_out, every, own = refs[
        chunks * sides :
    ]
    frames, feats = every.shape
    cols = own.shape[1]
    side = place_ref[1]
    shift = shift_ref[...]
    for j in range(chunks):
        for s in range(sides):
            there = lax.rem(side + sides - s, sides)
            row = pl.multiple_of((j * sides + there) * CHUNK, CHUNK)
            every[pl.ds(row, CHUNK), :] = pieces[j * sides + s][...] - shift
    for s in range(sides):

        @pl.when(side == s)
        def _():
            own[0:frames, :] = every[:, s * cols : (s + 1) * cols]
            own[frames : frames + HALO, :] = halo_ref[...] - shift[:, s * cols : (s + 1) * cols]

    own_out[...] = own[0:frames, :]
    valid = valid_ref[...]
    now = every[...]
    weighed = valid * now
    sums_out[0:1, :] = jnp.sum(weighed, 0, keepdims=True)
    sums_out[1:2, :] = jnp.sum(weighed * now, 0, keepdims=True)
    later = own[LAG : LAG + frames, :]
    weighed_later = valid * later
    sums_next_out[0:1, :] = jnp.sum(weighed_later, 0, keepdims=True)
    sums_next_out[1:2, :] = jnp.sum(weighed_later * later, 0, keepdims=True)
    left_high, left_low = split_in_two(now)
    left_high, left_low = left_high.T, left_low.T
    for part, right in enumerate((valid * own[0:frames, :], weighed_later)):
        right_high, right_low = split_in_two(right)
        total = jnp.dot(left_high, right_high, preferred_element_type=F32)
        total += jnp.dot(left_high, right_low, preferred_element_type=F32)
        total += jnp.dot(left_low, right_high, preferred_element_type=F32)
        out[:, part * cols : (part + 1) * cols] = total


def moments(pieces, halo, valid, shift, place, chunks, sides):
    frames, feats = chunks * sides * CHUNK, shift.shape[1]
    cols = halo.shape[1]
    vmem = pl.BlockSpec(memory_space=pltpu.VMEM)
    return pl.pallas_call(
        functools.partial(moment_kernel, chunks, sides),
        in_specs=[pl.BlockSpec(memory_space=pltpu.SMEM)] + [vmem] * (len(pieces) + 3),
        out_specs=[vmem] * 4,
        out_shape=[
            jax.ShapeDtypeStruct((feats, 2 * cols), F32),
            jax.ShapeDtypeStruct((frames, cols), F32),
            jax.ShapeDtypeStruct((2, feats), F32),
            jax.ShapeDtypeStruct((2, cols), F32),
        ],
        scratch_shapes=[pltpu.VMEM((frames, feats), F32), pltpu.VMEM((frames + HALO, cols), F32)],
        compiler_params=params(),
        name="moments",
    )(place, *pieces, halo, valid, shift)


def with_cap(cap, coords, rank_all, used_pairs, valid, place):
    groups, sides = lax.axis_size("atoms"), lax.axis_size("feat")
    atom_index, feat_index = place[0], place[1]
    width = coords.shape[2]
    frames = coords.shape[1] // groups
    feats = used_pairs.shape[1]
    cols = feats // sides
    chunks = frames // (sides * CHUNK)
    ring = ("atoms", "rep")

    rank = lax.dynamic_index_in_dim(rank_all, atom_index, 0, keepdims=False)[:, None]
    picked = [pick(coords, rank, cap, place, j, groups, sides) for j in range(chunks)]
    arrived = [
        [picked[j][0]] + [rotated(picked[j][s], "atoms", s) for s in range(1, groups)]
        for j in range(chunks)
    ]

    atoms = lax.broadcasted_iota(jnp.int32, (groups, 1, width), 0) * width
    atoms = atoms + lax.broadcasted_iota(jnp.int32, (groups, 1, width), 2)
    slots = lax.broadcasted_iota(jnp.int32, (groups, cap, width), 1)
    listed = jnp.max(jnp.where(rank_all[:, None, :] == slots, atoms, -1), axis=2)
    order = lax.rem(atom_index + groups - jnp.arange(groups, dtype=jnp.int32), groups)
    listed = jnp.take(listed, order, axis=0).reshape(groups * cap, 1)
    signs = (listed == used_pairs[0:1]).astype(BF16) - (listed == used_pairs[1:2]).astype(BF16)

    every, pieces = [], []
    for j in range(chunks):
        block = distances(arrived[j], signs, cap)
        every.append(block)
        pieces += [block] + [rotated(block, "feat", s) for s in range(1, sides)]

    first_valid = lax.dynamic_slice_in_dim(valid, feat_index * CHUNK, CHUNK, 0)
    early = jnp.concatenate(
        [
            jnp.sum(first_valid * every[0], 0, keepdims=True),
            jnp.full((1, feats), jnp.sum(first_valid), F32),
        ],
        0,
    )
    early = lax.psum(early, ("atoms", "feat", "rep"))
    shift = early[0:1] / jnp.maximum(early[1:2], 1.0)

    opening = sum_or_pick(pieces[:sides], feat_index)[:HALO]
    opening = lax.dynamic_slice_in_dim(opening, feat_index * cols, cols, 1)
    halo = passed_down(opening, "atoms")

    local, own, sums, sums_next = moments(pieces, halo, valid, shift, place, chunks, sides)
    mine = lax.psum_scatter(local, ring, scatter_dimension=0, tiled=True)
    count, sums, sums_next = lax.psum((jnp.sum(valid), sums, sums_next), ring)

    mean, mean_next = sums[0] / count, sums_next[0] / count
    spread = sums[1] - count * mean * mean
    spread_next = sums_next[1] - count * mean_next * mean_next
    scale = 1.0 / jnp.sqrt(spread / count + 1e-05)
    scale_next = 1.0 / jnp.sqrt(spread_next / count + 1e-05)
    row_count = feats // lax.axis_size(ring)
    row_start = lax.axis_index(ring) * row_count
    mean_rows = lax.dynamic_slice_in_dim(mean, row_start, row_count)[:, None]
    scale_rows = lax.dynamic_slice_in_dim(scale, row_start, row_count)[:, None]
    mean_cols = lax.dynamic_slice_in_dim(mean, feat_index * cols, cols)[None]
    scale_cols = lax.dynamic_slice_in_dim(scale, feat_index * cols, cols)[None]
    corr_inst = (mine[:, :cols] / count - mean_rows * mean_cols) * scale_rows * scale_cols
    corr_lag = (mine[:, cols:] / count - mean_rows * mean_next[None]) * scale_rows * scale_next
    projections = ((own - mean_cols) * scale_cols)[None]
    return corr_inst, corr_lag, projections


def sum_or_pick(blocks, side):
    sides = len(blocks)
    out = blocks[0]
    for s in range(1, sides):
        out = jnp.where(lax.rem(side + sides - s, sides) == 0, blocks[s], out)
    return out


def shards(atom_coords, atom_pairs, traj_ids):
    groups, sides = lax.axis_size("atoms"), lax.axis_size("feat")
    atom_index, feat_index = lax.axis_index("atoms"), lax.axis_index("feat")
    place = jnp.stack([atom_index, feat_index]).astype(jnp.int32)
    width = atom_coords.shape[3]
    frames = atom_coords.shape[1] // groups
    coords = jnp.transpose(atom_coords[0], (1, 0, 2))

    cols = atom_pairs.shape[1]
    used_pairs = jnp.zeros((2, cols * sides), jnp.int32)
    for s in range(sides):
        there = lax.rem(feat_index + sides - s, sides)
        block = atom_pairs if s == 0 else rotated(atom_pairs, "feat", s)
        used_pairs = lax.dynamic_update_slice_in_dim(used_pairs, block, there * cols, 1)

    atoms = jnp.arange(groups * width, dtype=jnp.int32)
    used = jnp.any(used_pairs.reshape(-1)[:, None] == atoms[None, :], axis=0)
    used = used.reshape(groups, width)
    upto = lax.broadcasted_iota(jnp.int32, (width, width), 0) <= lax.broadcasted_iota(
        jnp.int32, (width, width), 1
    )
    order = jnp.dot(used.astype(BF16), upto.astype(BF16), preferred_element_type=F32)
    order = order.astype(jnp.int32)
    rank_all = jnp.where(used, order - 1, -1)

    ids = jnp.concatenate([traj_ids[0], jnp.full((LAG,), -1, jnp.int32)])
    offset = atom_index * frames
    ids_now = lax.dynamic_slice_in_dim(ids, offset, frames)
    ids_later = lax.dynamic_slice_in_dim(ids, offset + LAG, frames)
    valid = (ids_now == ids_later).astype(F32)[:, None]

    cap = min(width, -(-(width * 9 // 16) // 64) * 64)
    operands = (coords, rank_all, used_pairs, valid, place)
    return lax.cond(
        jnp.max(order) <= cap,
        functools.partial(with_cap, cap),
        functools.partial(with_cap, width),
        *operands,
    )


def solution(mesh):
    placed = (P(("grp", "rep"), None, None, "atoms"), P(None, "feat"), P(("grp", "rep"), None))
    return jax.shard_map(
        shards,
        mesh=mesh,
        in_specs=placed,
        out_specs=(
            P(("grp", "atoms", "rep"), "feat"),
            P(("grp", "atoms", "rep"), "feat"),
            P(("grp", "rep"), "atoms", "feat"),
        ),
        check_vma=False,
    )
```

time: 384 us -> 190 us (0.49)
  waiting for transfers between devices: 231 us -> 47.2 us
  local copies, waits for them, and re-layouts: 67.2 us -> 8.38 us
  Pallas kernels: 0 us -> 21.8 us
  blocking collectives: 29.3 us -> 50.5 us
  starting transfers between devices: 7.32 us -> 28.4 us
  other arithmetic: 24.6 us -> 14.4 us
  matrix products: 8.6 us -> 0.87 us
    all_to_all x1 -> x0, waiting for transfers between devices: 97 us -> none  [shards(): lax.all_to_all(blocks, 'atoms', split_axis=1, concat_axis=4, tiled=True)]
    psum x1 -> x0, waiting for transfers between devices: 94.4 us -> none  [shards(): lax.psum((local_moments, spread_now_part, spread_next_part), ('atoms', 'r...]
    all_gather x1 -> x0, waiting for transfers between devices: 35.7 us -> none  [shards(): every = lax.all_gather(computed, 'feat', axis=0, tiled=True)]
    gather x2 -> x1, local copies, waits for them, and re-layouts: 28.4 us -> 0.56 us  [with_cap(): listed = jnp.take(listed, order, axis=0).reshape(groups * cap, 1)]
    ppermute x1 -> x18, starting transfers between devices: 2.17 us -> 28.3 us  [the longest x17 18.2 us: rotated(): lax.ppermute(block, axis, [(i, (i + shift) % size) for i in range(size)])]
    psum x2, blocking collectives: 25.8 us -> 50.5 us  [the longest x1 25.9 us: with_cap(): early = lax.psum(early, ('atoms', 'feat', 'rep'))]
    ppermute x1 -> x18, waiting for transfers between devices: 3.51 us -> 26.5 us  [the longest x17 25.5 us: rotated(): lax.ppermute(block, axis, [(i, (i + shift) % size) for i in range(size)])]
    convert_element_type x1 -> x0, local copies, waits for them, and re-layouts: 22.2 us -> none  [shards(): lax.all_to_all(blocks, 'atoms', split_axis=1, concat_axis=4, tiled=True)]
  transfers between devices with their start and end apart: 4 -> 19, of which waited for: 4 -> 8; matrix products, arithmetic and copies ran while one was open for 2% -> 6% of each run, Pallas kernels for 0% -> 6%
where the time goes in v1:
time: 190 us; the launch traced here: 187 us
  blocking collectives  50.5 us (27%)
  waiting for transfers between devices  47.2 us (25%)
  starting transfers between devices  28.4 us (15%)
  Pallas kernels  21.8 us (11%)
  between operations  14.7 us (8%)
  other arithmetic  14.4 us (8%)
  local copies, waits for them, and re-layouts  8.38 us (4%)
    psum x1, blocking collectives, with_cap(): early = lax.psum(early, ('atoms', 'feat', 'rep'))  25.9 us
    ppermute x17, waiting for transfers between devices, rotated(): lax.ppermute(block, axis, [(i, (i + shift) % size) for i in range(size)])  25.5 us
    psum x1, blocking collectives, with_cap(): count, sums, sums_next = lax.psum((jnp.sum(valid), sums, sums_next), ring)  24.6 us
    reduce_scatter x1, waiting for transfers between devices, with_cap(): mine = lax.psum_scatter(local, ring, scatter_dimension=0, tiled=True)  20.7 us
    ppermute x17, starting transfers between devices, rotated(): lax.ppermute(block, axis, [(i, (i + shift) % size) for i in range(size)])  18.2 us
    pallas_call x4, Pallas kernels, pick(): pl.pallas_call(functools.partial(pick_kernel, groups, cap), grid_spec=plt...  10.2 us
    ppermute x1, starting transfers between devices, passed_down(): lax.ppermute(block, axis, [(i + 1, i) for i in range(lax.axis_size(axis)...  10.2 us
    pallas_call x1, Pallas kernels, moments(): pl.pallas_call(functools.partial(moment_kernel, chunks, sides), in_specs=...  6.62 us
  transfers between devices with their start and end apart: 19, of which 8 were waited for; matrix products, arithmetic and copies ran while one was open for 6% of the time, Pallas kernels for 6%

profile of v1, /device:TPU:9, one launch (start us, length us, event | category | flops | bytes accessed | tf_op | source)
XLA Modules:
  0.0 186.7 jit_solution(16603830646187294560)
XLA Ops:
  7.2 1.3 collective-permute-start.34
  8.4 0.7 constant_dynamic-update-slice_fusion.1
  9.2 0.7 collective-permute-done.34
  9.9 3.3 %fusion.38 = pred[3072]{0:T(1024)(128)(4,1)S(1)} fusion(s32[2048]{0:T(1024)S(1)} %bitcast.74), kind=kLoop, calls=%fused_computation.105 | loop fusion | flops 12579840 | bytes 11264 | tf_op jit(solution)/shard_map/reduce_or | solution.py:260
  13.3 0.9 fusion.49
  14.8 165.0 %conditional.1 = (f32[128,512]{1,0:T(8,128)}, f32[128,512]{1,0:T(8,128)}, f32[1,512,512]{2,1,0:T(8,128)}) conditional(s32[]{:T(128)} %convert_element_type.22, (s32[]{:T(128)}, pred[4,768]{1,0:T(4,128)(4,1)S(1)}, s32[2]{0:T(128)S(1)}, bf16[3,2048,768]{2,1,0:T(8,128)(2,1)}, s32[2,1024]{1,0:T(2,128)S(1)}, /*index=5*/s32[]{:T(128)}, s32[2048]{0:T(1024)}, ...), branch_computations={%region_2.12_spmd, %region_12.22_spmd} | conditional | flops 24152740 | bytes 94943544 | solution.py:277
  15.4 3.0 %pick.12 = (bf16[3,32,896]{2,1,0:T(8,128)(2,1)S(1)}, bf16[3,32,896]{2,1,0:T(8,128)(2,1)S(1)}, bf16[3,32,896]{2,1,0:T(8,128)(2,1)S(1)}, bf16[3,32,896]{2,1,0:T(8,128)(2,1)S(1)}) custom-call(s32[2]{0:T(128)S(1)} %get-tuple-element.55.place_ref, bf16[3,2048,768]{2,1,0:T(8,128)(2,1)} %get-tuple-element.56.refs_0_.refs_1_.refs_2_.refs_3_, ...), custom_call_target="tpu_custom_call" | custom-call | tf_op jit(solution)/shard_map/cond/branch_1_fun/pick/pallas_call | solution.py:59
  18.4 1.4 collective-permute-start.17
  19.8 1.1 collective-permute-start.18
  20.9 1.4 collective-permute-start.19
  22.3 1.9 %pick.13 = (bf16[3,32,896]{2,1,0:T(8,128)(2,1)S(1)}, bf16[3,32,896]{2,1,0:T(8,128)(2,1)}, bf16[3,32,896]{2,1,0:T(8,128)(2,1)S(1)}, bf16[3,32,896]{2,1,0:T(8,128)(2,1)S(1)}) custom-call(s32[2]{0:T(128)S(1)} %get-tuple-element.55.place_ref, bf16[3,2048,768]{2,1,0:T(8,128)(2,1)S(1)} %bitcast.50, bf16[3,2048,768]{2,1,0:T(8,128)(2,1)S(1)} %bitcast.50, ...), custom_call_target="tpu_custom_call" | custom-call | tf_op jit(solution)/shard_map/cond/branch_1_fun/pick/pallas_call | solution.py:59
  24.3 3.1 %collective-permute-start.22 = (bf16[3,32,896]{2,1,0:T(8,128)(2,1)S(1)}, bf16[3,32,896]{2,1,0:T(8,128)(2,1)S(1)}, u32[]{:S(2)}, u32[]{:S(2)}) collective-permute-start(bf16[3,32,896]{2,1,0:T(8,128)(2,1)S(1)} %get-tuple-element.66), channel_id=1, source_target_pairs={{0,8},{4,12},{8,0},{12,4},{1,9},{5,13},{9,1},{13,5},{2,10},{6,14},... | collective-permute-start | bytes 516104 | tf_op jit(solution)/shard_map/cond/branch_1_fun/ppermute | solution.py:20
  27.4 2.2 %pick.14 = (bf16[3,32,896]{2,1,0:T(8,128)(2,1)S(1)}, bf16[3,32,896]{2,1,0:T(8,128)(2,1)}, bf16[3,32,896]{2,1,0:T(8,128)(2,1)}, bf16[3,32,896]{2,1,0:T(8,128)(2,1)}) custom-call(s32[2]{0:T(128)S(1)} %get-tuple-element.55.place_ref, bf16[3,2048,768]{2,1,0:T(8,128)(2,1)S(1)} %bitcast.50, bf16[3,2048,768]{2,1,0:T(8,128)(2,1)S(1)} %bitcast.50, ...), custom_call_target="tpu_custom_call" | custom-call | tf_op jit(solution)/shard_map/cond/branch_1_fun/pick/pallas_call | solution.py:59
  29.5 0.9 select_reduce_fusion.1
  31.4 2.3 %collective-permute-start.25 = (bf16[3,32,896]{2,1,0:T(8,128)(2,1)}, bf16[3,32,896]{2,1,0:T(8,128)(2,1)S(1)}, u32[]{:S(2)}, u32[]{:S(2)}) collective-permute-start(bf16[3,32,896]{2,1,0:T(8,128)(2,1)} %get-tuple-element.69), channel_id=1, source_target_pairs={{0,4},{4,8},{8,12},{12,0},{1,5},{5,9},{9,13},{13,1},{2,6},{6,10},{... | collective-permute-start | bytes 516104 | tf_op jit(solution)/shard_map/cond/branch_1_fun/ppermute | solution.py:20
  33.7 12.2 %collective-permute-done.19.refs_3_ = bf16[3,32,896]{2,1,0:T(8,128)(2,1)S(1)} collective-permute-done((bf16[3,32,896]{2,1,0:T(8,128)(2,1)S(1)}, bf16[3,32,896]{2,1,0:T(8,128)(2,1)S(1)}, u32[]{:S(2)}, u32[]{:S(2)}) %collective-permute-start.19) | collective-permute-done | bytes 172064 | tf_op jit(solution)/shard_map/cond/branch_1_fun/ppermute | solution.py:20
  45.9 2.8 %fusion.19.refs_4_ = bf16[1792,1024]{1,0:T(8,128)(2,1)} fusion(s32[1024]{0:T(1024)S(1)} %bitcast.63, s32[1024]{0:T(1024)S(1)} %bitcast.62, s32[1792]{0:T(1024)S(1)} %select_n.111), kind=kLoop, calls=%fused_computation.57 | loop fusion | flops 9175040 | bytes 3685376 | tf_op jit(solution)/shard_map/cond/branch_1_fun/sub | solution.py:192
  48.7 3.1 %pick.15 = (bf16[3,32,896]{2,1,0:T(8,128)(2,1)S(1)}, bf16[3,32,896]{2,1,0:T(8,128)(2,1)}, bf16[3,32,896]{2,1,0:T(8,128)(2,1)S(1)}, bf16[3,32,896]{2,1,0:T(8,128)(2,1)S(1)}) custom-call(s32[2]{0:T(128)S(1)} %get-tuple-element.55.place_ref, bf16[3,2048,768]{2,1,0:T(8,128)(2,1)} %get-tuple-element.56.refs_0_.refs_1_.refs_2_.refs_3_, ...), custom_call_target="tpu_custom_call" | custom-call | tf_op jit(solution)/shard_map/cond/branch_1_fun/pick/pallas_call | solution.py:59
  51.8 2.2 %copy-done = bf16[1792,1024]{1,0:T(8,128)(2,1)S(1)} copy-done((bf16[1792,1024]{1,0:T(8,128)(2,1)S(1)}, bf16[1792,1024]{1,0:T(8,128)(2,1)}, u32[]{:S(2)}) %copy-start) | copy-done | bytes 3670040 | tf_op jit(solution)/shard_map/cond
  54.0 1.0 distances.12.refs_0_
  55.1 1.4 collective-permute-start.29
  56.6 2.2 %collective-permute-done.23.refs_3_ = bf16[3,32,896]{2,1,0:T(8,128)(2,1)S(1)} collective-permute-done((bf16[3,32,896]{2,1,0:T(8,128)(2,1)S(1)}, bf16[3,32,896]{2,1,0:T(8,128)(2,1)S(1)}, u32[]{:S(2)}, u32[]{:S(2)}) %collective-permute-start.23) | collective-permute-done | bytes 172064 | tf_op jit(solution)/shard_map/cond/branch_1_fun/ppermute | solution.py:20
  58.8 2.0 %collective-permute-start.30 = (bf16[3,32,896]{2,1,0:T(8,128)(2,1)}, bf16[3,32,896]{2,1,0:T(8,128)(2,1)S(1)}, u32[]{:S(2)}, u32[]{:S(2)}) collective-permute-start(bf16[3,32,896]{2,1,0:T(8,128)(2,1)} %copy-done.13), channel_id=1, source_target_pairs={{0,8},{4,12},{8,0},{12,4},{1,9},{5,13},{9,1},{13,5},{2,10},{6,14},... | collective-permute-start | bytes 516104 | tf_op jit(solution)/shard_map/cond/branch_1_fun/ppermute | solution.py:20
  60.8 1.3 collective-permute-start.20
  62.0 0.7 fusion.44
  62.9 0.7 fusion.46
  63.6 2.0 %copy-done.1 = bf16[1792,1024]{1,0:T(8,128)(2,1)S(1)} copy-done((bf16[1792,1024]{1,0:T(8,128)(2,1)S(1)}, bf16[1792,1024]{1,0:T(8,128)(2,1)}, u32[]{:S(2)}) %copy-start.1) | copy-done | bytes 3670040 | tf_op jit(solution)/shard_map/cond
  65.6 1.0 distances.13.refs_2_
  66.6 6.9 %collective-permute-done.27.refs_3_ = bf16[3,32,896]{2,1,0:T(8,128)(2,1)S(1)} collective-permute-done((bf16[3,32,896]{2,1,0:T(8,128)(2,1)}, bf16[3,32,896]{2,1,0:T(8,128)(2,1)S(1)}, u32[]{:S(2)}, u32[]{:S(2)}) %collective-permute-start.27) | collective-permute-done | bytes 172064 | tf_op jit(solution)/shard_map/cond/branch_1_fun/ppermute | solution.py:20
  73.5 0.7 copy-done.4
  74.2 1.2 collective-permute-start.24
  75.4 0.9 copy-done.5
  76.3 1.0 distances.14.refs_4_
  77.7 3.3 %collective-permute-done.31.refs_3_ = bf16[3,32,896]{2,1,0:T(8,128)(2,1)} collective-permute-done((bf16[3,32,896]{2,1,0:T(8,128)(2,1)}, bf16[3,32,896]{2,1,0:T(8,128)(2,1)}, u32[]{:S(2)}, u32[]{:S(2)}) %collective-permute-start.31) | collective-permute-done | bytes 172064 | tf_op jit(solution)/shard_map/cond/branch_1_fun/ppermute | solution.py:20
  81.0 1.9 %distances.15.refs_6_ = f32[64,1024]{1,0:T(8,128)S(1)} custom-call(bf16[3,32,896]{2,1,0:T(8,128)(2,1)S(1)} %get-tuple-element.72.refs_0_, bf16[3,32,896]{2,1,0:T(8,128)(2,1)S(1)} %collective-permute-done.29.refs_1_, bf16[3,32,896]{2,1,0:T(8,128)(2,1)S(1)} %collective-permute-done.30.refs_2_, bf16[3,32,896]{2,1,0:T(8,128)(2,1)} %collective-permute-done.31.refs_3_, ...), custom_call_target="tpu_custom_call" | custom-call | tf_op jit(solution)/shard_map/cond/branch_1_fun/distances/pallas_call | solution.py:94
  82.9 1.3 collective-permute-start.32
  84.3 0.7 concatenate.7
  85.0 25.9 %psum.52 = f32[2,1024]{1,0:T(2,128)S(1)} all-reduce(f32[2,1024]{1,0:T(2,128)S(1)} %concatenate.7), channel_id=1, replica_groups=mesh['grp'=2,'atoms'=4,'feat'=2,'rep'=2] {'atoms','feat','rep'}, use_global_device_ids=true, to_apply=%region_16.16 | all-reduce | flops 2048 | bytes 16384 | tf_op jit(solution)/shard_map/cond/branch_1_fun/psum | solution.py:208
  110.9 10.2 %collective-permute-start.33 = (f32[16,512]{1,0:T(8,128)S(1)}, f32[16,512]{1,0:T(8,128)S(1)}, u32[]{:S(2)}, u32[]{:S(2)}) collective-permute-start(f32[16,512]{1,0:T(8,128)S(1)} %dynamic-slice_select_fusion.1), channel_id=1, source_target_pairs={{4,0},{8,4},{12,8},{5,1},{9,5},{13,9},{6,2},{10,6},{14,10},{7,3},{... | collective-permute-start | bytes 98312 | tf_op jit(solution)/shard_map/cond/branch_1_fun/ppermute | solution.py:24
  121.1 0.9 collective-permute-done.33.refs_8_
  122.1 6.6 %moments.3 = (f32[1024,1024]{1,0:T(8,128)}, f32[512,512]{1,0:T(8,128)S(1)}, f32[2,1024]{1,0:T(2,128)S(1)}, f32[2,512]{1,0:T(2,128)S(1)}) custom-call(s32[2]{0:T(128)S(1)} %get-tuple-element.55.place_ref, f32[64,1024]{1,0:T(8,128)S(1)} %distances.12.refs_0_, f32[64,1024]{1,0:T(8,128)S(1)} %collective-permute-done.20.refs_1_, ...), custom_call_target="tpu_custom_call" | custom-call | tf_op jit(solution)/shard_map/cond/branch_1_fun/moments/pallas_call | solution.py:153
  128.7 24.6 %all-reduce.4 = (f32[2,1024]{1,0:T(2,128)S(1)}, f32[]{:T(128)}, f32[2,512]{1,0:T(2,128)S(1)}) all-reduce(f32[2,1024]{1,0:T(2,128)S(1)} %get-tuple-element.79, f32[]{:T(128)} %get-tuple-element.166, f32[2,512]{1,0:T(2,128)S(1)} %get-tuple-element.80), channel_id=1, replica_groups=mesh['grp'=2,'atoms'=4,'feat'=2,'rep'=2] {'atoms','rep'}, use_global_device_ids=true, to_apply=%region_20.20 | all-reduce | flops 3073 | bytes 24584 | tf_op jit(solution)/shard_map/cond/branch_1_fun/psum | solution.py:217
  153.3 0.6 slice_divide_fusion.6
  153.9 0.6 fusion.29
  154.7 0.6 add_rsqrt_fusion.1
  155.4 1.1 multiply_bitcast_fusion.1
  156.5 20.7 %reduce-scatter.5.cloned.1.call-done = f32[128,1024]{1,0:T(8,128)} async-done(((f32[1024,1024]{1,0:T(8,128)}), f32[128,1024]{1,0:T(8,128)}) %reduce-scatter.5.cloned.1.call-update) | async-done | bytes 524304 | tf_op jit(solution)/shard_map/cond/branch_1_fun/reduce_scatter | solution.py:216
  177.2 2.6 %fusion.22 = (f32[128,512]{1,0:T(8,128)}, f32[128,512]{1,0:T(8,128)}) fusion(f32[128,1024]{1,0:T(8,128)} %reduce-scatter.5.cloned.1.call-done, f32[512]{0:T(512)S(1)} %bitcast.72, f32[512]{0:T(512)S(1)} %bitcast.73, f32[128]{0:T(128)S(1)} %dynamic_slice.53, f32[128]{0:T(128)S(1)} %fusion.34, f32[]{:T(128)} %get-tuple-element.156, f32[512]{0:T(512)S(1)} %dynamic_slice.54, ...), kind=kLoop, calls=%fused_computation.62 | loop fusion | flops 655360 | bytes 1057796 | tf_op jit(solution)/shard_map/cond/branch_1_fun/mul | solution.py:231
  (63 shorter events, 2.4 us)
Async XLA Ops:
  7.2 2.7 %collective-permute-start.34 = (s32[2,512]{1,0:T(2,128)}, s32[2,512]{1,0:T(2,128)S(1)}, u32[]{:S(2)}, u32[]{:S(2)}) collective-permute-start(s32[2,512]{1,0:T(2,128)} %param.6), channel_id=1, source_target_pairs={{0,2},{2,0},{1,3},{3,1},{4,6},{6,4},{5,7},{7,5},{8,10},{10,8},{9,1... | collective-permute-start | bytes 12296 | tf_op jit(solution)/shard_map/ppermute | solution.py:20
  15.0 162.2 %reduce-scatter.5.cloned.1.call-start = ((), (), s32[]{:S(2)}) async-start(), calls=%async_computation.3 | async-start | bytes 4718592 | tf_op jit(solution)/shard_map/cond/branch_1_fun/reduce_scatter | solution.py:216
  15.4 6.9 %slice-start.3 = ((s8[9437184]{0:T(1024)(128)(4,1)}), s8[4194304]{0:T(1024)(128)(4,1)S(1)}, s32[]{:S(2)}) async-start(s8[9437184]{0:T(1024)(128)(4,1)} %bitcast.49), calls=%async_computation.7 | async-start | bytes 8388608 | tf_op jit(solution)/shard_map/cond
  15.4 6.9 %slice-start.4 = ((s8[9437184]{0:T(1024)(128)(4,1)}), s8[4194304]{0:T(1024)(128)(4,1)S(1)}, s32[]{:S(2)}) async-start(s8[9437184]{0:T(1024)(128)(4,1)} %bitcast.49), calls=%async_computation.8 | async-start | bytes 8388608 | tf_op jit(solution)/shard_map/cond
  15.4 6.9 %slice-start.5 = ((s8[9437184]{0:T(1024)(128)(4,1)}), s8[1048576]{0:T(1024)(128)(4,1)S(1)}, s32[]{:S(2)}) async-start(s8[9437184]{0:T(1024)(128)(4,1)} %bitcast.49), calls=%async_computation.9 | async-start | bytes 2097152 | tf_op jit(solution)/shard_map/cond
  18.4 12.8 %collective-permute-start.17 = (bf16[3,32,896]{2,1,0:T(8,128)(2,1)S(1)}, bf16[3,32,896]{2,1,0:T(8,128)(2,1)S(1)}, u32[]{:S(2)}, u32[]{:S(2)}) collective-permute-start(bf16[3,32,896]{2,1,0:T(8,128)(2,1)S(1)} %get-tuple-element.60), channel_id=1, source_target_pairs={{0,4},{4,8},{8,12},{12,0},{1,5},{5,9},{9,13},{13,1},{2,6},{6,10},{... | collective-permute-start | bytes 516104 | tf_op jit(solution)/shard_map/cond/branch_1_fun/ppermute | solution.py:20
  19.8 11.6 %collective-permute-start.18 = (bf16[3,32,896]{2,1,0:T(8,128)(2,1)S(1)}, bf16[3,32,896]{2,1,0:T(8,128)(2,1)S(1)}, u32[]{:S(2)}, u32[]{:S(2)}) collective-permute-start(bf16[3,32,896]{2,1,0:T(8,128)(2,1)S(1)} %get-tuple-element.61), channel_id=1, source_target_pairs={{0,8},{4,12},{8,0},{12,4},{1,9},{5,13},{9,1},{13,5},{2,10},{6,14},... | collective-permute-start | bytes 516104 | tf_op jit(solution)/shard_map/cond/branch_1_fun/ppermute | solution.py:20
  20.9 25.0 %collective-permute-start.19 = (bf16[3,32,896]{2,1,0:T(8,128)(2,1)S(1)}, bf16[3,32,896]{2,1,0:T(8,128)(2,1)S(1)}, u32[]{:S(2)}, u32[]{:S(2)}) collective-permute-start(bf16[3,32,896]{2,1,0:T(8,128)(2,1)S(1)} %get-tuple-element.62), channel_id=1, source_target_pairs={{0,12},{4,0},{8,4},{12,8},{1,13},{5,1},{9,5},{13,9},{2,14},{6,2},{... | collective-permute-start | bytes 516104 | tf_op jit(solution)/shard_map/cond/branch_1_fun/ppermute | solution.py:20
  24.2 30.8 %collective-permute-start.21 = (bf16[3,32,896]{2,1,0:T(8,128)(2,1)}, bf16[3,32,896]{2,1,0:T(8,128)(2,1)S(1)}, u32[]{:S(2)}, u32[]{:S(2)}) collective-permute-start(bf16[3,32,896]{2,1,0:T(8,128)(2,1)} %get-tuple-element.65), channel_id=1, source_target_pairs={{0,4},{4,8},{8,12},{12,0},{1,5},{5,9},{9,13},{13,1},{2,6},{6,10},{... | collective-permute-start | bytes 516104 | tf_op jit(solution)/shard_map/cond/branch_1_fun/ppermute | solution.py:20
  24.3 30.9 %collective-permute-start.22 = (bf16[3,32,896]{2,1,0:T(8,128)(2,1)S(1)}, bf16[3,32,896]{2,1,0:T(8,128)(2,1)S(1)}, u32[]{:S(2)}, u32[]{:S(2)}) collective-permute-start(bf16[3,32,896]{2,1,0:T(8,128)(2,1)S(1)} %get-tuple-element.66), channel_id=1, source_target_pairs={{0,8},{4,12},{8,0},{12,4},{1,9},{5,13},{9,1},{13,5},{2,10},{6,14},... | collective-permute-start | bytes 516104 | tf_op jit(solution)/shard_map/cond/branch_1_fun/ppermute | solution.py:20
  31.2 27.6 %collective-permute-start.23 = (bf16[3,32,896]{2,1,0:T(8,128)(2,1)S(1)}, bf16[3,32,896]{2,1,0:T(8,128)(2,1)S(1)}, u32[]{:S(2)}, u32[]{:S(2)}) collective-permute-start(bf16[3,32,896]{2,1,0:T(8,128)(2,1)S(1)} %get-tuple-element.67), channel_id=1, source_target_pairs={{0,12},{4,0},{8,4},{12,8},{1,13},{5,1},{9,5},{13,9},{2,14},{6,2},{... | collective-permute-start | bytes 516104 | tf_op jit(solution)/shard_map/cond/branch_1_fun/ppermute | solution.py:20
  31.4 29.4 %collective-permute-start.25 = (bf16[3,32,896]{2,1,0:T(8,128)(2,1)}, bf16[3,32,896]{2,1,0:T(8,128)(2,1)S(1)}, u32[]{:S(2)}, u32[]{:S(2)}) collective-permute-start(bf16[3,32,896]{2,1,0:T(8,128)(2,1)} %get-tuple-element.69), channel_id=1, source_target_pairs={{0,4},{4,8},{8,12},{12,0},{1,5},{5,9},{9,13},{13,1},{2,6},{6,10},{... | collective-permute-start | bytes 516104 | tf_op jit(solution)/shard_map/cond/branch_1_fun/ppermute | solution.py:20
  45.9 14.9 %collective-permute-start.26 = (bf16[3,32,896]{2,1,0:T(8,128)(2,1)}, bf16[3,32,896]{2,1,0:T(8,128)(2,1)S(1)}, u32[]{:S(2)}, u32[]{:S(2)}) collective-permute-start(bf16[3,32,896]{2,1,0:T(8,128)(2,1)} %get-tuple-element.70), channel_id=1, source_target_pairs={{0,8},{4,12},{8,0},{12,4},{1,9},{5,13},{9,1},{13,5},{2,10},{6,14},... | collective-permute-start | bytes 516104 | tf_op jit(solution)/shard_map/cond/branch_1_fun/ppermute | solution.py:20
  48.7 13.3 %copy-start.15 = (s32[2048]{0:T(1024)S(1)}, s32[2048]{0:T(1024)}, u32[]{:S(2)}) copy-start(s32[2048]{0:T(1024)} %get-tuple-element.146) | copy-start | bytes 24580 | tf_op jit(solution)/shard_map/cond
  51.8 3.2 %copy-start.12 = (bf16[3,32,896]{2,1,0:T(8,128)(2,1)}, bf16[3,32,896]{2,1,0:T(8,128)(2,1)S(1)}, u32[]{:S(2)}) copy-start(bf16[3,32,896]{2,1,0:T(8,128)(2,1)S(1)} %get-tuple-element.75) | copy-start | bytes 516100 | tf_op jit(solution)/shard_map/cond
  51.8 3.2 %copy-start.13 = (bf16[3,32,896]{2,1,0:T(8,128)(2,1)}, bf16[3,32,896]{2,1,0:T(8,128)(2,1)S(1)}, u32[]{:S(2)}) copy-start(bf16[3,32,896]{2,1,0:T(8,128)(2,1)S(1)} %get-tuple-element.74) | copy-start | bytes 516100 | tf_op jit(solution)/shard_map/cond
  51.8 2.2 %copy-start = (bf16[1792,1024]{1,0:T(8,128)(2,1)S(1)}, bf16[1792,1024]{1,0:T(8,128)(2,1)}, u32[]{:S(2)}) copy-start(bf16[1792,1024]{1,0:T(8,128)(2,1)} %fusion.19.refs_4_) | copy-start | bytes 11010052 | tf_op jit(solution)/shard_map/cond
  55.1 18.5 %collective-permute-start.27 = (bf16[3,32,896]{2,1,0:T(8,128)(2,1)}, bf16[3,32,896]{2,1,0:T(8,128)(2,1)S(1)}, u32[]{:S(2)}, u32[]{:S(2)}) collective-permute-start(bf16[3,32,896]{2,1,0:T(8,128)(2,1)} %get-tuple-element.71), channel_id=1, source_target_pairs={{0,12},{4,0},{8,4},{12,8},{1,13},{5,1},{9,5},{13,9},{2,14},{6,2},{... | collective-permute-start | bytes 516104 | tf_op jit(solution)/shard_map/cond/branch_1_fun/ppermute | solution.py:20
  55.1 22.2 %collective-permute-start.29 = (bf16[3,32,896]{2,1,0:T(8,128)(2,1)}, bf16[3,32,896]{2,1,0:T(8,128)(2,1)S(1)}, u32[]{:S(2)}, u32[]{:S(2)}) collective-permute-start(bf16[3,32,896]{2,1,0:T(8,128)(2,1)} %get-tuple-element.73), channel_id=1, source_target_pairs={{0,4},{4,8},{8,12},{12,0},{1,5},{5,9},{9,13},{13,1},{2,6},{6,10},{... | collective-permute-start | bytes 516104 | tf_op jit(solution)/shard_map/cond/branch_1_fun/ppermute | solution.py:20
  58.8 18.9 %collective-permute-start.30 = (bf16[3,32,896]{2,1,0:T(8,128)(2,1)}, bf16[3,32,896]{2,1,0:T(8,128)(2,1)S(1)}, u32[]{:S(2)}, u32[]{:S(2)}) collective-permute-start(bf16[3,32,896]{2,1,0:T(8,128)(2,1)} %copy-done.13), channel_id=1, source_target_pairs={{0,8},{4,12},{8,0},{12,4},{1,9},{5,13},{9,1},{13,5},{2,10},{6,14},... | collective-permute-start | bytes 516104 | tf_op jit(solution)/shard_map/cond/branch_1_fun/ppermute | solution.py:20
  60.8 20.3 %collective-permute-start.31 = (bf16[3,32,896]{2,1,0:T(8,128)(2,1)}, bf16[3,32,896]{2,1,0:T(8,128)(2,1)}, u32[]{:S(2)}, u32[]{:S(2)}) collective-permute-start(bf16[3,32,896]{2,1,0:T(8,128)(2,1)} %copy-done.12), channel_id=1, source_target_pairs={{0,12},{4,0},{8,4},{12,8},{1,13},{5,1},{9,5},{13,9},{2,14},{6,2},{... | collective-permute-start | bytes 516104 | tf_op jit(solution)/shard_map/cond/branch_1_fun/ppermute | solution.py:20
  60.8 50.1 %collective-permute-start.20 = (f32[64,1024]{1,0:T(8,128)S(1)}, f32[64,1024]{1,0:T(8,128)S(1)}, u32[]{:S(2)}, u32[]{:S(2)}) collective-permute-start(f32[64,1024]{1,0:T(8,128)S(1)} %distances.12.refs_0_), channel_id=1, source_target_pairs={{0,2},{2,0},{1,3},{3,1},{4,6},{6,4},{5,7},{7,5},{8,10},{10,8},{9,1... | collective-permute-start | bytes 786440 | tf_op jit(solution)/shard_map/cond/branch_1_fun/ppermute | solution.py:20
  63.6 2.0 %copy-start.1 = (bf16[1792,1024]{1,0:T(8,128)(2,1)S(1)}, bf16[1792,1024]{1,0:T(8,128)(2,1)}, u32[]{:S(2)}) copy-start(bf16[1792,1024]{1,0:T(8,128)(2,1)} %fusion.19.refs_4_) | copy-start | bytes 11010052 | tf_op jit(solution)/shard_map/cond
  73.5 0.7 copy-start.4
  74.2 46.9 %collective-permute-start.24 = (f32[64,1024]{1,0:T(8,128)S(1)}, f32[64,1024]{1,0:T(8,128)S(1)}, u32[]{:S(2)}, u32[]{:S(2)}) collective-permute-start(f32[64,1024]{1,0:T(8,128)S(1)} %distances.13.refs_2_), channel_id=1, source_target_pairs={{0,2},{2,0},{1,3},{3,1},{4,6},{6,4},{5,7},{7,5},{8,10},{10,8},{9,1... | collective-permute-start | bytes 786440 | tf_op jit(solution)/shard_map/cond/branch_1_fun/ppermute | solution.py:20
  75.4 0.9 copy-start.5
  77.3 43.8 %collective-permute-start.28 = (f32[64,1024]{1,0:T(8,128)S(1)}, f32[64,1024]{1,0:T(8,128)S(1)}, u32[]{:S(2)}, u32[]{:S(2)}) collective-permute-start(f32[64,1024]{1,0:T(8,128)S(1)} %distances.14.refs_4_), channel_id=1, source_target_pairs={{0,2},{2,0},{1,3},{3,1},{4,6},{6,4},{5,7},{7,5},{8,10},{10,8},{9,1... | collective-permute-start | bytes 786440 | tf_op jit(solution)/shard_map/cond/branch_1_fun/ppermute | solution.py:20
  82.9 38.2 %collective-permute-start.32 = (f32[64,1024]{1,0:T(8,128)S(1)}, f32[64,1024]{1,0:T(8,128)S(1)}, u32[]{:S(2)}, u32[]{:S(2)}) collective-permute-start(f32[64,1024]{1,0:T(8,128)S(1)} %distances.15.refs_6_), channel_id=1, source_target_pairs={{0,2},{2,0},{1,3},{3,1},{4,6},{6,4},{5,7},{7,5},{8,10},{10,8},{9,1... | collective-permute-start | bytes 786440 | tf_op jit(solution)/shard_map/cond/branch_1_fun/ppermute | solution.py:20
  110.9 11.2 %collective-permute-start.33 = (f32[16,512]{1,0:T(8,128)S(1)}, f32[16,512]{1,0:T(8,128)S(1)}, u32[]{:S(2)}, u32[]{:S(2)}) collective-permute-start(f32[16,512]{1,0:T(8,128)S(1)} %dynamic-slice_select_fusion.1), channel_id=1, source_target_pairs={{4,0},{8,4},{12,8},{5,1},{9,5},{13,9},{6,2},{10,6},{14,10},{7,3},{... | collective-permute-start | bytes 98312 | tf_op jit(solution)/shard_map/cond/branch_1_fun/ppermute | solution.py:24
Sparse Core Ops, SparseCore 0:
  128.8 48.3 reduce-scatter.4

commit v2 on v1

v2 whole, which is shorter than its diff:
```python
import functools

import jax
import jax.numpy as jnp
from jax import lax
from jax.experimental import pallas as pl
from jax.experimental.pallas import tpu as pltpu
from jax.sharding import PartitionSpec as P

LAG = 10
HALO = 16
CHUNK = 64
CODE = 32700.0
FINE = 60000.0
MEAN_STEP = 0.001
ROOT_STEP = 0.02
TINY = 1e-30
VMEM_LIMIT = 48 * 1024 * 1024
F32 = jnp.float32
BF16 = jnp.bfloat16
LARGE = pl.CostEstimate(flops=10**11, bytes_accessed=1024, transcendentals=0)
SMALL = pl.CostEstimate(flops=1024, bytes_accessed=1024, transcendentals=0)


def rotated(block, axis, shift):
    size = lax.axis_size(axis)
    return lax.ppermute(block, axis, [(i, (i + shift) % size) for i in range(size)])


def passed_down(block, axis):
    return lax.ppermute(block, axis, [(i + 1, i) for i in range(lax.axis_size(axis) - 1)])


def params():
    return pltpu.CompilerParams(vmem_limit_bytes=VMEM_LIMIT)


def pick_kernel(start, place_ref, coords_ref, rank_ref, after_ref, *refs):
    groups = len(refs) - 2
    outs, rows_ref, sems = refs[:groups], refs[groups], refs[groups + 1]
    size, width = rows_ref.shape[2], rows_ref.shape[3]
    cap = outs[0].shape[2] // 2
    frames = coords_ref.shape[1] // groups
    copies = []
    for s in range(groups):
        there = lax.rem(place_ref[0] + s, groups)
        row = pl.multiple_of(there * frames + start + place_ref[1] * size, CHUNK)
        copies.append(
            pltpu.make_async_copy(
                coords_ref.at[:, pl.ds(row, size), :], rows_ref.at[s], sems.at[s]
            )
        )
    for copy in copies:
        copy.start()
    slots = lax.broadcasted_iota(jnp.int32, (width, cap), 1)
    chosen = (rank_ref[...] == slots).astype(F32).astype(BF16)
    half = size // 2
    for s in range(groups):
        copies[s].wait()
        rows = rows_ref[s].reshape(3 * size, width)
        picked = jnp.dot(rows, chosen, preferred_element_type=F32).astype(BF16)
        picked = picked.reshape(3, size, cap)
        outs[s][:, :, 0:cap] = picked[:, :half, :]
        outs[s][:, :, cap : 2 * cap] = picked[:, half:, :]


def pick(coords, rank, after, cap, place, start, size, groups):
    width = coords.shape[2]
    vmem = pl.BlockSpec(memory_space=pltpu.VMEM)
    return pl.pallas_call(
        functools.partial(pick_kernel, start),
        in_specs=[
            pl.BlockSpec(memory_space=pltpu.SMEM),
            pl.BlockSpec(memory_space=pltpu.HBM),
            vmem,
            pl.BlockSpec(memory_space=pl.ANY),
        ],
        out_specs=[vmem] * groups,
        out_shape=[jax.ShapeDtypeStruct((3, size // 2, 2 * cap), BF16)] * groups,
        scratch_shapes=[
            pltpu.VMEM((groups, 3, size, width), BF16),
            pltpu.SemaphoreType.DMA((groups,)),
        ],
        compiler_params=params(),
        cost_estimate=SMALL,
        name="pick",
    )(place, coords, rank, after)


def distance_kernel(*refs):
    blocks, (signs_ref, after_ref, out, joined) = refs[:-4], refs[-4:]
    half, cap = blocks[0].shape[1], blocks[0].shape[2] // 2
    size = 2 * half
    for s, block in enumerate(blocks):
        columns = slice(s * cap, (s + 1) * cap)
        for k in range(3):
            joined[k * size : k * size + half, columns] = block[k, :, 0:cap]
            joined[k * size + half : (k + 1) * size, columns] = block[k, :, cap : 2 * cap]
    delta = jnp.dot(joined[...], signs_ref[...], preferred_element_type=F32)
    square = delta * delta
    total = square[:size] + square[size : 2 * size] + square[2 * size :]
    out[...] = jnp.sqrt(total + 0.01)


def distances(blocks, signs, after):
    size = 2 * blocks[0].shape[1]
    vmem = pl.BlockSpec(memory_space=pltpu.VMEM)
    return pl.pallas_call(
        distance_kernel,
        in_specs=[vmem] * (len(blocks) + 1) + [pl.BlockSpec(memory_space=pl.ANY)],
        out_specs=vmem,
        out_shape=jax.ShapeDtypeStruct((size, signs.shape[1]), F32),
        scratch_shapes=[pltpu.VMEM((3 * size, signs.shape[0]), BF16)],
        compiler_params=params(),
        cost_estimate=LARGE,
        name="distances",
    )(*blocks, signs, after)


def split_in_two(value):
    high = value.astype(BF16)
    return high, (value - high.astype(F32)).astype(BF16)


def product(left, right):
    left_high, left_low = split_in_two(left)
    right_high, right_low = split_in_two(right)
    left_high, left_low = left_high.T, left_low.T
    total = jnp.dot(left_high, right_high, preferred_element_type=F32)
    total += jnp.dot(left_high, right_low, preferred_element_type=F32)
    return total + jnp.dot(left_low, right_high, preferred_element_type=F32)


def place_pieces(sizes, side, sides, pieces, every, first):
    row = first
    for j, size in enumerate(sizes):
        for s in range(sides):
            there = lax.rem(side + sides - s, sides)
            at = pl.multiple_of(row + there * size, HALO)
            every[pl.ds(at, size), :] = pieces[j * sides + s][...]
        row += sides * size


def own_columns(side, sides, whole, own):
    cols = own.shape[1]
    for s in range(sides):

        @pl.when(side == s)
        def _():
            own[...] = whole[:, s * cols : (s + 1) * cols]


def row_sum(value):
    return jnp.sum(value, 0, keepdims=True)


def early_kernel(sizes, sides, place_ref, *refs):
    pieces = refs[: len(sizes) * sides]
    valid_ref, out, own_out, shift_out, sums_out, tail_out, every, own = refs[len(pieces) :]
    frames = every.shape[0]
    cols = own.shape[1]
    side = place_ref[1]
    place_pieces(sizes, side, sides, pieces, every, 0)
    valid = valid_ref[0:frames, :]
    count = jnp.maximum(jnp.sum(valid), 1.0)
    shift = row_sum(valid * every[...]) / count
    shift_out[...] = shift
    every[...] = every[...] - shift
    tail_out[...] = every[frames - HALO : frames, :]
    own_columns(side, sides, every, own)
    own_out[...] = own[...]
    now = every[...]
    weighed = valid * now
    weighed_later = valid[: frames - LAG] * own[LAG:frames, :]
    sums_out[0:1, :] = row_sum(weighed)
    sums_out[1:2, :] = row_sum(weighed * now)
    sums_out[2:3, 0:cols] = row_sum(weighed_later)
    sums_out[3:4, 0:cols] = row_sum(weighed_later * own[LAG:frames, :])
    weighed_later = jnp.concatenate([weighed_later, jnp.zeros((LAG, cols), F32)], 0)
    out[:, 0:cols] = product(now, valid * own[...])
    out[:, cols : 2 * cols] = product(now, weighed_later)


def early_moments(pieces, valid, place, sizes, sides):
    frames, feats = sides * sum(sizes), pieces[0].shape[1]
    cols = feats // sides
    vmem = pl.BlockSpec(memory_space=pltpu.VMEM)
    return pl.pallas_call(
        functools.partial(early_kernel, sizes, sides),
        in_specs=[pl.BlockSpec(memory_space=pltpu.SMEM)] + [vmem] * (len(pieces) + 1),
        out_specs=[vmem] * 5,
        out_shape=[
            jax.ShapeDtypeStruct((feats, 2 * cols), F32),
            jax.ShapeDtypeStruct((frames, cols), F32),
            jax.ShapeDtypeStruct((1, feats), F32),
            jax.ShapeDtypeStruct((4, feats), F32),
            jax.ShapeDtypeStruct((HALO, feats), F32),
        ],
        scratch_shapes=[pltpu.VMEM((frames, feats), F32), pltpu.VMEM((frames, cols), F32)],
        compiler_params=params(),
        cost_estimate=LARGE,
        name="early_moments",
    )(place, *pieces, valid)


def late_kernel(size, sides, groups, reps, place_ref, *refs):
    pieces = refs[:sides]
    before_ref, shift_ref, sums_ref, tail_ref, halo_ref, valid_ref = refs[sides : sides + 6]
    outs = refs[sides + 6 : sides + 6 + reps]
    own_out, every, own, right, left_high, left_low = refs[sides + 6 + reps :]
    frames, cols = sides * size, own_out.shape[1]
    feats = every.shape[1]
    rows = feats // (groups * reps)
    side = place_ref[1]
    shift = shift_ref[...]
    every[0:HALO, :] = tail_ref[...]
    place_pieces((size,), side, sides, pieces, every, HALO)
    every[HALO : HALO + frames, :] = every[HALO : HALO + frames, :] - shift
    own_columns(side, sides, every, own)
    for s in range(sides):

        @pl.when(side == s)
        def _():
            own[HALO + frames :, :] = halo_ref[...] - shift[:, s * cols : (s + 1) * cols]

    own_out[...] = own[HALO : HALO + frames, :]
    valid_all = valid_ref[...]
    total = jnp.sum(valid_all)
    count = jnp.maximum(total, 1.0)
    valid = valid_all[valid_all.shape[0] - frames :]
    now = every[HALO : HALO + frames, :]
    weighed = valid * now
    sums = sums_ref[0:1, :] + row_sum(weighed)
    squares = sums_ref[1:2, :] + row_sum(weighed * now)
    later = own[HALO : HALO + frames + LAG, :]
    weighed_later = valid_all[valid_all.shape[0] - frames - LAG :] * later
    sums_next = sums_ref[2:3, 0:cols] + row_sum(weighed_later)
    squares_next = sums_ref[3:4, 0:cols] + row_sum(weighed_later * later)
    own_sums = jnp.zeros((1, cols), F32)
    own_shift = jnp.zeros((1, cols), F32)
    for s in range(sides):
        mine = (side == s).astype(F32)
        own_sums += mine * sums[:, s * cols : (s + 1) * cols]
        own_shift += mine * shift[:, s * cols : (s + 1) * cols]
    first = lax.broadcasted_iota(jnp.int32, (HALO, 1), 0) == 0
    every[HALO + frames :, :] = jnp.where(first, sums, 0.0)
    right[0:HALO, :] = jnp.zeros((HALO, 2 * cols), F32)
    right[HALO : HALO + frames, 0:cols] = valid * own[HALO : HALO + frames, :]
    right[HALO - LAG : HALO + frames, cols : 2 * cols] = weighed_later
    right[HALO + frames :, 0:cols] = jnp.where(first, -own_sums / count, 0.0)
    right[HALO + frames :, cols : 2 * cols] = jnp.where(first, -sums_next / count, 0.0)
    high, low = split_in_two(every[...])
    left_high[...] = high.T
    left_low[...] = low.T
    right_high, right_low = split_in_two(right[...])
    for s in reversed(range(reps)):
        rep = lax.rem(place_ref[2] + s, reps)
        out = outs[s]
        for z in range(groups):
            at = pl.ds(pl.multiple_of((z * reps + rep) * rows, rows), rows)
            part = before_ref[at, :]
            part += jnp.dot(left_high[at, :], right_high, preferred_element_type=F32)
            part += jnp.dot(left_high[at, :], right_low, preferred_element_type=F32)
            part += jnp.dot(left_low[at, :], right_high, preferred_element_type=F32)
            out[z * rows : (z + 1) * rows, :] = part
        end = groups * rows
        fold = feats // (2 * cols)
        mean, square = shift + sums / count, squares - sums * sums / count
        for f in range(fold):
            part = slice(2 * cols * f, 2 * cols * (f + 1))
            out[end + f : end + f + 1, :] = mean[:, part]
            out[end + fold + f : end + fold + f + 1, :] = square[:, part]
        end += 2 * fold
        out[end : end + 1, 0:cols] = own_shift + sums_next / count
        out[end : end + 1, cols : 2 * cols] = squares_next - sums_next * sums_next / count
        out[end + 1 : end + 2, :] = jnp.zeros((1, 2 * cols), F32) + total
        spare = out.shape[0] - end - 2
        if spare:
            out[end + 2 :, :] = jnp.zeros((spare, 2 * cols), F32)


def late_moments(pieces, before, shift, sums, tail, halo, valid, place, sides, groups, reps):
    size, feats = pieces[0].shape
    cols = feats // sides
    frames = sides * size
    vmem = pl.BlockSpec(memory_space=pltpu.VMEM)
    outs = pl.pallas_call(
        functools.partial(late_kernel, size, sides, groups, reps),
        in_specs=[pl.BlockSpec(memory_space=pltpu.SMEM)] + [vmem] * (len(pieces) + 6),
        out_specs=[vmem] * (reps + 1),
        out_shape=[jax.ShapeDtypeStruct((feats // reps + 8, 2 * cols), F32)] * reps
        + [jax.ShapeDtypeStruct((frames, cols), F32)],
        scratch_shapes=[
            pltpu.VMEM((frames + 2 * HALO, feats), F32),
            pltpu.VMEM((frames + 2 * HALO, cols), F32),
            pltpu.VMEM((frames + 2 * HALO, 2 * cols), F32),
            pltpu.VMEM((feats, frames + 2 * HALO), BF16),
            pltpu.VMEM((feats, frames + 2 * HALO), BF16),
        ],
        compiler_params=params(),
        cost_estimate=SMALL,
        name="late_moments",
    )(place, *pieces, before, shift, sums, tail, halo, valid)
    return outs[:reps], outs[reps]


def coded(value, step):
    first = jnp.round(value / step)
    second = jnp.round((value - first * step) * (FINE / step))
    return [first, second]


def decoded(first, second, step):
    return first * step + second * (step / FINE)


def rolled(value, first):
    rows, width = value.shape
    wide = jnp.broadcast_to(value, (8, width)) if rows == 1 else value
    return pltpu.roll(wide, lax.rem(width - first, width), 1)[:rows]


def as_column(row):
    return jnp.broadcast_to(row, (8, row.shape[1])).T[:, 0:1]


def share_kernel(groups, feats, place_ref, *refs):
    parts, outs = refs[: -groups - 1], refs[-groups - 1 :]
    reps, width = len(parts), outs[0].shape[1]
    cols = width // 2
    fold = feats // width
    rows = outs[0].shape[0]
    end = groups * rows
    square = jnp.zeros((1, feats), F32)
    square_next = jnp.zeros((1, cols), F32)
    codes = []
    for part in parts:
        own = part[end : end + 8, :]
        mean = [own[f : f + 1] for f in range(fold)]
        squares = [own[fold + f : fold + f + 1] for f in range(fold)]
        final = own[2 * fold : 2 * fold + 1]
        square += jnp.concatenate(squares, 1)
        square_next += final[:, cols:]
        for line in mean:
            codes += coded(line, MEAN_STEP)
        for line in squares:
            codes += coded(jnp.sqrt(jnp.maximum(line, 0.0)), ROOT_STEP)
        codes += coded(final[:, :cols], MEAN_STEP)
        codes[-2:] = [
            jnp.concatenate(pair, 1)
            for pair in zip(codes[-2:], coded(jnp.sqrt(jnp.maximum(final[:, cols:], 0.0)), ROOT_STEP))
        ]
        codes.append(own[2 * fold + 1 : 2 * fold + 2])
    spare = outs[1].shape[0] - rows - len(codes)
    if spare:
        codes.append(jnp.zeros((spare, width), F32))
    codes = jnp.concatenate(codes, 0).astype(jnp.int32).astype(jnp.int16)
    inverse = lax.rsqrt(jnp.maximum(square, TINY))
    inverse_next = lax.rsqrt(jnp.maximum(square_next, TINY))
    inverse_cols = jnp.concatenate(
        [rolled(inverse, place_ref[1] * cols)[:, :cols], inverse_next], 1
    )
    for s in range(groups):
        there = lax.rem(place_ref[0] + s, groups)
        at = pl.ds(pl.multiple_of(there * rows, rows), rows)
        total = parts[0][at, :]
        for part in parts[1:]:
            total += part[at, :]
        if s == 0:
            outs[0][...] = total
            continue
        first = (there * reps + place_ref[2]) * rows
        ratio = total * as_column(rolled(inverse, first)[:, :rows]) * inverse_cols
        root = jnp.sqrt(jnp.minimum(jnp.abs(ratio), 1.001)) * CODE
        root = jnp.where(ratio < 0.0, -root, root)
        outs[s][0:rows, :] = jnp.round(root).astype(jnp.int32).astype(jnp.int16)
        outs[s][rows:, :] = codes
    outs[groups][...] = codes


def share(parts, place, groups, feats):
    width = parts[0].shape[1]
    rows = (parts[0].shape[0] - 8) // groups
    lines = -(-len(parts) * (4 * (feats // width) + 3) // 16) * 16
    vmem = pl.BlockSpec(memory_space=pltpu.VMEM)
    return pl.pallas_call(
        functools.partial(share_kernel, groups, feats),
        in_specs=[pl.BlockSpec(memory_space=pltpu.SMEM)] + [vmem] * len(parts),
        out_specs=[vmem] * (groups + 1),
        out_shape=[jax.ShapeDtypeStruct((rows, width), F32)]
        + [jax.ShapeDtypeStruct((rows + lines, width), jnp.int16)] * (groups - 1)
        + [jax.ShapeDtypeStruct((lines, width), jnp.int16)],
        compiler_params=params(),
        cost_estimate=SMALL,
        name="share",
    )(place, *parts)


def finish_kernel(reps, place_ref, kept_ref, codes_ref, *refs):
    blocks = refs[:-6]
    shift_ref, early_ref, late_ref, inst_out, lag_out, projections_out = refs[-6:]
    rows, cols = inst_out.shape
    feats = shift_ref.shape[1]
    width = 2 * cols
    fold = feats // width
    count = jnp.zeros((1, 1), F32)
    mean = jnp.zeros((1, feats), F32)
    mean_next = jnp.zeros((1, cols), F32)
    stats = []
    for block in (codes_ref,) + tuple(blocks):
        start = 0 if block is codes_ref else rows
        codes = block[start:, :].astype(jnp.int32).astype(F32)
        at = 0
        for r in range(reps):
            lines = [codes[at + i : at + i + 1] for i in range(4 * fold + 3)]
            at += 4 * fold + 3
            pairs = [(lines[2 * i], lines[2 * i + 1]) for i in range(2 * fold + 1)]
            means = [decoded(*pair, MEAN_STEP) for pair in pairs[:fold]]
            roots = [decoded(*pair, ROOT_STEP) for pair in pairs[fold : 2 * fold]]
            one, two = pairs[2 * fold]
            roots_next = decoded(one[:, cols:], two[:, cols:], ROOT_STEP)
            here = [
                jnp.concatenate(means, 1),
                jnp.concatenate([root * root for root in roots], 1),
                decoded(one[:, :cols], two[:, :cols], MEAN_STEP),
                roots_next * roots_next,
                lines[-1][:, 0:1],
            ]
            stats.append(here)
            count += here[4]
            mean += here[4] * here[0]
            mean_next += here[4] * here[2]
    mean, mean_next = mean / count, mean_next / count
    spread = jnp.zeros((1, feats), F32)
    spread_next = jnp.zeros((1, cols), F32)
    away, away_next = [], []
    for here in stats:
        away.append(here[0] - mean)
        away_next.append(here[2] - mean_next)
        spread += here[1] + here[4] * away[-1] * away[-1]
        spread_next += here[3] + here[4] * away_next[-1] * away_next[-1]
    numbers = jnp.concatenate([here[4] for here in stats], 0)
    scale = 1.0 / jnp.sqrt(spread / count + 1e-05)
    scale_next = 1.0 / jnp.sqrt(spread_next / count + 1e-05)
    away = jnp.concatenate(away, 0)

    first_row = (place_ref[0] * reps + place_ref[2]) * rows
    first_col = place_ref[1] * cols
    right = numbers * jnp.concatenate(
        [rolled(away, first_col)[:, :cols], jnp.concatenate(away_next, 0)], 1
    )
    moment = kept_ref[...] + jnp.dot(
        rolled(away, first_row)[:, :rows].T,
        right,
        precision=lax.Precision.HIGHEST,
        preferred_element_type=F32,
    )
    for g, block in enumerate(blocks):
        here = stats[(g + 1) * reps : (g + 2) * reps]
        root = jnp.sqrt(sum(one[1] for one in here))
        root_next = jnp.sqrt(sum(one[3] for one in here))
        root_rows = as_column(rolled(root, first_row)[:, :rows])
        root_cols = jnp.concatenate([rolled(root, first_col)[:, :cols], root_next], 1)
        code = block[0:rows, :].astype(jnp.int32).astype(F32) * (1.0 / CODE)
        moment += code * jnp.abs(code) * root_rows * root_cols
    scale_cols = rolled(scale, first_col)[:, :cols]
    moment = moment / count * as_column(rolled(scale, first_row)[:, :rows])
    inst_out[...] = moment[:, 0:cols] * scale_cols
    lag_out[...] = moment[:, cols : 2 * cols] * scale_next
    offset = rolled(shift_ref[...] - mean, first_col)[:, :cols]
    split = early_ref.shape[0]
    projections_out[0:split, :] = (early_ref[...] + offset) * scale_cols
    projections_out[split:, :] = (late_ref[...] + offset) * scale_cols


def finish(kept, codes, blocks, shift, early, late, place, reps):
    rows = kept.shape[0]
    cols = early.shape[1]
    frames = early.shape[0] + late.shape[0]
    vmem = pl.BlockSpec(memory_space=pltpu.VMEM)
    return pl.pallas_call(
        functools.partial(finish_kernel, reps),
        in_specs=[pl.BlockSpec(memory_space=pltpu.SMEM)] + [vmem] * (len(blocks) + 5),
        out_specs=[vmem] * 3,
        out_shape=[
            jax.ShapeDtypeStruct((rows, cols), F32),
            jax.ShapeDtypeStruct((rows, cols), F32),
            jax.ShapeDtypeStruct((frames, cols), F32),
        ],
        compiler_params=params(),
        cost_estimate=SMALL,
        name="finish",
    )(place, kept, codes, *blocks, shift, early, late)


def chunk_sizes(frames):
    return (frames // 2, frames // 2)


def with_cap(cap, coords, rank_all, used_pairs, valid, place):
    groups, sides = lax.axis_size("atoms"), lax.axis_size("feat")
    atom_index, feat_index = place[0], place[1]
    width = coords.shape[2]
    frames = coords.shape[1] // groups
    feats = used_pairs.shape[1]
    cols = feats // sides
    sizes = chunk_sizes(frames // sides)

    rank = lax.dynamic_index_in_dim(rank_all, atom_index, 0, keepdims=False)[:, None]
    arrived, start, after = [], 0, rank
    for size in sizes:
        picked = pick(coords, rank, after, cap, place, start, size, groups)
        arrived.append([picked[0]] + [rotated(picked[s], "atoms", s) for s in range(1, groups)])
        after = arrived[-1][1]
        start += sides * size

    atoms = lax.broadcasted_iota(jnp.int32, (groups, 1, width), 0) * width
    atoms = atoms + lax.broadcasted_iota(jnp.int32, (groups, 1, width), 2)
    slots = lax.broadcasted_iota(jnp.int32, (groups, cap, width), 1)
    listed = jnp.max(jnp.where(rank_all[:, None, :] == slots, atoms, -1), axis=2)
    order = lax.rem(atom_index + groups - jnp.arange(groups, dtype=jnp.int32), groups)
    listed = jnp.take(listed, order, axis=0).reshape(groups * cap, 1)
    signs = (listed == used_pairs[0:1]).astype(BF16) - (listed == used_pairs[1:2]).astype(BF16)

    pieces, after = [], arrived[-1][0]
    for blocks in arrived:
        block = distances(blocks, signs, after)
        after = block
        pieces.append([block] + [rotated(block, "feat", s) for s in range(1, sides)])

    opening = sum_or_pick(pieces[0], feat_index)[:HALO]
    opening = lax.dynamic_slice_in_dim(opening, feat_index * cols, cols, 1)
    halo = passed_down(opening, "atoms")

    early = [piece for chunk in pieces[:-1] for piece in chunk]
    before, own_early, shift, sums, tail = early_moments(early, valid, place, sizes[:-1], sides)
    reps = lax.axis_size("rep")
    parts, own_late = late_moments(
        pieces[-1], before, shift, sums, tail, halo, valid, place, sides, groups, reps
    )
    parts = [parts[0]] + [rotated(parts[s], "rep", s) for s in range(1, reps)]
    kept, *blocks, codes = share(parts, place, groups, feats)
    blocks = [rotated(block, "atoms", s + 1) for s, block in enumerate(blocks)]
    corr_inst, corr_lag, projections = finish(
        kept, codes, blocks, shift, own_early, own_late, place, reps
    )
    return corr_inst, corr_lag, projections[None]


def sum_or_pick(blocks, side):
    sides = len(blocks)
    out = blocks[0]
    for s in range(1, sides):
        out = jnp.where(lax.rem(side + sides - s, sides) == 0, blocks[s], out)
    return out


def shards(atom_coords, atom_pairs, traj_ids):
    groups, sides = lax.axis_size("atoms"), lax.axis_size("feat")
    atom_index, feat_index = lax.axis_index("atoms"), lax.axis_index("feat")
    place = jnp.stack([atom_index, feat_index, lax.axis_index("rep")]).astype(jnp.int32)
    width = atom_coords.shape[3]
    frames = atom_coords.shape[1] // groups
    coords = jnp.transpose(atom_coords[0], (1, 0, 2))

    cols = atom_pairs.shape[1]
    used_pairs = jnp.zeros((2, cols * sides), jnp.int32)
    for s in range(sides):
        there = lax.rem(feat_index + sides - s, sides)
        block = atom_pairs if s == 0 else rotated(atom_pairs, "feat", s)
        used_pairs = lax.dynamic_update_slice_in_dim(used_pairs, block, there * cols, 1)

    atoms = jnp.arange(groups * width, dtype=jnp.int32)
    used = jnp.any(used_pairs.reshape(-1)[:, None] == atoms[None, :], axis=0)
    used = used.reshape(groups, width)
    upto = lax.broadcasted_iota(jnp.int32, (width, width), 0) <= lax.broadcasted_iota(
        jnp.int32, (width, width), 1
    )
    order = jnp.dot(used.astype(BF16), upto.astype(BF16), preferred_element_type=F32)
    order = order.astype(jnp.int32)
    rank_all = jnp.where(used, order - 1, -1)

    ids = jnp.concatenate([traj_ids[0], jnp.full((LAG,), -1, jnp.int32)])
    offset = atom_index * frames
    ids_now = lax.dynamic_slice_in_dim(ids, offset, frames)
    ids_later = lax.dynamic_slice_in_dim(ids, offset + LAG, frames)
    valid = (ids_now == ids_later).astype(F32)[:, None]

    cap = min(width, -(-(width * 9 // 16) // 64) * 64)
    def again(carry):
        ranks = rank_all + (carry[0] - 1)
        return carry[0] - 1, with_cap(width, coords, ranks, used_pairs, valid, place)

    overflow = (jnp.max(order) > cap).astype(jnp.int32)
    outs = with_cap(cap, coords, rank_all, used_pairs, valid, place)
    return lax.while_loop(lambda carry: carry[0] > 0, again, (overflow, outs))[1]


def solution(mesh):
    placed = (P(("grp", "rep"), None, None, "atoms"), P(None, "feat"), P(("grp", "rep"), None))
    return jax.shard_map(
        shards,
        mesh=mesh,
        in_specs=placed,
        out_specs=(
            P(("grp", "atoms", "rep"), "feat"),
            P(("grp", "atoms", "rep"), "feat"),
            P(("grp", "rep"), "atoms", "feat"),
        ),
        check_vma=False,
    )
```

time: 190 us -> 135 us (0.71); the launches traced: 187 us -> 135 us
  blocking collectives: 50.5 us -> 0 us
  waiting for transfers between devices: 47.2 us -> 81.1 us
  starting transfers between devices: 28.4 us -> 14.9 us
  between operations: 14.7 us -> 1.54 us
  other arithmetic: 14.4 us -> 6.96 us
  local copies, waits for them, and re-layouts: 8.38 us -> 4.42 us
  Pallas kernels: 21.8 us -> 25.1 us
    ppermute x17 -> x13, waiting for transfers between devices: 25.5 us -> 81.1 us  [rotated(): lax.ppermute(block, axis, [(i, (i + shift) % size) for i in range(size)])]
    psum x2 -> x0, blocking collectives: 50.5 us -> none  [the longest x1 25.9 us: with_cap(): early = lax.psum(early, ('atoms', 'feat', 'rep'))]
    reduce_scatter x1 -> x0, waiting for transfers between devices: 20.7 us -> none  [with_cap(): mine = lax.psum_scatter(local, ring, scatter_dimension=0, tiled=True)]
    ppermute x1, starting transfers between devices: 10.2 us -> 1.92 us  [passed_down(): lax.ppermute(block, axis, [(i + 1, i) for i in range(lax.axis_size(axis)...]
    cond x20 -> x0, local copies, waits for them, and re-layouts: 5.82 us -> none
    ppermute x17 -> x13, starting transfers between devices: 18.2 us -> 12.9 us  [rotated(): lax.ppermute(block, axis, [(i, (i + shift) % size) for i in range(size)])]
    pallas_call x9 -> x8, Pallas kernels: 21.8 us -> 25.1 us  [the longest x2 7.8 us: pick(): pl.pallas_call(functools.partial(pick_kernel, start), in_specs=[pl.BlockS...]
    mul x1 -> x0, other arithmetic: 2.6 us -> none  [with_cap(): (mine[:, cols:] / count - mean_rows * mean_next[None]) * scale_rows]
  transfers between devices with their start and end apart: 19 -> 14, of which waited for: 8 -> 11; matrix products, arithmetic and copies ran while one was open for 6% -> 3% of each run, Pallas kernels for 6% -> 7%
where the time goes in v2:
time: 135 us
  waiting for transfers between devices  81.1 us (60%)
  Pallas kernels  25.1 us (19%)
  starting transfers between devices  14.9 us (11%)
  other arithmetic  6.96 us (5%)
  local copies, waits for them, and re-layouts  4.42 us (3%)
  between operations  1.54 us (1%)
    ppermute x13, waiting for transfers between devices, rotated(): lax.ppermute(block, axis, [(i, (i + shift) % size) for i in range(size)])  81.1 us
    ppermute x13, starting transfers between devices, rotated(): lax.ppermute(block, axis, [(i, (i + shift) % size) for i in range(size)])  12.9 us
    pallas_call x2, Pallas kernels, pick(): pl.pallas_call(functools.partial(pick_kernel, start), in_specs=[pl.BlockS...  7.8 us
    pallas_call x1, Pallas kernels, late_moments(): pl.pallas_call(functools.partial(late_kernel, size, sides, groups, reps),...  6.53 us
    pallas_call x2, Pallas kernels, distances(): pl.pallas_call(distance_kernel, in_specs=[vmem] * (len(blocks) + 1) + [pl...  3.43 us
    reduce_or x1, other arithmetic, shards(): used = jnp.any(used_pairs.reshape(-1)[:, None] == atoms[None, :], axis=0)  3.33 us
    pallas_call x1, Pallas kernels, finish(): pl.pallas_call(functools.partial(finish_kernel, reps), in_specs=[pl.Block...  2.83 us
    pallas_call x1, Pallas kernels, early_moments(): pl.pallas_call(functools.partial(early_kernel, sizes, sides), in_specs=[p...  2.75 us
  transfers between devices with their start and end apart: 14, of which 11 were waited for; matrix products, arithmetic and copies ran while one was open for 3% of the time, Pallas kernels for 7%

profile of v2, /device:TPU:9, one launch (start us, length us, event | category | flops | bytes accessed | tf_op | source)
XLA Modules:
  0.0 134.8 jit_solution(6322056792483301953)
XLA Ops:
  0.6 1.3 collective-permute-start.13
  2.0 0.1 iota_add_fusion.1
  2.0 0.7 constant_dynamic-update-slice_fusion.1
  2.7 0.8 fusion.9
  3.6 0.1 pad_add_fusion.place_ref
  3.7 0.9 copy.21.refs_2_.refs_7_
  4.5 0.0 collective-permute-done.13
  4.6 3.3 %fusion.4 = pred[3072]{0:T(1024)(128)(4,1)S(1)} fusion(s32[2048]{0:T(1024)S(1)} %bitcast.47), kind=kLoop, calls=%fused_computation.25 | loop fusion | flops 12579840 | bytes 11264 | tf_op jit(solution)/shard_map/reduce_or | solution.py:574
  7.9 0.9 add_select_fusion
  8.8 0.9 select_reduce_fusion.1
  9.7 0.6 gather_fusion.1
  10.3 0.1 broadcast_select_fusion.1
  10.3 0.1 select_n.140
  10.4 0.2 copy.20.rank_ref.after_ref
  10.6 3.9 %pick.12 = (bf16[3,64,896]{2,1,0:T(8,128)(2,1)S(1)}, bf16[3,64,896]{2,1,0:T(8,128)(2,1)S(1)}, bf16[3,64,896]{2,1,0:T(8,128)(2,1)S(1)}, bf16[3,64,896]{2,1,0:T(8,128)(2,1)S(1)}) custom-call(s32[3]{0:T(128)S(1)} %pad_add_fusion.place_ref, bf16[3,2048,768]{2,1,0:T(8,128)(2,1)} %bitcast.37, s32[768,1]{1,0:T(8,128)S(1)} %copy.20.rank_ref.after_ref, ...), custom_call_target="tpu_custom_call" | custom-call | flops 1024 | bytes 1024 | tf_op jit(solution)/shard_map/pick/pallas_call | solution.py:70
  14.5 1.3 collective-permute-start.14
  15.9 1.1 collective-permute-start.18
  17.0 1.4 %collective-permute-start.19 = (bf16[3,64,896]{2,1,0:T(8,128)(2,1)S(1)}, bf16[3,64,896]{2,1,0:T(8,128)(2,1)S(1)}, u32[]{:S(2)}, u32[]{:S(2)}) collective-permute-start(bf16[3,64,896]{2,1,0:T(8,128)(2,1)S(1)} %get-tuple-element.271), channel_id=1, source_target_pairs={{0,12},{4,0},{8,4},{12,8},{1,13},{5,1},{9,5},{13,9},{2,14},{6,2},{... | collective-permute-start | bytes 1032200 | tf_op jit(solution)/shard_map/ppermute | solution.py:27
  18.3 1.6 %fusion.5.refs_4_ = bf16[1792,1024]{1,0:T(8,128)(2,1)S(1)} fusion(s32[1024]{0:T(1024)S(1)} %bitcast.44, s32[1024]{0:T(1024)S(1)} %bitcast.43, s32[1792]{0:T(1024)S(1)} %select_n.140), kind=kLoop, calls=%fused_computation.30 | loop fusion | flops 9175040 | bytes 3685376 | tf_op jit(solution)/shard_map/sub | solution.py:523
  20.0 3.2 %collective-permute-done.14.after_ref.refs_1_ = bf16[3,64,896]{2,1,0:T(8,128)(2,1)S(1)} collective-permute-done((bf16[3,64,896]{2,1,0:T(8,128)(2,1)S(1)}, bf16[3,64,896]{2,1,0:T(8,128)(2,1)S(1)}, u32[]{:S(2)}, u32[]{:S(2)}) %collective-permute-start.14) | collective-permute-done | bytes 344096 | tf_op jit(solution)/shard_map/ppermute | solution.py:27
  23.2 3.9 %pick.13 = (bf16[3,64,896]{2,1,0:T(8,128)(2,1)S(1)}, bf16[3,64,896]{2,1,0:T(8,128)(2,1)S(1)}, bf16[3,64,896]{2,1,0:T(8,128)(2,1)S(1)}, bf16[3,64,896]{2,1,0:T(8,128)(2,1)S(1)}) custom-call(s32[3]{0:T(128)S(1)} %pad_add_fusion.place_ref, bf16[3,2048,768]{2,1,0:T(8,128)(2,1)} %bitcast.38, s32[768,1]{1,0:T(8,128)S(1)} %copy.20.rank_ref.after_ref, ...), custom_call_target="tpu_custom_call" | custom-call | flops 1024 | bytes 1024 | tf_op jit(solution)/shard_map/pick/pallas_call | solution.py:70
  27.1 1.4 %collective-permute-start.15 = (bf16[3,64,896]{2,1,0:T(8,128)(2,1)S(1)}, bf16[3,64,896]{2,1,0:T(8,128)(2,1)S(1)}, u32[]{:S(2)}, u32[]{:S(2)}) collective-permute-start(bf16[3,64,896]{2,1,0:T(8,128)(2,1)S(1)} %get-tuple-element.266), channel_id=1, source_target_pairs={{0,4},{4,8},{8,12},{12,0},{1,5},{5,9},{9,13},{13,1},{2,6},{6,10},{... | collective-permute-start | bytes 1032200 | tf_op jit(solution)/shard_map/ppermute | solution.py:27
  28.5 2.9 %collective-permute-start.16 = (bf16[3,64,896]{2,1,0:T(8,128)(2,1)S(1)}, bf16[3,64,896]{2,1,0:T(8,128)(2,1)S(1)}, u32[]{:S(2)}, u32[]{:S(2)}) collective-permute-start(bf16[3,64,896]{2,1,0:T(8,128)(2,1)S(1)} %get-tuple-element.267), channel_id=1, source_target_pairs={{0,8},{4,12},{8,0},{12,4},{1,9},{5,13},{9,1},{13,5},{2,10},{6,14},... | collective-permute-start | bytes 1032200 | tf_op jit(solution)/shard_map/ppermute | solution.py:27
  31.4 0.0 collective-permute-start.17
  31.4 18.8 %collective-permute-done.18.refs_2_ = bf16[3,64,896]{2,1,0:T(8,128)(2,1)S(1)} collective-permute-done((bf16[3,64,896]{2,1,0:T(8,128)(2,1)S(1)}, bf16[3,64,896]{2,1,0:T(8,128)(2,1)S(1)}, u32[]{:S(2)}, u32[]{:S(2)}) %collective-permute-start.18) | collective-permute-done | bytes 344096 | tf_op jit(solution)/shard_map/ppermute | solution.py:27
  50.2 12.2 %collective-permute-done.19.refs_3_ = bf16[3,64,896]{2,1,0:T(8,128)(2,1)S(1)} collective-permute-done((bf16[3,64,896]{2,1,0:T(8,128)(2,1)S(1)}, bf16[3,64,896]{2,1,0:T(8,128)(2,1)S(1)}, u32[]{:S(2)}, u32[]{:S(2)}) %collective-permute-start.19) | collective-permute-done | bytes 344096 | tf_op jit(solution)/shard_map/ppermute | solution.py:27
  62.4 1.7 %distances.4.refs_5_.refs_0_ = f32[128,1024]{1,0:T(8,128)S(1)} custom-call(bf16[3,64,896]{2,1,0:T(8,128)(2,1)S(1)} %get-tuple-element.269.refs_0_, bf16[3,64,896]{2,1,0:T(8,128)(2,1)S(1)} %collective-permute-done.14.after_ref.refs_1_, bf16[3,64,896]{2,1,0:T(8,128)(2,1)S(1)} %collective-permute-done.18.refs_2_, ...), custom_call_target="tpu_custom_call" | custom-call | flops 99999997952 | bytes 1024 | tf_op jit(solution)/shard_map/distances/pallas_call | solution.py:108
  64.1 0.3 collective-permute-start.21
  64.4 2.2 %collective-permute-done.15.refs_1_ = bf16[3,64,896]{2,1,0:T(8,128)(2,1)S(1)} collective-permute-done((bf16[3,64,896]{2,1,0:T(8,128)(2,1)S(1)}, bf16[3,64,896]{2,1,0:T(8,128)(2,1)S(1)}, u32[]{:S(2)}, u32[]{:S(2)}) %collective-permute-start.15) | collective-permute-done | bytes 344096 | tf_op jit(solution)/shard_map/ppermute | solution.py:27
  66.6 7.4 %collective-permute-done.16.refs_2_ = bf16[3,64,896]{2,1,0:T(8,128)(2,1)S(1)} collective-permute-done((bf16[3,64,896]{2,1,0:T(8,128)(2,1)S(1)}, bf16[3,64,896]{2,1,0:T(8,128)(2,1)S(1)}, u32[]{:S(2)}, u32[]{:S(2)}) %collective-permute-start.16) | collective-permute-done | bytes 344096 | tf_op jit(solution)/shard_map/ppermute | solution.py:27
  74.0 3.1 %collective-permute-done.17.refs_3_ = bf16[3,64,896]{2,1,0:T(8,128)(2,1)S(1)} collective-permute-done((bf16[3,64,896]{2,1,0:T(8,128)(2,1)S(1)}, bf16[3,64,896]{2,1,0:T(8,128)(2,1)S(1)}, u32[]{:S(2)}, u32[]{:S(2)}) %collective-permute-start.17) | collective-permute-done | bytes 344096 | tf_op jit(solution)/shard_map/ppermute | solution.py:27
  77.1 1.7 %distances.5.refs_0_ = f32[128,1024]{1,0:T(8,128)S(1)} custom-call(bf16[3,64,896]{2,1,0:T(8,128)(2,1)S(1)} %get-tuple-element.265.refs_5_.refs_0_, bf16[3,64,896]{2,1,0:T(8,128)(2,1)S(1)} %collective-permute-done.15.refs_1_, bf16[3,64,896]{2,1,0:T(8,128)(2,1)S(1)} %collective-permute-done.16.refs_2_, ...), custom_call_target="tpu_custom_call" | custom-call | flops 99999997952 | bytes 1024 | tf_op jit(solution)/shard_map/distances/pallas_call | solution.py:108
  78.8 0.3 collective-permute-start.20
  79.2 1.9 %collective-permute-start.22 = (f32[16,512]{1,0:T(8,128)S(1)}, f32[16,512]{1,0:T(8,128)S(1)}, u32[]{:S(2)}, u32[]{:S(2)}) collective-permute-start(f32[16,512]{1,0:T(8,128)S(1)} %dynamic-slice_select_fusion.1), channel_id=1, source_target_pairs={{4,0},{8,4},{12,8},{5,1},{9,5},{13,9},{6,2},{10,6},{14,10},{7,3},{... | collective-permute-start | bytes 98312 | tf_op jit(solution)/shard_map/ppermute | solution.py:31
  81.1 2.7 %early_moments.6 = (f32[1024,1024]{1,0:T(8,128)S(1)}, f32[256,512]{1,0:T(8,128)S(1)}, f32[1,1024]{1,0:T(1,128)S(1)}, f32[4,1024]{1,0:T(4,128)S(1)}, f32[16,1024]{1,0:T(8,128)S(1)}) custom-call(s32[3]{0:T(128)S(1)} %copy-done.8, f32[128,1024]{1,0:T(8,128)S(1)} %distances.4.refs_5_.refs_0_, f32[128,1024]{1,0:T(8,128)S(1)} %collective-permute-done.21.refs_1_, ...), custom_call_target="tpu_custom_call" | custom-call | flops 99999997952 | bytes 1024 | tf_op jit(solution)/shard_map/early_moments/pallas_call | solution.py:188
  83.9 2.0 %copy-done.1 = f32[1024,1024]{1,0:T(8,128)} copy-done((f32[1024,1024]{1,0:T(8,128)}, f32[1024,1024]{1,0:T(8,128)S(1)}, u32[]{:S(2)}) %copy-start.1) | copy-done | bytes 4194328
  85.8 6.0 %collective-permute-done.20.refs_1_ = f32[128,1024]{1,0:T(8,128)S(1)} collective-permute-done((f32[128,1024]{1,0:T(8,128)S(1)}, f32[128,1024]{1,0:T(8,128)S(1)}, u32[]{:S(2)}, u32[]{:S(2)}) %collective-permute-start.20) | collective-permute-done | bytes 524320 | tf_op jit(solution)/shard_map/ppermute | solution.py:27
  91.9 6.5 %late_moments.6 = (f32[520,1024]{1,0:T(8,128)S(1)}, f32[520,1024]{1,0:T(8,128)S(1)}, f32[256,512]{1,0:T(8,128)S(1)}) custom-call(s32[3]{0:T(128)S(1)} %copy-done.8, f32[128,1024]{1,0:T(8,128)S(1)} %distances.5.refs_0_, f32[128,1024]{1,0:T(8,128)S(1)} %collective-permute-done.20.refs_1_, f32[1024,1024]{1,0:T(8,128)} %copy-done.1, ...), custom_call_target="tpu_custom_call" | custom-call | flops 1024 | bytes 1024 | tf_op jit(solution)/shard_map/late_moments/pallas_call | solution.py:287
  98.4 1.4 %collective-permute-start.23 = (f32[520,1024]{1,0:T(8,128)S(1)}, f32[520,1024]{1,0:T(8,128)S(1)}, u32[]{:S(2)}, u32[]{:S(2)}) collective-permute-start(f32[520,1024]{1,0:T(8,128)S(1)} %get-tuple-element.277), channel_id=1, source_target_pairs={{0,1},{1,0},{2,3},{3,2},{4,5},{5,4},{6,7},{7,6},{8,9},{9,8},{10,11... | collective-permute-start | bytes 6389768 | tf_op jit(solution)/shard_map/ppermute | solution.py:27
  99.8 3.8 %collective-permute-done.23.refs_1_ = f32[520,1024]{1,0:T(8,128)S(1)} collective-permute-done((f32[520,1024]{1,0:T(8,128)S(1)}, f32[520,1024]{1,0:T(8,128)S(1)}, u32[]{:S(2)}, u32[]{:S(2)}) %collective-permute-start.23) | collective-permute-done | bytes 2129952 | tf_op jit(solution)/shard_map/ppermute | solution.py:27
  103.7 1.8 %share.6 = (f32[128,1024]{1,0:T(8,128)S(1)}, s16[144,1024]{1,0:T(8,128)(2,1)S(1)}, s16[144,1024]{1,0:T(8,128)(2,1)S(1)}, s16[144,1024]{1,0:T(8,128)(2,1)S(1)}, s16[16,1024]{1,0:T(8,128)(2,1)S(1)}) custom-call(s32[3]{0:T(128)S(1)} %copy-done.8, f32[520,1024]{1,0:T(8,128)S(1)} %get-tuple-element.276.refs_0_, f32[520,1024]{1,0:T(8,128)S(1)} %collective-permute-done.23.refs_1_), custom_call_target="tpu_custom_call" | custom-call | flops 1024 | bytes 1024 | tf_op jit(solution)/shard_map/share/pallas_call | solution.py:386
  105.5 0.1 collective-permute-start.24
  105.5 0.1 collective-permute-start.25
  105.6 1.4 %collective-permute-start.26 = (s16[144,1024]{1,0:T(8,128)(2,1)S(1)}, s16[144,1024]{1,0:T(8,128)(2,1)S(1)}, u32[]{:S(2)}, u32[]{:S(2)}) collective-permute-start(s16[144,1024]{1,0:T(8,128)(2,1)S(1)} %get-tuple-element.282), channel_id=1, source_target_pairs={{0,12},{4,0},{8,4},{12,8},{1,13},{5,1},{9,5},{13,9},{2,14},{6,2},{... | collective-permute-start | bytes 884744 | tf_op jit(solution)/shard_map/ppermute | solution.py:27
  107.6 6.1 %collective-permute-done.24.refs_0_ = s16[144,1024]{1,0:T(8,128)(2,1)S(1)} collective-permute-done((s16[144,1024]{1,0:T(8,128)(2,1)S(1)}, s16[144,1024]{1,0:T(8,128)(2,1)S(1)}, u32[]{:S(2)}, u32[]{:S(2)}) %collective-permute-start.24) | collective-permute-done | bytes 294944 | tf_op jit(solution)/shard_map/ppermute | solution.py:27
  113.7 17.1 %collective-permute-done.25.refs_1_ = s16[144,1024]{1,0:T(8,128)(2,1)S(1)} collective-permute-done((s16[144,1024]{1,0:T(8,128)(2,1)S(1)}, s16[144,1024]{1,0:T(8,128)(2,1)S(1)}, u32[]{:S(2)}, u32[]{:S(2)}) %collective-permute-start.25) | collective-permute-done | bytes 294944 | tf_op jit(solution)/shard_map/ppermute | solution.py:27
  130.8 1.1 collective-permute-done.26.refs_2_
  132.0 2.8 %finish.6 = (f32[128,512]{1,0:T(8,128)}, f32[128,512]{1,0:T(8,128)}, f32[512,512]{1,0:T(8,128)}) custom-call(s32[3]{0:T(128)S(1)} %copy-done.8, f32[128,1024]{1,0:T(8,128)S(1)} %get-tuple-element.278.kept_ref, s16[16,1024]{1,0:T(8,128)(2,1)S(1)} %get-tuple-element.279.codes_ref, s16[144,1024]{1,0:T(8,128)(2,1)S(1)} %collective-permute-done.24.refs_0_, ...), custom_call_target="tpu_custom_call" | custom-call | flops 1024 | bytes 1024 | tf_op jit(solution)/shard_map/finish/pallas_call | solution.py:481
  (31 shorter events, 0.1 us)
Async XLA Ops:
  0.6 3.9 %collective-permute-start.13 = (s32[2,512]{1,0:T(2,128)}, s32[2,512]{1,0:T(2,128)S(1)}, u32[]{:S(2)}, u32[]{:S(2)}) collective-permute-start(s32[2,512]{1,0:T(2,128)} %param.6), channel_id=1, source_target_pairs={{0,2},{2,0},{1,3},{3,1},{4,6},{6,4},{5,7},{7,5},{8,10},{10,8},{9,1... | collective-permute-start | bytes 12296 | tf_op jit(solution)/shard_map/ppermute | solution.py:27
  3.7 19.5 %copy-start.7 = (s32[3]{0:T(128)}, s32[3]{0:T(128)S(1)}, u32[]{:S(2)}) copy-start(s32[3]{0:T(128)S(1)} %pad_add_fusion.place_ref) | copy-start | bytes 40
  4.5 4.2 %copy-start.4 = (s32[2,1024]{1,0:T(2,128)}, s32[2,1024]{1,0:T(2,128)S(1)}, u32[]{:S(2)}) copy-start(s32[2,1024]{1,0:T(2,128)S(1)} %constant_dynamic-update-slice_fusion) | copy-start | bytes 24580
  8.8 1.6 %copy-start.10 = (s32[4,768]{1,0:T(4,128)}, s32[4,768]{1,0:T(4,128)S(1)}, u32[]{:S(2)}) copy-start(s32[4,768]{1,0:T(4,128)S(1)} %get-tuple-element.485) | copy-start | bytes 36868
  14.5 8.7 %collective-permute-start.14 = (bf16[3,64,896]{2,1,0:T(8,128)(2,1)S(1)}, bf16[3,64,896]{2,1,0:T(8,128)(2,1)S(1)}, u32[]{:S(2)}, u32[]{:S(2)}) collective-permute-start(bf16[3,64,896]{2,1,0:T(8,128)(2,1)S(1)} %get-tuple-element.264), channel_id=1, source_target_pairs={{0,4},{4,8},{8,12},{12,0},{1,5},{5,9},{9,13},{13,1},{2,6},{6,10},{... | collective-permute-start | bytes 1032200 | tf_op jit(solution)/shard_map/ppermute | solution.py:27
  15.9 34.3 %collective-permute-start.18 = (bf16[3,64,896]{2,1,0:T(8,128)(2,1)S(1)}, bf16[3,64,896]{2,1,0:T(8,128)(2,1)S(1)}, u32[]{:S(2)}, u32[]{:S(2)}) collective-permute-start(bf16[3,64,896]{2,1,0:T(8,128)(2,1)S(1)} %get-tuple-element.270), channel_id=1, source_target_pairs={{0,8},{4,12},{8,0},{12,4},{1,9},{5,13},{9,1},{13,5},{2,10},{6,14},... | collective-permute-start | bytes 1032200 | tf_op jit(solution)/shard_map/ppermute | solution.py:27
  17.0 45.4 %collective-permute-start.19 = (bf16[3,64,896]{2,1,0:T(8,128)(2,1)S(1)}, bf16[3,64,896]{2,1,0:T(8,128)(2,1)S(1)}, u32[]{:S(2)}, u32[]{:S(2)}) collective-permute-start(bf16[3,64,896]{2,1,0:T(8,128)(2,1)S(1)} %get-tuple-element.271), channel_id=1, source_target_pairs={{0,12},{4,0},{8,4},{12,8},{1,13},{5,1},{9,5},{13,9},{2,14},{6,2},{... | collective-permute-start | bytes 1032200 | tf_op jit(solution)/shard_map/ppermute | solution.py:27
  27.1 39.5 %collective-permute-start.15 = (bf16[3,64,896]{2,1,0:T(8,128)(2,1)S(1)}, bf16[3,64,896]{2,1,0:T(8,128)(2,1)S(1)}, u32[]{:S(2)}, u32[]{:S(2)}) collective-permute-start(bf16[3,64,896]{2,1,0:T(8,128)(2,1)S(1)} %get-tuple-element.266), channel_id=1, source_target_pairs={{0,4},{4,8},{8,12},{12,0},{1,5},{5,9},{9,13},{13,1},{2,6},{6,10},{... | collective-permute-start | bytes 1032200 | tf_op jit(solution)/shard_map/ppermute | solution.py:27
  28.5 45.4 %collective-permute-start.16 = (bf16[3,64,896]{2,1,0:T(8,128)(2,1)S(1)}, bf16[3,64,896]{2,1,0:T(8,128)(2,1)S(1)}, u32[]{:S(2)}, u32[]{:S(2)}) collective-permute-start(bf16[3,64,896]{2,1,0:T(8,128)(2,1)S(1)} %get-tuple-element.267), channel_id=1, source_target_pairs={{0,8},{4,12},{8,0},{12,4},{1,9},{5,13},{9,1},{13,5},{2,10},{6,14},... | collective-permute-start | bytes 1032200 | tf_op jit(solution)/shard_map/ppermute | solution.py:27
  31.4 45.7 %collective-permute-start.17 = (bf16[3,64,896]{2,1,0:T(8,128)(2,1)S(1)}, bf16[3,64,896]{2,1,0:T(8,128)(2,1)S(1)}, u32[]{:S(2)}, u32[]{:S(2)}) collective-permute-start(bf16[3,64,896]{2,1,0:T(8,128)(2,1)S(1)} %get-tuple-element.268), channel_id=1, source_target_pairs={{0,12},{4,0},{8,4},{12,8},{1,13},{5,1},{9,5},{13,9},{2,14},{6,2},{... | collective-permute-start | bytes 1032200 | tf_op jit(solution)/shard_map/ppermute | solution.py:27
  64.1 17.0 %copy-start.2 = (f32[512,1]{1,0:T(8,128)S(1)}, f32[512,1]{1,0:T(8,128)}, u32[]{:S(2)}) copy-start(f32[512,1]{1,0:T(8,128)} %copy.21.refs_2_.refs_7_) | copy-start | bytes 6148
  64.1 17.0 %copy-start.8 = (s32[3]{0:T(128)S(1)}, s32[3]{0:T(128)}, u32[]{:S(2)}) copy-start(s32[3]{0:T(128)} %copy-done.7) | copy-start | bytes 40
  64.1 15.0 %collective-permute-start.21 = (f32[128,1024]{1,0:T(8,128)S(1)}, f32[128,1024]{1,0:T(8,128)S(1)}, u32[]{:S(2)}, u32[]{:S(2)}) collective-permute-start(f32[128,1024]{1,0:T(8,128)S(1)} %distances.4.refs_5_.refs_0_), channel_id=1, source_target_pairs={{0,2},{2,0},{1,3},{3,1},{4,6},{6,4},{5,7},{7,5},{8,10},{10,8},{9,1... | collective-permute-start | bytes 1572872 | tf_op jit(solution)/shard_map/ppermute | solution.py:27
  78.8 13.1 %collective-permute-start.20 = (f32[128,1024]{1,0:T(8,128)S(1)}, f32[128,1024]{1,0:T(8,128)S(1)}, u32[]{:S(2)}, u32[]{:S(2)}) collective-permute-start(f32[128,1024]{1,0:T(8,128)S(1)} %distances.5.refs_0_), channel_id=1, source_target_pairs={{0,2},{2,0},{1,3},{3,1},{4,6},{6,4},{5,7},{7,5},{8,10},{10,8},{9,1... | collective-permute-start | bytes 1572872 | tf_op jit(solution)/shard_map/ppermute | solution.py:27
  79.2 6.7 %collective-permute-start.22 = (f32[16,512]{1,0:T(8,128)S(1)}, f32[16,512]{1,0:T(8,128)S(1)}, u32[]{:S(2)}, u32[]{:S(2)}) collective-permute-start(f32[16,512]{1,0:T(8,128)S(1)} %dynamic-slice_select_fusion.1), channel_id=1, source_target_pairs={{4,0},{8,4},{12,8},{5,1},{9,5},{13,9},{6,2},{10,6},{14,10},{7,3},{... | collective-permute-start | bytes 98312 | tf_op jit(solution)/shard_map/ppermute | solution.py:31
  83.9 2.0 %copy-start.1 = (f32[1024,1024]{1,0:T(8,128)}, f32[1024,1024]{1,0:T(8,128)S(1)}, u32[]{:S(2)}) copy-start(f32[1024,1024]{1,0:T(8,128)S(1)} %get-tuple-element.272.refs_2_) | copy-start | bytes 12582916
  91.9 42.9 %copy-start.5 = (s32[2,1024]{1,0:T(2,128)S(1)}, s32[2,1024]{1,0:T(2,128)}, u32[]{:S(2)}) copy-start(s32[2,1024]{1,0:T(2,128)} %copy-done.4) | copy-start | bytes 24580
  91.9 42.9 %copy-start.11 = (s32[4,768]{1,0:T(4,128)S(1)}, s32[4,768]{1,0:T(4,128)}, u32[]{:S(2)}) copy-start(s32[4,768]{1,0:T(4,128)} %copy-done.10) | copy-start | bytes 36868
  98.4 5.2 %collective-permute-start.23 = (f32[520,1024]{1,0:T(8,128)S(1)}, f32[520,1024]{1,0:T(8,128)S(1)}, u32[]{:S(2)}, u32[]{:S(2)}) collective-permute-start(f32[520,1024]{1,0:T(8,128)S(1)} %get-tuple-element.277), channel_id=1, source_target_pairs={{0,1},{1,0},{2,3},{3,2},{4,5},{5,4},{6,7},{7,6},{8,9},{9,8},{10,11... | collective-permute-start | bytes 6389768 | tf_op jit(solution)/shard_map/ppermute | solution.py:27
  105.5 8.3 %collective-permute-start.24 = (s16[144,1024]{1,0:T(8,128)(2,1)S(1)}, s16[144,1024]{1,0:T(8,128)(2,1)S(1)}, u32[]{:S(2)}, u32[]{:S(2)}) collective-permute-start(s16[144,1024]{1,0:T(8,128)(2,1)S(1)} %get-tuple-element.280), channel_id=1, source_target_pairs={{0,4},{4,8},{8,12},{12,0},{1,5},{5,9},{9,13},{13,1},{2,6},{6,10},{... | collective-permute-start | bytes 884744 | tf_op jit(solution)/shard_map/ppermute | solution.py:27
  105.5 25.3 %collective-permute-start.25 = (s16[144,1024]{1,0:T(8,128)(2,1)S(1)}, s16[144,1024]{1,0:T(8,128)(2,1)S(1)}, u32[]{:S(2)}, u32[]{:S(2)}) collective-permute-start(s16[144,1024]{1,0:T(8,128)(2,1)S(1)} %get-tuple-element.281), channel_id=1, source_target_pairs={{0,8},{4,12},{8,0},{12,4},{1,9},{5,13},{9,1},{13,5},{2,10},{6,14},... | collective-permute-start | bytes 884744 | tf_op jit(solution)/shard_map/ppermute | solution.py:27
  105.6 26.4 %collective-permute-start.26 = (s16[144,1024]{1,0:T(8,128)(2,1)S(1)}, s16[144,1024]{1,0:T(8,128)(2,1)S(1)}, u32[]{:S(2)}, u32[]{:S(2)}) collective-permute-start(s16[144,1024]{1,0:T(8,128)(2,1)S(1)} %get-tuple-element.282), channel_id=1, source_target_pairs={{0,12},{4,0},{8,4},{12,8},{1,13},{5,1},{9,5},{13,9},{2,14},{6,2},{... | collective-permute-start | bytes 884744 | tf_op jit(solution)/shard_map/ppermute | solution.py:27

commit v3 on v2

--- a/solution.py
+++ b/solution.py
@@ -15,6 +15,7 @@
 MEAN_STEP = 0.001
 ROOT_STEP = 0.02
 TINY = 1e-30
+REACH = 1e-6
 VMEM_LIMIT = 48 * 1024 * 1024
 F32 = jnp.float32
 BF16 = jnp.bfloat16
@@ -35,37 +36,97 @@
     return pltpu.CompilerParams(vmem_limit_bytes=VMEM_LIMIT)
 
 
-def pick_kernel(start, place_ref, coords_ref, rank_ref, after_ref, *refs):
-    groups = len(refs) - 2
-    outs, rows_ref, sems = refs[:groups], refs[groups], refs[groups + 1]
-    size, width = rows_ref.shape[2], rows_ref.shape[3]
-    cap = outs[0].shape[2] // 2
+def start_rows(sizes, start, place_ref, coords_ref, rows_refs, sems):
+    groups, sides = rows_refs[0].shape[0], lax.axis_size("feat")
     frames = coords_ref.shape[1] // groups
     copies = []
-    for s in range(groups):
-        there = lax.rem(place_ref[0] + s, groups)
-        row = pl.multiple_of(there * frames + start + place_ref[1] * size, CHUNK)
-        copies.append(
-            pltpu.make_async_copy(
-                coords_ref.at[:, pl.ds(row, size), :], rows_ref.at[s], sems.at[s]
+    for j, size in enumerate(sizes):
+        for s in range(groups):
+            there = lax.rem(place_ref[0] + s, groups)
+            row = there * frames + start + place_ref[1] * size
+            copies.append(
+                pltpu.make_async_copy(
+                    coords_ref.at[:, pl.ds(pl.multiple_of(row, HALO), size), :],
+                    rows_refs[j].at[s],
+                    sems.at[j, s],
+                )
             )
-        )
+        start += sides * size
     for copy in copies:
         copy.start()
-    slots = lax.broadcasted_iota(jnp.int32, (width, cap), 1)
-    chosen = (rank_ref[...] == slots).astype(F32).astype(BF16)
-    half = size // 2
-    for s in range(groups):
+    return copies
+
+
+def pick_rows(rows, chosen, out):
+    _, size, width = rows.shape
+    cap, half = chosen.shape[1], size // 2
+    picked = jnp.dot(
+        rows[...].reshape(3 * size, width), chosen, preferred_element_type=F32
+    ).astype(BF16)
+    picked = picked.reshape(3, size, cap)
+    out[:, :, 0:cap] = picked[:, :half, :]
+    out[:, :, cap : 2 * cap] = picked[:, half:, :]
+
+
+def first_pick_kernel(sides, place_ref, coords_ref, ids_ref, *refs):
+    pairs, refs = refs[:sides], refs[sides:]
+    chosen_ref, ids_out, pairs_out, refs = refs[0], refs[1], refs[2 : 2 + sides], refs[2 + sides :]
+    outs, rows_ref, sems = refs[:-2], refs[-2], refs[-1]
+    width, cap = chosen_ref.shape
+    copies = start_rows((rows_ref.shape[2],), 0, place_ref, coords_ref, [rows_ref], sems)
+    ids_out[...] = ids_ref[...]
+    for block, copy in zip(pairs, pairs_out):
+        copy[...] = block[...]
+    rank, _ = ranked(pairs, place_ref[0] * width, width, upto(width))
+    lanes = lax.broadcasted_iota(jnp.int32, (width, 128), 1)
+    for l in range(0, cap, 128):
+        some = min(128, cap - l)
+        here = (rank == (lanes + l).astype(F32)).astype(F32).astype(BF16)
+        chosen_ref[:, l : l + some] = here[:, :some]
+    for s, out in enumerate(outs):
         copies[s].wait()
-        rows = rows_ref[s].reshape(3 * size, width)
-        picked = jnp.dot(rows, chosen, preferred_element_type=F32).astype(BF16)
-        picked = picked.reshape(3, size, cap)
-        outs[s][:, :, 0:cap] = picked[:, :half, :]
-        outs[s][:, :, cap : 2 * cap] = picked[:, half:, :]
-
-
-def pick(coords, rank, after, cap, place, start, size, groups):
+        pick_rows(rows_ref.at[s], chosen_ref[...], out)
+
+
+def first_pick(coords, ids, pairs, cap, place, size, groups):
     width = coords.shape[2]
+    vmem = pl.BlockSpec(memory_space=pltpu.VMEM)
+    outs = pl.pallas_call(
+        functools.partial(first_pick_kernel, len(pairs)),
+        in_specs=[
+            pl.BlockSpec(memory_space=pltpu.SMEM),
+            pl.BlockSpec(memory_space=pltpu.HBM),
+        ]
+        + [vmem] * (len(pairs) + 1),
+        out_specs=[vmem] * (2 + len(pairs) + groups),
+        out_shape=[
+            jax.ShapeDtypeStruct((width, cap), BF16),
+            jax.ShapeDtypeStruct(ids.shape, ids.dtype),
+        ]
+        + [jax.ShapeDtypeStruct(block.shape, block.dtype) for block in pairs]
+        + [jax.ShapeDtypeStruct((3, size // 2, 2 * cap), BF16)] * groups,
+        scratch_shapes=[
+            pltpu.VMEM((groups, 3, size, width), BF16),
+            pltpu.SemaphoreType.DMA((1, groups)),
+        ],
+        compiler_params=params(),
+        cost_estimate=SMALL,
+        name="first_pick",
+    )(place, coords, ids, *pairs)
+    sides = len(pairs)
+    return outs[0], outs[1], outs[2 : 2 + sides], outs[2 + sides :]
+
+
+def pick_kernel(start, place_ref, coords_ref, chosen_ref, after_ref, *refs):
+    outs, rows_ref, sems = refs[:-2], refs[-2], refs[-1]
+    copies = start_rows((rows_ref.shape[2],), start, place_ref, coords_ref, [rows_ref], sems)
+    for s, out in enumerate(outs):
+        copies[s].wait()
+        pick_rows(rows_ref.at[s], chosen_ref[...], out)
+
+
+def pick(coords, chosen, after, place, start, size, groups):
+    width, cap = chosen.shape
     vmem = pl.BlockSpec(memory_space=pltpu.VMEM)
     return pl.pallas_call(
         functools.partial(pick_kernel, start),
@@ -79,16 +140,34 @@
         out_shape=[jax.ShapeDtypeStruct((3, size // 2, 2 * cap), BF16)] * groups,
         scratch_shapes=[
             pltpu.VMEM((groups, 3, size, width), BF16),
-            pltpu.SemaphoreType.DMA((groups,)),
+            pltpu.SemaphoreType.DMA((1, groups)),
         ],
         compiler_params=params(),
         cost_estimate=SMALL,
         name="pick",
-    )(place, coords, rank, after)
+    )(place, coords, chosen, after)
+
+
+def coded(value, step):
+    first = jnp.round(value / step)
+    second = jnp.round((value - first * step) * (FINE / step))
+    return [first, second]
+
+
+def decoded(first, second, step):
+    return first * step + second * (step / FINE)
+
+
+def decoded_piece(codes, rows):
+    size = codes.shape[0] - HALO
+    ends = codes[size:, :].astype(jnp.int32).astype(F32)
+    middle = decoded(ends[0:1], ends[1:2], MEAN_STEP)
+    reach = decoded(ends[2:3], ends[3:4], MEAN_STEP)
+    return middle + codes[0:rows, :].astype(jnp.int32).astype(F32) * (reach * (1.0 / CODE))
 
 
 def distance_kernel(*refs):
-    blocks, (signs_ref, after_ref, out, joined) = refs[:-4], refs[-4:]
+    blocks, (signs_ref, after_ref, out, codes_out, joined) = refs[:-5], refs[-5:]
     half, cap = blocks[0].shape[1], blocks[0].shape[2] // 2
     size = 2 * half
     for s, block in enumerate(blocks):
@@ -99,7 +178,17 @@
     delta = jnp.dot(joined[...], signs_ref[...], preferred_element_type=F32)
     square = delta * delta
     total = square[:size] + square[size : 2 * size] + square[2 * size :]
-    out[...] = jnp.sqrt(total + 0.01)
+    value = jnp.sqrt(total + 0.01)
+    out[...] = value
+    least, most = jnp.min(value, 0, keepdims=True), jnp.max(value, 0, keepdims=True)
+    ends = coded(0.5 * (most + least), MEAN_STEP) + coded(0.5 * (most - least), MEAN_STEP)
+    middle = decoded(ends[0], ends[1], MEAN_STEP)
+    reach = decoded(ends[2], ends[3], MEAN_STEP)
+    ratio = (value - middle) * (CODE / jnp.maximum(reach, REACH))
+    ratio = jnp.round(jnp.clip(ratio, -32767.0, 32767.0))
+    codes_out[0:size, :] = ratio.astype(jnp.int32).astype(jnp.int16)
+    ends = jnp.concatenate(ends + [jnp.zeros((HALO - 4, out.shape[1]), F32)], 0)
+    codes_out[size:, :] = ends.astype(jnp.int32).astype(jnp.int16)
 
 
 def distances(blocks, signs, after):
@@ -108,8 +197,11 @@
     return pl.pallas_call(
         distance_kernel,
         in_specs=[vmem] * (len(blocks) + 1) + [pl.BlockSpec(memory_space=pl.ANY)],
-        out_specs=vmem,
-        out_shape=jax.ShapeDtypeStruct((size, signs.shape[1]), F32),
+        out_specs=[vmem] * 2,
+        out_shape=[
+            jax.ShapeDtypeStruct((size, signs.shape[1]), F32),
+            jax.ShapeDtypeStruct((size + HALO, signs.shape[1]), jnp.int16),
+        ],
         scratch_shapes=[pltpu.VMEM((3 * size, signs.shape[0]), BF16)],
         compiler_params=params(),
         cost_estimate=LARGE,
@@ -137,7 +229,8 @@
         for s in range(sides):
             there = lax.rem(side + sides - s, sides)
             at = pl.multiple_of(row + there * size, HALO)
-            every[pl.ds(at, size), :] = pieces[j * sides + s][...]
+            piece = pieces[j * sides + s]
+            every[pl.ds(at, size), :] = piece[...] if s == 0 else decoded_piece(piece, size)
         row += sides * size
 
 
@@ -198,7 +291,7 @@
         ],
         scratch_shapes=[pltpu.VMEM((frames, feats), F32), pltpu.VMEM((frames, cols), F32)],
         compiler_params=params(),
-        cost_estimate=LARGE,
+        cost_estimate=SMALL,
         name="early_moments",
     )(place, *pieces, valid)
 
@@ -304,16 +397,6 @@
     return outs[:reps], outs[reps]
 
 
-def coded(value, step):
-    first = jnp.round(value / step)
-    second = jnp.round((value - first * step) * (FINE / step))
-    return [first, second]
-
-
-def decoded(first, second, step):
-    return first * step + second * (step / FINE)
-
-
 def rolled(value, first):
     rows, width = value.shape
     wide = jnp.broadcast_to(value, (8, width)) if rows == 1 else value
@@ -493,42 +576,113 @@
     )(place, kept, codes, *blocks, shift, early, late)
 
 
+def upto(width):
+    rows = lax.broadcasted_iota(jnp.int32, (width, width), 0)
+    lanes = lax.broadcasted_iota(jnp.int32, (width, width), 1)
+    return (lanes <= rows).astype(F32).astype(BF16)
+
+
+def ranked(pairs, first, width, below):
+    atoms = lax.broadcasted_iota(jnp.int32, (width, 128), 0) + first
+    hit = jnp.zeros((width, 128), F32)
+    for block in pairs:
+        for r in range(2):
+            for l in range(0, block.shape[1], 128):
+                hit = jnp.where(block[r : r + 1, l : l + 128] == atoms, 1.0, hit)
+    used = jnp.broadcast_to(jnp.max(hit, axis=1, keepdims=True), (width, 128))
+    order = jnp.dot(below, used.astype(BF16), preferred_element_type=F32)
+    return jnp.where(used > 0.0, order - 1.0, -1.0), order[width - 1 : width, :]
+
+
+def signs_kernel(groups, width, cap, place_ref, after_ref, *refs):
+    pairs, (signs_out, most_out) = refs[:-2], refs[-2:]
+    sides = len(pairs)
+    below = upto(width)
+    number = lax.broadcasted_iota(jnp.int32, (width, 128), 0) + 1
+    high = (number // 8).astype(F32).astype(BF16)
+    low = (number % 8).astype(F32).astype(BF16)
+    slots = lax.broadcasted_iota(jnp.int32, (cap, width), 0).astype(F32)
+    most = jnp.zeros((1, 128), F32)
+    for s in range(groups):
+        first = lax.rem(place_ref[0] + groups - s, groups) * width
+        rank, count = ranked(pairs, first, width, below)
+        most = jnp.maximum(most, count)
+        chosen = (rank.T[0:1, :] == slots).astype(F32).astype(BF16)
+        listed = 8.0 * jnp.dot(chosen, high, preferred_element_type=F32)
+        listed += jnp.dot(chosen, low, preferred_element_type=F32)
+        listed = listed.astype(jnp.int32) - 1
+        listed = jnp.where(listed < 0, -1, listed + first)
+        for b, block in enumerate(pairs):
+            cols = block.shape[1]
+            there = lax.rem(place_ref[1] + sides - b, sides) * cols
+            for l in range(0, cols, 128):
+                one = (block[0:1, l : l + 128] == listed).astype(F32)
+                two = (block[1:2, l : l + 128] == listed).astype(F32)
+                at = pl.ds(pl.multiple_of(there + l, 128), 128)
+                signs_out[s * cap : (s + 1) * cap, at] = (one - two).astype(BF16)
+    most_out[...] = most
+
+
+def pair_signs(pairs, after, place, groups, width, cap):
+    feats = len(pairs) * pairs[0].shape[1]
+    vmem = pl.BlockSpec(memory_space=pltpu.VMEM)
+    return pl.pallas_call(
+        functools.partial(signs_kernel, groups, width, cap),
+        in_specs=[pl.BlockSpec(memory_space=pltpu.SMEM), pl.BlockSpec(memory_space=pl.ANY)]
+        + [vmem] * len(pairs),
+        out_specs=[vmem] * 2,
+        out_shape=[
+            jax.ShapeDtypeStruct((groups * cap, feats), BF16),
+            jax.ShapeDtypeStruct((1, 128), F32),
+        ],
+        compiler_params=params(),
+        cost_estimate=SMALL,
+        name="pair_signs",
+    )(place, after, *pairs)
+
+
 def chunk_sizes(frames):
-    return (frames // 2, frames // 2)
-
-
-def with_cap(cap, coords, rank_all, used_pairs, valid, place):
+    last = frames // 8 * 3
+    return frames - last, last
+
+
+def with_cap(cap, coords, pairs, traj_ids, place):
     groups, sides = lax.axis_size("atoms"), lax.axis_size("feat")
     atom_index, feat_index = place[0], place[1]
     width = coords.shape[2]
     frames = coords.shape[1] // groups
-    feats = used_pairs.shape[1]
-    cols = feats // sides
+    cols = pairs[0].shape[1]
+    feats = cols * sides
     sizes = chunk_sizes(frames // sides)
 
-    rank = lax.dynamic_index_in_dim(rank_all, atom_index, 0, keepdims=False)[:, None]
-    arrived, start, after = [], 0, rank
-    for size in sizes:
-        picked = pick(coords, rank, after, cap, place, start, size, groups)
+    chosen, traj_ids, pairs, picked = first_pick(
+        coords, traj_ids, pairs, cap, place, sizes[0], groups
+    )
+    arrived, start = [], 0
+    for j, size in enumerate(sizes):
+        if j:
+            picked = pick(coords, chosen, arrived[-1][1], place, start, size, groups)
         arrived.append([picked[0]] + [rotated(picked[s], "atoms", s) for s in range(1, groups)])
-        after = arrived[-1][1]
         start += sides * size
 
-    atoms = lax.broadcasted_iota(jnp.int32, (groups, 1, width), 0) * width
-    atoms = atoms + lax.broadcasted_iota(jnp.int32, (groups, 1, width), 2)
-    slots = lax.broadcasted_iota(jnp.int32, (groups, cap, width), 1)
-    listed = jnp.max(jnp.where(rank_all[:, None, :] == slots, atoms, -1), axis=2)
-    order = lax.rem(atom_index + groups - jnp.arange(groups, dtype=jnp.int32), groups)
-    listed = jnp.take(listed, order, axis=0).reshape(groups * cap, 1)
-    signs = (listed == used_pairs[0:1]).astype(BF16) - (listed == used_pairs[1:2]).astype(BF16)
+    signs, most_used = pair_signs(pairs, arrived[-1][0], place, groups, width, cap)
+
+    ids = jnp.concatenate([traj_ids[0], jnp.full((LAG,), -1, jnp.int32)])
+    offset = atom_index * frames
+    ids_now = lax.dynamic_slice_in_dim(ids, offset, frames)
+    ids_later = lax.dynamic_slice_in_dim(ids, offset + LAG, frames)
+    valid = (ids_now == ids_later).astype(F32)[:, None]
 
     pieces, after = [], arrived[-1][0]
     for blocks in arrived:
-        block = distances(blocks, signs, after)
+        block, codes = distances(blocks, signs, after)
         after = block
-        pieces.append([block] + [rotated(block, "feat", s) for s in range(1, sides)])
-
-    opening = sum_or_pick(pieces[0], feat_index)[:HALO]
+        pieces.append([block] + [rotated(codes, "feat", s) for s in range(1, sides)])
+
+    opening = pieces[0][0][:HALO]
+    for s in range(1, sides):
+        first = lax.rem(feat_index + sides - s, sides) == 0
+        opening = jnp.where(first, decoded_piece(pieces[0][s], HALO), opening)
     opening = lax.dynamic_slice_in_dim(opening, feat_index * cols, cols, 1)
     halo = passed_down(opening, "atoms")
 
@@ -544,55 +698,23 @@
     corr_inst, corr_lag, projections = finish(
         kept, codes, blocks, shift, own_early, own_late, place, reps
     )
-    return corr_inst, corr_lag, projections[None]
-
-
-def sum_or_pick(blocks, side):
-    sides = len(blocks)
-    out = blocks[0]
-    for s in range(1, sides):
-        out = jnp.where(lax.rem(side + sides - s, sides) == 0, blocks[s], out)
-    return out
+    return (corr_inst, corr_lag, projections[None]), most_used[0, 0]
 
 
 def shards(atom_coords, atom_pairs, traj_ids):
-    groups, sides = lax.axis_size("atoms"), lax.axis_size("feat")
-    atom_index, feat_index = lax.axis_index("atoms"), lax.axis_index("feat")
-    place = jnp.stack([atom_index, feat_index, lax.axis_index("rep")]).astype(jnp.int32)
+    place = [lax.axis_index(axis) for axis in ("atoms", "feat", "rep")]
+    place = jnp.stack(place).astype(jnp.int32)
     width = atom_coords.shape[3]
-    frames = atom_coords.shape[1] // groups
     coords = jnp.transpose(atom_coords[0], (1, 0, 2))
-
-    cols = atom_pairs.shape[1]
-    used_pairs = jnp.zeros((2, cols * sides), jnp.int32)
-    for s in range(sides):
-        there = lax.rem(feat_index + sides - s, sides)
-        block = atom_pairs if s == 0 else rotated(atom_pairs, "feat", s)
-        used_pairs = lax.dynamic_update_slice_in_dim(used_pairs, block, there * cols, 1)
-
-    atoms = jnp.arange(groups * width, dtype=jnp.int32)
-    used = jnp.any(used_pairs.reshape(-1)[:, None] == atoms[None, :], axis=0)
-    used = used.reshape(groups, width)
-    upto = lax.broadcasted_iota(jnp.int32, (width, width), 0) <= lax.broadcasted_iota(
-        jnp.int32, (width, width), 1
-    )
-    order = jnp.dot(used.astype(BF16), upto.astype(BF16), preferred_element_type=F32)
-    order = order.astype(jnp.int32)
-    rank_all = jnp.where(used, order - 1, -1)
-
-    ids = jnp.concatenate([traj_ids[0], jnp.full((LAG,), -1, jnp.int32)])
-    offset = atom_index * frames
-    ids_now = lax.dynamic_slice_in_dim(ids, offset, frames)
-    ids_later = lax.dynamic_slice_in_dim(ids, offset + LAG, frames)
-    valid = (ids_now == ids_later).astype(F32)[:, None]
-
+    pairs = [atom_pairs] + [rotated(atom_pairs, "feat", s) for s in range(1, lax.axis_size("feat"))]
     cap = min(width, -(-(width * 9 // 16) // 64) * 64)
+    outs, most_used = with_cap(cap, coords, pairs, traj_ids, place)
+
     def again(carry):
-        ranks = rank_all + (carry[0] - 1)
-        return carry[0] - 1, with_cap(width, coords, ranks, used_pairs, valid, place)
-
-    overflow = (jnp.max(order) > cap).astype(jnp.int32)
-    outs = with_cap(cap, coords, rank_all, used_pairs, valid, place)
+        same = [block + (carry[0] - 1) for block in pairs]
+        return carry[0] - 1, with_cap(width, coords, same, traj_ids, place)[0]
+
+    overflow = (most_used > cap).astype(jnp.int32)
     return lax.while_loop(lambda carry: carry[0] > 0, again, (overflow, outs))[1]
 
 

time: 135 us -> 127 us (0.941); the launches traced: 135 us -> 125 us
  waiting for transfers between devices: 81.1 us -> 66.9 us
  Pallas kernels: 25.1 us -> 34 us
  other arithmetic: 6.96 us -> 0.21 us
  starting transfers between devices: 14.9 us -> 18.7 us
    ppermute x13, waiting for transfers between devices: 81.1 us -> 66.9 us  [rotated(): lax.ppermute(block, axis, [(i, (i + shift) % size) for i in range(size)])]
    pallas_call x0 -> x2, Pallas kernels: none -> 10.5 us  [the longest x1 5.81 us: pair_signs(): pl.pallas_call(functools.partial(signs_kernel, groups, width, cap), in_sp...]
    pallas_call x2 -> x1, Pallas kernels: 7.8 us -> 3.46 us  [pick(): pl.pallas_call(functools.partial(pick_kernel, start), in_specs=[pl.BlockS...]
    ppermute x13, starting transfers between devices: 12.9 us -> 16.8 us  [rotated(): lax.ppermute(block, axis, [(i, (i + shift) % size) for i in range(size)])]
    reduce_or x1 -> x0, other arithmetic: 3.33 us -> none  [shards(): used = jnp.any(used_pairs.reshape(-1)[:, None] == atoms[None, :], axis=0)]
    pallas_call x2, Pallas kernels: 3.43 us -> 6.2 us  [distances(): pl.pallas_call(distance_kernel, in_specs=[vmem] * (len(blocks) + 1) + [pl...]
    unnamed x17 -> x18, local copies, waits for them, and re-layouts: 1.99 us -> 3.81 us
    pallas_call x1, Pallas kernels: 6.53 us -> 4.77 us  [late_moments(): pl.pallas_call(functools.partial(late_kernel, size, sides, groups, reps),...]
  transfers between devices with their start and end apart: 14 -> 14, of which waited for: 11 -> 11; matrix products, arithmetic and copies ran while one was open for 3% -> 0% of each run, Pallas kernels for 7% -> 16%
where the time goes in v3:
time: 127 us; the launch traced here: 125 us
  waiting for transfers between devices  66.9 us (53%)
  Pallas kernels  34 us (27%)
  starting transfers between devices  18.7 us (15%)
  local copies, waits for them, and re-layouts  4.12 us (3%)
    ppermute x13, waiting for transfers between devices, rotated(): lax.ppermute(block, axis, [(i, (i + shift) % size) for i in range(size)])  66.9 us
    ppermute x13, starting transfers between devices, rotated(): lax.ppermute(block, axis, [(i, (i + shift) % size) for i in range(size)])  16.8 us
    pallas_call x2, Pallas kernels, distances(): pl.pallas_call(distance_kernel, in_specs=[vmem] * (len(blocks) + 1) + [pl...  6.2 us
    pallas_call x1, Pallas kernels, pair_signs(): pl.pallas_call(functools.partial(signs_kernel, groups, width, cap), in_sp...  5.81 us
    pallas_call x1, Pallas kernels, late_moments(): pl.pallas_call(functools.partial(late_kernel, size, sides, groups, reps),...  4.77 us
    pallas_call x1, Pallas kernels, first_pick(): pl.pallas_call(functools.partial(first_pick_kernel, len(pairs)), in_specs...  4.71 us
    pallas_call x1, Pallas kernels, early_moments(): pl.pallas_call(functools.partial(early_kernel, sizes, sides), in_specs=[p...  4.44 us
    unnamed x18, local copies, waits for them, and re-layouts  3.81 us
  transfers between devices with their start and end apart: 14, of which 11 were waited for; matrix products, arithmetic and copies ran while one was open for 0% of the time, Pallas kernels for 16%

profile of v3, /device:TPU:9, one launch (start us, length us, event | category | flops | bytes accessed | tf_op | source)
XLA Modules:
  0.0 125.2 jit_solution(1838192086154683400)
XLA Ops:
  0.6 1.3 %collective-permute-start.13 = (s32[2,512]{1,0:T(2,128)}, s32[2,512]{1,0:T(2,128)S(1)}, u32[]{:S(2)}, u32[]{:S(2)}) collective-permute-start(s32[2,512]{1,0:T(2,128)} %refs_0_.1), channel_id=1, source_target_pairs={{0,2},{2,0},{1,3},{3,1},{4,6},{6,4},{5,7},{7,5},{8,10},{10,8},{9,1... | collective-permute-start | bytes 12296 | tf_op jit(solution)/shard_map/ppermute | solution.py:28
  1.9 0.1 pad_add_fusion.place_ref
  2.0 1.4 %collective-permute-done.13.refs_1_ = s32[2,512]{1,0:T(2,128)S(1)} collective-permute-done((s32[2,512]{1,0:T(2,128)}, s32[2,512]{1,0:T(2,128)S(1)}, u32[]{:S(2)}, u32[]{:S(2)}) %collective-permute-start.13) | collective-permute-done | bytes 4128 | tf_op jit(solution)/shard_map/ppermute | solution.py:28
  3.4 4.7 %first_pick.6 = (bf16[768,448]{1,0:T(8,128)(2,1)S(1)}, s32[1,2048]{1,0:T(1,128)S(1)}, s32[2,512]{1,0:T(2,128)S(1)}, s32[2,512]{1,0:T(2,128)S(1)}, bf16[3,80,896]...) custom-call(s32[3]{0:T(128)S(1)} %pad_add_fusion.place_ref, ...), custom_call_target="tpu_custom_call" | custom-call | flops 1024 | bytes 1024 | tf_op jit(solution)/shard_map/first_pick/pallas_call | solution.py:94
  8.1 0.0 copy-done.11
  8.1 1.3 %collective-permute-start.14 = (bf16[3,80,896]{2,1,0:T(8,128)(2,1)}, bf16[3,80,896]{2,1,0:T(8,128)(2,1)S(1)}, u32[]{:S(2)}, u32[]{:S(2)}) collective-permute-start(bf16[3,80,896]{2,1,0:T(8,128)(2,1)} %get-tuple-element.302), channel_id=1, source_target_pairs={{0,4},{4,8},{8,12},{12,0},{1,5},{5,9},{9,13},{13,1},{2,6},{6,10},{... | collective-permute-start | bytes 1290248 | tf_op jit(solution)/shard_map/ppermute | solution.py:28
  9.4 1.1 collective-permute-start.18
  10.5 1.4 %collective-permute-start.19 = (bf16[3,80,896]{2,1,0:T(8,128)(2,1)S(1)}, bf16[3,80,896]{2,1,0:T(8,128)(2,1)}, u32[]{:S(2)}, u32[]{:S(2)}) collective-permute-start(bf16[3,80,896]{2,1,0:T(8,128)(2,1)S(1)} %get-tuple-element.313), channel_id=1, source_target_pairs={{0,12},{4,0},{8,4},{12,8},{1,13},{5,1},{9,5},{13,9},{2,14},{6,2},{... | collective-permute-start | bytes 1290248 | tf_op jit(solution)/shard_map/ppermute | solution.py:28
  11.9 6.0 %collective-permute-done.14.after_ref.refs_1_ = bf16[3,80,896]{2,1,0:T(8,128)(2,1)S(1)} collective-permute-done((bf16[3,80,896]{2,1,0:T(8,128)(2,1)}, bf16[3,80,896]{2,1,0:T(8,128)(2,1)S(1)}, u32[]{:S(2)}, u32[]{:S(2)}) %collective-permute-start.14) | collective-permute-done | bytes 430112 | tf_op jit(solution)/shard_map/ppermute | solution.py:28
  17.9 3.5 %pick.6 = (bf16[3,48,896]{2,1,0:T(8,128)(2,1)S(1)}, bf16[3,48,896]{2,1,0:T(8,128)(2,1)S(1)}, bf16[3,48,896]{2,1,0:T(8,128)(2,1)S(1)}, bf16[3,48,896]{2,1,0:T(8,128)(2,1)S(1)}) custom-call(s32[3]{0:T(128)S(1)} %pad_add_fusion.place_ref, bf16[3,2048,768]{2,1,0:T(8,128)(2,1)} %bitcast.32, bf16[768,448]{1,0:T(8,128)(2,1)S(1)} %get-tuple-element.301.chosen_ref, ...), custom_call_target="tpu_custom_call" | custom-call | flops 1024 | bytes 1024 | tf_op jit(solution)/shard_map/pick/pallas_call | solution.py:131
  21.4 1.5 %collective-permute-start.15 = (bf16[3,48,896]{2,1,0:T(8,128)(2,1)S(1)}, bf16[3,48,896]{2,1,0:T(8,128)(2,1)S(1)}, u32[]{:S(2)}, u32[]{:S(2)}) collective-permute-start(bf16[3,48,896]{2,1,0:T(8,128)(2,1)S(1)} %get-tuple-element.307), channel_id=1, source_target_pairs={{0,4},{4,8},{8,12},{12,0},{1,5},{5,9},{9,13},{13,1},{2,6},{6,10},{... | collective-permute-start | bytes 774152 | tf_op jit(solution)/shard_map/ppermute | solution.py:28
  22.9 3.1 %collective-permute-start.16 = (bf16[3,48,896]{2,1,0:T(8,128)(2,1)S(1)}, bf16[3,48,896]{2,1,0:T(8,128)(2,1)S(1)}, u32[]{:S(2)}, u32[]{:S(2)}) collective-permute-start(bf16[3,48,896]{2,1,0:T(8,128)(2,1)S(1)} %get-tuple-element.308), channel_id=1, source_target_pairs={{0,8},{4,12},{8,0},{12,4},{1,9},{5,13},{9,1},{13,5},{2,10},{6,14},... | collective-permute-start | bytes 774152 | tf_op jit(solution)/shard_map/ppermute | solution.py:28
  26.0 5.8 %pair_signs.6 = (bf16[1792,1024]{1,0:T(8,128)(2,1)S(1)}, f32[1,128]{1,0:T(1,128)S(1)}) custom-call(s32[3]{0:T(128)S(1)} %pad_add_fusion.place_ref, bf16[3,48,896]{2,1,0:T(8,128)(2,1)S(1)} %get-tuple-element.303.after_ref.refs_5_.refs_0_, s32[2,512]{1,0:T(2,128)S(1)} %get-tuple-element.304.refs_0_, s32[2,512]{1,0:T(2,128)S(1)} %get-tuple-element.305.refs_1_), custom_call_target="tpu_custom_call" | custom-call | flops 1024 | bytes 1024 | tf_op jit(solution)/shard_map/pair_signs/pallas_call | solution.py:629
  31.8 1.8 %copy-done.2 = bf16[1792,1024]{1,0:T(8,128)(2,1)} copy-done((bf16[1792,1024]{1,0:T(8,128)(2,1)}, bf16[1792,1024]{1,0:T(8,128)(2,1)S(1)}, u32[]{:S(2)}) %copy-start.2) | copy-done | bytes 3670040
  33.6 0.0 collective-permute-start.17
  33.6 19.4 %collective-permute-done.18.refs_2_ = bf16[3,80,896]{2,1,0:T(8,128)(2,1)S(1)} collective-permute-done((bf16[3,80,896]{2,1,0:T(8,128)(2,1)S(1)}, bf16[3,80,896]{2,1,0:T(8,128)(2,1)S(1)}, u32[]{:S(2)}, u32[]{:S(2)}) %collective-permute-start.18) | collective-permute-done | bytes 430112 | tf_op jit(solution)/shard_map/ppermute | solution.py:28
  53.0 6.9 %collective-permute-done.19.refs_3_ = bf16[3,80,896]{2,1,0:T(8,128)(2,1)} collective-permute-done((bf16[3,80,896]{2,1,0:T(8,128)(2,1)S(1)}, bf16[3,80,896]{2,1,0:T(8,128)(2,1)}, u32[]{:S(2)}, u32[]{:S(2)}) %collective-permute-start.19) | collective-permute-done | bytes 430112 | tf_op jit(solution)/shard_map/ppermute | solution.py:28
  59.9 4.6 %distances.12 = (f32[160,1024]{1,0:T(8,128)S(1)}, s16[176,1024]{1,0:T(8,128)(2,1)S(1)}) custom-call(bf16[3,80,896]{2,1,0:T(8,128)(2,1)S(1)} %get-tuple-element.311.refs_0_, bf16[3,80,896]{2,1,0:T(8,128)(2,1)S(1)} %collective-permute-done.14.after_ref.refs_1_, bf16[3,80,896]{2,1,0:T(8,128)(2,1)S(1)} %collective-permute-done.18.refs_2_, ...), custom_call_target="tpu_custom_call" | custom-call | flops 99999997952 | bytes 1024 | tf_op jit(solution)/shard_map/distances/pallas_call | solution.py:197
  64.6 1.3 %collective-permute-start.21 = (s16[176,1024]{1,0:T(8,128)(2,1)S(1)}, s16[176,1024]{1,0:T(8,128)(2,1)S(1)}, u32[]{:S(2)}, u32[]{:S(2)}) collective-permute-start(s16[176,1024]{1,0:T(8,128)(2,1)S(1)} %get-tuple-element.317), channel_id=1, source_target_pairs={{0,2},{2,0},{1,3},{3,1},{4,6},{6,4},{5,7},{7,5},{8,10},{10,8},{9,1... | collective-permute-start | bytes 1081352 | tf_op jit(solution)/shard_map/ppermute | solution.py:28
  65.9 0.0 collective-permute-done.15.refs_1_
  65.9 0.9 collective-permute-done.16.refs_2_
  66.8 4.1 %collective-permute-done.17.refs_3_ = bf16[3,48,896]{2,1,0:T(8,128)(2,1)S(1)} collective-permute-done((bf16[3,48,896]{2,1,0:T(8,128)(2,1)S(1)}, bf16[3,48,896]{2,1,0:T(8,128)(2,1)S(1)}, u32[]{:S(2)}, u32[]{:S(2)}) %collective-permute-start.17) | collective-permute-done | bytes 258080 | tf_op jit(solution)/shard_map/ppermute | solution.py:28
  70.9 1.6 %distances.13 = (f32[96,1024]{1,0:T(8,128)S(1)}, s16[112,1024]{1,0:T(8,128)(2,1)S(1)}) custom-call(bf16[3,48,896]{2,1,0:T(8,128)(2,1)S(1)} %get-tuple-element.303.after_ref.refs_5_.refs_0_, bf16[3,48,896]{2,1,0:T(8,128)(2,1)S(1)} %collective-permute-done.15.refs_1_, bf16[3,48,896]{2,1,0:T(8,128)(2,1)S(1)} %collective-permute-done.16.refs_2_, ...), custom_call_target="tpu_custom_call" | custom-call | flops 99999997952 | bytes 1024 | tf_op jit(solution)/shard_map/distances/pallas_call | solution.py:197
  72.5 1.3 %collective-permute-start.20 = (s16[112,1024]{1,0:T(8,128)(2,1)S(1)}, s16[112,1024]{1,0:T(8,128)(2,1)S(1)}, u32[]{:S(2)}, u32[]{:S(2)}) collective-permute-start(s16[112,1024]{1,0:T(8,128)(2,1)S(1)} %get-tuple-element.316), channel_id=1, source_target_pairs={{0,2},{2,0},{1,3},{3,1},{4,6},{6,4},{5,7},{7,5},{8,10},{10,8},{9,1... | collective-permute-start | bytes 688136 | tf_op jit(solution)/shard_map/ppermute | solution.py:28
  73.8 0.3 collective-permute-done.21.refs_1_
  74.1 0.1 dynamic-slice.3
  74.2 0.1 dynamic-slice.2
  74.3 1.9 %collective-permute-start.22 = (f32[16,512]{1,0:T(8,128)S(1)}, f32[16,512]{1,0:T(8,128)S(1)}, u32[]{:S(2)}, u32[]{:S(2)}) collective-permute-start(f32[16,512]{1,0:T(8,128)S(1)} %dynamic-slice_select_fusion.1), channel_id=1, source_target_pairs={{4,0},{8,4},{12,8},{5,1},{9,5},{13,9},{6,2},{10,6},{14,10},{7,3},{... | collective-permute-start | bytes 98312 | tf_op jit(solution)/shard_map/ppermute | solution.py:32
  76.2 0.1 fusion.9
  76.3 0.2 copy.8.refs_2_.refs_7_
  76.4 4.4 %early_moments.6 = (f32[1024,1024]{1,0:T(8,128)S(1)}, f32[320,512]{1,0:T(8,128)S(1)}, f32[1,1024]{1,0:T(1,128)S(1)}, f32[4,1024]{1,0:T(4,128)S(1)}, f32[16,1024]{1,0:T(8,128)S(1)}) custom-call(s32[3]{0:T(128)S(1)} %copy-done.5, f32[160,1024]{1,0:T(8,128)S(1)} %get-tuple-element.314.refs_5_.refs_0_, s16[176,1024]{1,0:T(8,128)(2,1)S(1)} %collective-permute-done.21.refs_1_, ...), custom_call_target="tpu_custom_call" | custom-call | flops 1024 | bytes 1024 | tf_op jit(solution)/shard_map/early_moments/pallas_call | solution.py:281
  80.9 2.0 %copy-done.1 = f32[1024,1024]{1,0:T(8,128)} copy-done((f32[1024,1024]{1,0:T(8,128)}, f32[1024,1024]{1,0:T(8,128)S(1)}, u32[]{:S(2)}) %copy-start.1) | copy-done | bytes 4194328
  82.9 0.0 collective-permute-done.22.refs_6_
  82.9 0.0 collective-permute-done.20.refs_1_
  82.9 4.8 %late_moments.6 = (f32[520,1024]{1,0:T(8,128)S(1)}, f32[520,1024]{1,0:T(8,128)S(1)}, f32[192,512]{1,0:T(8,128)S(1)}) custom-call(s32[3]{0:T(128)S(1)} %copy-done.5, f32[96,1024]{1,0:T(8,128)S(1)} %get-tuple-element.315.refs_0_, s16[112,1024]{1,0:T(8,128)(2,1)S(1)} %collective-permute-done.20.refs_1_, f32[1024,1024]{1,0:T(8,128)} %copy-done.1, ...), custom_call_target="tpu_custom_call" | custom-call | flops 1024 | bytes 1024 | tf_op jit(solution)/shard_map/late_moments/pallas_call | solution.py:380
  87.7 1.5 %collective-permute-start.23 = (f32[520,1024]{1,0:T(8,128)S(1)}, f32[520,1024]{1,0:T(8,128)S(1)}, u32[]{:S(2)}, u32[]{:S(2)}) collective-permute-start(f32[520,1024]{1,0:T(8,128)S(1)} %get-tuple-element.324), channel_id=1, source_target_pairs={{0,1},{1,0},{2,3},{3,2},{4,5},{5,4},{6,7},{7,6},{8,9},{9,8},{10,11... | collective-permute-start | bytes 6389768 | tf_op jit(solution)/shard_map/ppermute | solution.py:28
  89.2 3.8 %collective-permute-done.23.refs_1_ = f32[520,1024]{1,0:T(8,128)S(1)} collective-permute-done((f32[520,1024]{1,0:T(8,128)S(1)}, f32[520,1024]{1,0:T(8,128)S(1)}, u32[]{:S(2)}, u32[]{:S(2)}) %collective-permute-start.23) | collective-permute-done | bytes 2129952 | tf_op jit(solution)/shard_map/ppermute | solution.py:28
  93.0 1.8 %share.6 = (f32[128,1024]{1,0:T(8,128)S(1)}, s16[144,1024]{1,0:T(8,128)(2,1)S(1)}, s16[144,1024]{1,0:T(8,128)(2,1)S(1)}, s16[144,1024]{1,0:T(8,128)(2,1)S(1)}, s16[16,1024]{1,0:T(8,128)(2,1)S(1)}) custom-call(s32[3]{0:T(128)S(1)} %copy-done.5, f32[520,1024]{1,0:T(8,128)S(1)} %get-tuple-element.323.refs_0_, f32[520,1024]{1,0:T(8,128)S(1)} %collective-permute-done.23.refs_1_), custom_call_target="tpu_custom_call" | custom-call | flops 1024 | bytes 1024 | tf_op jit(solution)/shard_map/share/pallas_call | solution.py:469
  94.8 0.0 copy-start.7
  94.8 0.0 copy-start.9
  94.9 1.8 %collective-permute-start.24 = (s16[144,1024]{1,0:T(8,128)(2,1)S(1)}, s16[144,1024]{1,0:T(8,128)(2,1)S(1)}, u32[]{:S(2)}, u32[]{:S(2)}) collective-permute-start(s16[144,1024]{1,0:T(8,128)(2,1)S(1)} %get-tuple-element.327), channel_id=1, source_target_pairs={{0,4},{4,8},{8,12},{12,0},{1,5},{5,9},{9,13},{13,1},{2,6},{6,10},{... | collective-permute-start | bytes 884744 | tf_op jit(solution)/shard_map/ppermute | solution.py:28
  96.6 0.0 collective-permute-start.25
  96.6 1.3 %collective-permute-start.26 = (s16[144,1024]{1,0:T(8,128)(2,1)S(1)}, s16[144,1024]{1,0:T(8,128)(2,1)S(1)}, u32[]{:S(2)}, u32[]{:S(2)}) collective-permute-start(s16[144,1024]{1,0:T(8,128)(2,1)S(1)} %get-tuple-element.329), channel_id=1, source_target_pairs={{0,12},{4,0},{8,4},{12,8},{1,13},{5,1},{9,5},{13,9},{2,14},{6,2},{... | collective-permute-start | bytes 884744 | tf_op jit(solution)/shard_map/ppermute | solution.py:28
  97.9 5.2 %collective-permute-done.24.refs_0_ = s16[144,1024]{1,0:T(8,128)(2,1)S(1)} collective-permute-done((s16[144,1024]{1,0:T(8,128)(2,1)S(1)}, s16[144,1024]{1,0:T(8,128)(2,1)S(1)}, u32[]{:S(2)}, u32[]{:S(2)}) %collective-permute-start.24) | collective-permute-done | bytes 294944 | tf_op jit(solution)/shard_map/ppermute | solution.py:28
  103.1 18.5 %collective-permute-done.25.refs_1_ = s16[144,1024]{1,0:T(8,128)(2,1)S(1)} collective-permute-done((s16[144,1024]{1,0:T(8,128)(2,1)S(1)}, s16[144,1024]{1,0:T(8,128)(2,1)S(1)}, u32[]{:S(2)}, u32[]{:S(2)}) %collective-permute-start.25) | collective-permute-done | bytes 294944 | tf_op jit(solution)/shard_map/ppermute | solution.py:28
  121.6 0.4 collective-permute-done.26.refs_2_
  122.0 2.8 %finish.6 = (f32[128,512]{1,0:T(8,128)}, f32[128,512]{1,0:T(8,128)}, f32[512,512]{1,0:T(8,128)}) custom-call(s32[3]{0:T(128)S(1)} %copy-done.5, f32[128,1024]{1,0:T(8,128)S(1)} %get-tuple-element.325.kept_ref, s16[16,1024]{1,0:T(8,128)(2,1)S(1)} %get-tuple-element.326.codes_ref, s16[144,1024]{1,0:T(8,128)(2,1)S(1)} %collective-permute-done.24.refs_0_, ...), custom_call_target="tpu_custom_call" | custom-call | flops 1024 | bytes 1024 | tf_op jit(solution)/shard_map/finish/pallas_call | solution.py:564
  124.8 0.2 while.17
  (17 shorter events, 0.1 us)
Async XLA Ops:
  0.6 2.7 %collective-permute-start.13 = (s32[2,512]{1,0:T(2,128)}, s32[2,512]{1,0:T(2,128)S(1)}, u32[]{:S(2)}, u32[]{:S(2)}) collective-permute-start(s32[2,512]{1,0:T(2,128)} %refs_0_.1), channel_id=1, source_target_pairs={{0,2},{2,0},{1,3},{3,1},{4,6},{6,4},{5,7},{7,5},{8,10},{10,8},{9,1... | collective-permute-start | bytes 12296 | tf_op jit(solution)/shard_map/ppermute | solution.py:28
  2.0 24.0 %copy-start.4 = (s32[3]{0:T(128)}, s32[3]{0:T(128)S(1)}, u32[]{:S(2)}) copy-start(s32[3]{0:T(128)S(1)} %pad_add_fusion.place_ref) | copy-start | bytes 40
  3.4 4.7 %copy-start.11 = (s32[2,512]{1,0:T(2,128)}, s32[2,512]{1,0:T(2,128)S(1)}, u32[]{:S(2)}) copy-start(s32[2,512]{1,0:T(2,128)S(1)} %collective-permute-done.13.refs_1_) | copy-start | bytes 12292
  8.1 9.8 %collective-permute-start.14 = (bf16[3,80,896]{2,1,0:T(8,128)(2,1)}, bf16[3,80,896]{2,1,0:T(8,128)(2,1)S(1)}, u32[]{:S(2)}, u32[]{:S(2)}) collective-permute-start(bf16[3,80,896]{2,1,0:T(8,128)(2,1)} %get-tuple-element.302), channel_id=1, source_target_pairs={{0,4},{4,8},{8,12},{12,0},{1,5},{5,9},{9,13},{13,1},{2,6},{6,10},{... | collective-permute-start | bytes 1290248 | tf_op jit(solution)/shard_map/ppermute | solution.py:28
  9.4 43.6 %collective-permute-start.18 = (bf16[3,80,896]{2,1,0:T(8,128)(2,1)S(1)}, bf16[3,80,896]{2,1,0:T(8,128)(2,1)S(1)}, u32[]{:S(2)}, u32[]{:S(2)}) collective-permute-start(bf16[3,80,896]{2,1,0:T(8,128)(2,1)S(1)} %get-tuple-element.312), channel_id=1, source_target_pairs={{0,8},{4,12},{8,0},{12,4},{1,9},{5,13},{9,1},{13,5},{2,10},{6,14},... | collective-permute-start | bytes 1290248 | tf_op jit(solution)/shard_map/ppermute | solution.py:28
  10.5 49.4 %collective-permute-start.19 = (bf16[3,80,896]{2,1,0:T(8,128)(2,1)S(1)}, bf16[3,80,896]{2,1,0:T(8,128)(2,1)}, u32[]{:S(2)}, u32[]{:S(2)}) collective-permute-start(bf16[3,80,896]{2,1,0:T(8,128)(2,1)S(1)} %get-tuple-element.313), channel_id=1, source_target_pairs={{0,12},{4,0},{8,4},{12,8},{1,13},{5,1},{9,5},{13,9},{2,14},{6,2},{... | collective-permute-start | bytes 1290248 | tf_op jit(solution)/shard_map/ppermute | solution.py:28
  21.4 44.5 %collective-permute-start.15 = (bf16[3,48,896]{2,1,0:T(8,128)(2,1)S(1)}, bf16[3,48,896]{2,1,0:T(8,128)(2,1)S(1)}, u32[]{:S(2)}, u32[]{:S(2)}) collective-permute-start(bf16[3,48,896]{2,1,0:T(8,128)(2,1)S(1)} %get-tuple-element.307), channel_id=1, source_target_pairs={{0,4},{4,8},{8,12},{12,0},{1,5},{5,9},{9,13},{13,1},{2,6},{6,10},{... | collective-permute-start | bytes 774152 | tf_op jit(solution)/shard_map/ppermute | solution.py:28
  22.9 44.0 %collective-permute-start.16 = (bf16[3,48,896]{2,1,0:T(8,128)(2,1)S(1)}, bf16[3,48,896]{2,1,0:T(8,128)(2,1)S(1)}, u32[]{:S(2)}, u32[]{:S(2)}) collective-permute-start(bf16[3,48,896]{2,1,0:T(8,128)(2,1)S(1)} %get-tuple-element.308), channel_id=1, source_target_pairs={{0,8},{4,12},{8,0},{12,4},{1,9},{5,13},{9,1},{13,5},{2,10},{6,14},... | collective-permute-start | bytes 774152 | tf_op jit(solution)/shard_map/ppermute | solution.py:28
  31.8 1.8 %copy-start.2 = (bf16[1792,1024]{1,0:T(8,128)(2,1)}, bf16[1792,1024]{1,0:T(8,128)(2,1)S(1)}, u32[]{:S(2)}) copy-start(bf16[1792,1024]{1,0:T(8,128)(2,1)S(1)} %get-tuple-element.310.refs_4_) | copy-start | bytes 11010052
  33.6 37.3 %collective-permute-start.17 = (bf16[3,48,896]{2,1,0:T(8,128)(2,1)S(1)}, bf16[3,48,896]{2,1,0:T(8,128)(2,1)S(1)}, u32[]{:S(2)}, u32[]{:S(2)}) collective-permute-start(bf16[3,48,896]{2,1,0:T(8,128)(2,1)S(1)} %get-tuple-element.309), channel_id=1, source_target_pairs={{0,12},{4,0},{8,4},{12,8},{1,13},{5,1},{9,5},{13,9},{2,14},{6,2},{... | collective-permute-start | bytes 774152 | tf_op jit(solution)/shard_map/ppermute | solution.py:28
  59.9 11.0 %copy-start.3 = (bf16[1792,1024]{1,0:T(8,128)(2,1)S(1)}, bf16[1792,1024]{1,0:T(8,128)(2,1)}, u32[]{:S(2)}) copy-start(bf16[1792,1024]{1,0:T(8,128)(2,1)} %copy-done.2) | copy-start | bytes 11010052
  64.6 9.4 %collective-permute-start.21 = (s16[176,1024]{1,0:T(8,128)(2,1)S(1)}, s16[176,1024]{1,0:T(8,128)(2,1)S(1)}, u32[]{:S(2)}, u32[]{:S(2)}) collective-permute-start(s16[176,1024]{1,0:T(8,128)(2,1)S(1)} %get-tuple-element.317), channel_id=1, source_target_pairs={{0,2},{2,0},{1,3},{3,1},{4,6},{6,4},{5,7},{7,5},{8,10},{10,8},{9,1... | collective-permute-start | bytes 1081352 | tf_op jit(solution)/shard_map/ppermute | solution.py:28
  65.9 10.5 %copy-start.5 = (s32[3]{0:T(128)S(1)}, s32[3]{0:T(128)}, u32[]{:S(2)}) copy-start(s32[3]{0:T(128)} %copy-done.4) | copy-start | bytes 40
  72.5 10.4 %collective-permute-start.20 = (s16[112,1024]{1,0:T(8,128)(2,1)S(1)}, s16[112,1024]{1,0:T(8,128)(2,1)S(1)}, u32[]{:S(2)}, u32[]{:S(2)}) collective-permute-start(s16[112,1024]{1,0:T(8,128)(2,1)S(1)} %get-tuple-element.316), channel_id=1, source_target_pairs={{0,2},{2,0},{1,3},{3,1},{4,6},{6,4},{5,7},{7,5},{8,10},{10,8},{9,1... | collective-permute-start | bytes 688136 | tf_op jit(solution)/shard_map/ppermute | solution.py:28
  74.3 8.6 %collective-permute-start.22 = (f32[16,512]{1,0:T(8,128)S(1)}, f32[16,512]{1,0:T(8,128)S(1)}, u32[]{:S(2)}, u32[]{:S(2)}) collective-permute-start(f32[16,512]{1,0:T(8,128)S(1)} %dynamic-slice_select_fusion.1), channel_id=1, source_target_pairs={{4,0},{8,4},{12,8},{5,1},{9,5},{13,9},{6,2},{10,6},{14,10},{7,3},{... | collective-permute-start | bytes 98312 | tf_op jit(solution)/shard_map/ppermute | solution.py:32
  80.9 2.0 %copy-start.1 = (f32[1024,1024]{1,0:T(8,128)}, f32[1024,1024]{1,0:T(8,128)S(1)}, u32[]{:S(2)}) copy-start(f32[1024,1024]{1,0:T(8,128)S(1)} %get-tuple-element.319.refs_2_) | copy-start | bytes 12582916
  87.7 5.4 %collective-permute-start.23 = (f32[520,1024]{1,0:T(8,128)S(1)}, f32[520,1024]{1,0:T(8,128)S(1)}, u32[]{:S(2)}, u32[]{:S(2)}) collective-permute-start(f32[520,1024]{1,0:T(8,128)S(1)} %get-tuple-element.324), channel_id=1, source_target_pairs={{0,1},{1,0},{2,3},{3,2},{4,5},{5,4},{6,7},{7,6},{8,9},{9,8},{10,11... | collective-permute-start | bytes 6389768 | tf_op jit(solution)/shard_map/ppermute | solution.py:28
  94.8 30.0 %copy-start.7 = (s32[1,2048]{1,0:T(1,128)S(1)}, s32[1,2048]{1,0:T(1,128)}, u32[]{:S(2)}) copy-start(s32[1,2048]{1,0:T(1,128)} %ids_ref.1) | copy-start | bytes 24580
  94.8 30.0 %copy-start.9 = (s32[2,512]{1,0:T(2,128)S(1)}, s32[2,512]{1,0:T(2,128)}, u32[]{:S(2)}) copy-start(s32[2,512]{1,0:T(2,128)} %refs_0_.1) | copy-start | bytes 12292
  94.8 30.0 %copy-start.12 = (s32[2,512]{1,0:T(2,128)S(1)}, s32[2,512]{1,0:T(2,128)}, u32[]{:S(2)}) copy-start(s32[2,512]{1,0:T(2,128)} %copy-done.11) | copy-start | bytes 12292
  94.9 8.3 %collective-permute-start.24 = (s16[144,1024]{1,0:T(8,128)(2,1)S(1)}, s16[144,1024]{1,0:T(8,128)(2,1)S(1)}, u32[]{:S(2)}, u32[]{:S(2)}) collective-permute-start(s16[144,1024]{1,0:T(8,128)(2,1)S(1)} %get-tuple-element.327), channel_id=1, source_target_pairs={{0,4},{4,8},{8,12},{12,0},{1,5},{5,9},{9,13},{13,1},{2,6},{6,10},{... | collective-permute-start | bytes 884744 | tf_op jit(solution)/shard_map/ppermute | solution.py:28
  96.6 25.0 %collective-permute-start.25 = (s16[144,1024]{1,0:T(8,128)(2,1)S(1)}, s16[144,1024]{1,0:T(8,128)(2,1)S(1)}, u32[]{:S(2)}, u32[]{:S(2)}) collective-permute-start(s16[144,1024]{1,0:T(8,128)(2,1)S(1)} %get-tuple-element.328), channel_id=1, source_target_pairs={{0,8},{4,12},{8,0},{12,4},{1,9},{5,13},{9,1},{13,5},{2,10},{6,14},... | collective-permute-start | bytes 884744 | tf_op jit(solution)/shard_map/ppermute | solution.py:28
  96.6 25.3 %collective-permute-start.26 = (s16[144,1024]{1,0:T(8,128)(2,1)S(1)}, s16[144,1024]{1,0:T(8,128)(2,1)S(1)}, u32[]{:S(2)}, u32[]{:S(2)}) collective-permute-start(s16[144,1024]{1,0:T(8,128)(2,1)S(1)} %get-tuple-element.329), channel_id=1, source_target_pairs={{0,12},{4,0},{8,4},{12,8},{1,13},{5,1},{9,5},{13,9},{2,14},{6,2},{... | collective-permute-start | bytes 884744 | tf_op jit(solution)/shard_map/ppermute | solution.py:28

commit v4 on v3

--- a/solution.py
+++ b/solution.py
@@ -16,7 +16,7 @@
 ROOT_STEP = 0.02
 TINY = 1e-30
 REACH = 1e-6
-VMEM_LIMIT = 48 * 1024 * 1024
+VMEM_LIMIT = 32 * 1024 * 1024
 F32 = jnp.float32
 BF16 = jnp.bfloat16
 LARGE = pl.CostEstimate(flops=10**11, bytes_accessed=1024, transcendentals=0)
@@ -43,7 +43,7 @@
     for j, size in enumerate(sizes):
         for s in range(groups):
             there = lax.rem(place_ref[0] + s, groups)
-            row = there * frames + start + place_ref[1] * size
+            row = there * frames + place_ref[1] * (frames // sides) + start
             copies.append(
                 pltpu.make_async_copy(
                     coords_ref.at[:, pl.ds(pl.multiple_of(row, HALO), size), :],
@@ -51,21 +51,26 @@
                     sems.at[j, s],
                 )
             )
-        start += sides * size
+        start += size
     for copy in copies:
         copy.start()
     return copies
 
 
+def packed(cap):
+    return -(-3 * cap // 128) * 128
+
+
 def pick_rows(rows, chosen, out):
     _, size, width = rows.shape
-    cap, half = chosen.shape[1], size // 2
+    cap = chosen.shape[1]
     picked = jnp.dot(
         rows[...].reshape(3 * size, width), chosen, preferred_element_type=F32
     ).astype(BF16)
-    picked = picked.reshape(3, size, cap)
-    out[:, :, 0:cap] = picked[:, :half, :]
-    out[:, :, cap : 2 * cap] = picked[:, half:, :]
+    for k in range(3):
+        out[:, k * cap : (k + 1) * cap] = picked[k * size : (k + 1) * size, :]
+    if out.shape[1] > 3 * cap:
+        out[:, 3 * cap :] = jnp.zeros((size, out.shape[1] - 3 * cap), BF16)
 
 
 def first_pick_kernel(sides, place_ref, coords_ref, ids_ref, *refs):
@@ -104,7 +109,7 @@
             jax.ShapeDtypeStruct(ids.shape, ids.dtype),
         ]
         + [jax.ShapeDtypeStruct(block.shape, block.dtype) for block in pairs]
-        + [jax.ShapeDtypeStruct((3, size // 2, 2 * cap), BF16)] * groups,
+        + [jax.ShapeDtypeStruct((size, packed(cap)), BF16)] * groups,
         scratch_shapes=[
             pltpu.VMEM((groups, 3, size, width), BF16),
             pltpu.SemaphoreType.DMA((1, groups)),
@@ -137,7 +142,7 @@
             pl.BlockSpec(memory_space=pl.ANY),
         ],
         out_specs=[vmem] * groups,
-        out_shape=[jax.ShapeDtypeStruct((3, size // 2, 2 * cap), BF16)] * groups,
+        out_shape=[jax.ShapeDtypeStruct((size, packed(cap)), BF16)] * groups,
         scratch_shapes=[
             pltpu.VMEM((groups, 3, size, width), BF16),
             pltpu.SemaphoreType.DMA((1, groups)),
@@ -168,13 +173,13 @@
 
 def distance_kernel(*refs):
     blocks, (signs_ref, after_ref, out, codes_out, joined) = refs[:-5], refs[-5:]
-    half, cap = blocks[0].shape[1], blocks[0].shape[2] // 2
-    size = 2 * half
+    size = blocks[0].shape[0]
+    cap = signs_ref.shape[0] // len(blocks)
     for s, block in enumerate(blocks):
-        columns = slice(s * cap, (s + 1) * cap)
         for k in range(3):
-            joined[k * size : k * size + half, columns] = block[k, :, 0:cap]
-            joined[k * size + half : (k + 1) * size, columns] = block[k, :, cap : 2 * cap]
+            joined[k * size : (k + 1) * size, s * cap : (s + 1) * cap] = block[
+                :, k * cap : (k + 1) * cap
+            ]
     delta = jnp.dot(joined[...], signs_ref[...], preferred_element_type=F32)
     square = delta * delta
     total = square[:size] + square[size : 2 * size] + square[2 * size :]
@@ -192,7 +197,7 @@
 
 
 def distances(blocks, signs, after):
-    size = 2 * blocks[0].shape[1]
+    size = blocks[0].shape[0]
     vmem = pl.BlockSpec(memory_space=pltpu.VMEM)
     return pl.pallas_call(
         distance_kernel,
@@ -223,63 +228,58 @@
     return total + jnp.dot(left_low, right_high, preferred_element_type=F32)
 
 
-def place_pieces(sizes, side, sides, pieces, every, first):
-    row = first
-    for j, size in enumerate(sizes):
-        for s in range(sides):
-            there = lax.rem(side + sides - s, sides)
-            at = pl.multiple_of(row + there * size, HALO)
-            piece = pieces[j * sides + s]
-            every[pl.ds(at, size), :] = piece[...] if s == 0 else decoded_piece(piece, size)
-        row += sides * size
-
-
-def own_columns(side, sides, whole, own):
-    cols = own.shape[1]
+def row_sum(value):
+    return jnp.sum(value, 0, keepdims=True)
+
+
+def side_columns(side, sides, cols, write):
     for s in range(sides):
 
         @pl.when(side == s)
         def _():
-            own[...] = whole[:, s * cols : (s + 1) * cols]
-
-
-def row_sum(value):
-    return jnp.sum(value, 0, keepdims=True)
-
-
-def early_kernel(sizes, sides, place_ref, *refs):
-    pieces = refs[: len(sizes) * sides]
-    valid_ref, out, own_out, shift_out, sums_out, tail_out, every, own = refs[len(pieces) :]
+            write(slice(s * cols, (s + 1) * cols))
+
+
+def early_kernel(chunks, sides, place_ref, *refs):
+    pieces = refs[:chunks]
+    valid_ref, out, own_out, shift_out, sums_out, tail_out, every = refs[chunks:]
     frames = every.shape[0]
-    cols = own.shape[1]
+    cols = own_out.shape[1]
+    row = 0
+    for piece in pieces:
+        every[row : row + piece.shape[0], :] = piece[...]
+        row += piece.shape[0]
     side = place_ref[1]
-    place_pieces(sizes, side, sides, pieces, every, 0)
-    valid = valid_ref[0:frames, :]
+    valid = valid_ref[pl.ds(pl.multiple_of(side * frames, HALO), frames), :]
     count = jnp.maximum(jnp.sum(valid), 1.0)
     shift = row_sum(valid * every[...]) / count
     shift_out[...] = shift
     every[...] = every[...] - shift
     tail_out[...] = every[frames - HALO : frames, :]
-    own_columns(side, sides, every, own)
-    own_out[...] = own[...]
+
+    def keep_own(part):
+        own_out[...] = every[:, part]
+
+    side_columns(side, sides, cols, keep_own)
     now = every[...]
+    own = own_out[...]
     weighed = valid * now
-    weighed_later = valid[: frames - LAG] * own[LAG:frames, :]
+    later = own[LAG:frames, :]
+    weighed_later = valid[: frames - LAG] * later
     sums_out[0:1, :] = row_sum(weighed)
     sums_out[1:2, :] = row_sum(weighed * now)
     sums_out[2:3, 0:cols] = row_sum(weighed_later)
-    sums_out[3:4, 0:cols] = row_sum(weighed_later * own[LAG:frames, :])
+    sums_out[3:4, 0:cols] = row_sum(weighed_later * later)
     weighed_later = jnp.concatenate([weighed_later, jnp.zeros((LAG, cols), F32)], 0)
-    out[:, 0:cols] = product(now, valid * own[...])
-    out[:, cols : 2 * cols] = product(now, weighed_later)
-
-
-def early_moments(pieces, valid, place, sizes, sides):
-    frames, feats = sides * sum(sizes), pieces[0].shape[1]
+    out[...] = product(now, jnp.concatenate([valid * own, weighed_later], 1))
+
+
+def early_moments(pieces, valid, place, sides):
+    frames, feats = sum(piece.shape[0] for piece in pieces), pieces[0].shape[1]
     cols = feats // sides
     vmem = pl.BlockSpec(memory_space=pltpu.VMEM)
     return pl.pallas_call(
-        functools.partial(early_kernel, sizes, sides),
+        functools.partial(early_kernel, len(pieces), sides),
         in_specs=[pl.BlockSpec(memory_space=pltpu.SMEM)] + [vmem] * (len(pieces) + 1),
         out_specs=[vmem] * 5,
         out_shape=[
@@ -289,46 +289,85 @@
             jax.ShapeDtypeStruct((4, feats), F32),
             jax.ShapeDtypeStruct((HALO, feats), F32),
         ],
-        scratch_shapes=[pltpu.VMEM((frames, feats), F32), pltpu.VMEM((frames, cols), F32)],
+        scratch_shapes=[pltpu.VMEM((frames, feats), F32)],
         compiler_params=params(),
         cost_estimate=SMALL,
         name="early_moments",
     )(place, *pieces, valid)
 
 
-def late_kernel(size, sides, groups, reps, place_ref, *refs):
-    pieces = refs[:sides]
-    before_ref, shift_ref, sums_ref, tail_ref, halo_ref, valid_ref = refs[sides : sides + 6]
-    outs = refs[sides + 6 : sides + 6 + reps]
-    own_out, every, own, right, left_high, left_low = refs[sides + 6 + reps :]
-    frames, cols = sides * size, own_out.shape[1]
-    feats = every.shape[1]
-    rows = feats // (groups * reps)
+def add_blocks(place_ref, shifts, groups, before_ref, left_refs, right_refs, outs):
+    reps = len(outs)
+    rows = before_ref.shape[0] // (groups * reps)
+    left_high, left_low = left_refs
+    right_high, right_low = right_refs[0][...], right_refs[1][...]
+    for r in reversed(range(reps)):
+        rep = lax.rem(place_ref[2] + r, reps)
+        for i, s in enumerate(shifts):
+            there = lax.rem(place_ref[0] + s, groups)
+            at = pl.ds(pl.multiple_of((there * reps + rep) * rows, rows), rows)
+            part = before_ref[at, :]
+            part += jnp.dot(left_high[at, :], right_high, preferred_element_type=F32)
+            part += jnp.dot(left_high[at, :], right_low, preferred_element_type=F32)
+            part += jnp.dot(left_low[at, :], right_high, preferred_element_type=F32)
+            outs[r][i * rows : (i + 1) * rows, :] = part
+
+
+def late_kernel(sizes, sides, groups, reps, shifts, place_ref, *refs):
+    chunks = len(sizes)
+    codes = refs[: chunks * (sides - 1)]
+    refs = refs[chunks * (sides - 1) :]
+    before_ref, shift_ref, sums_ref, tail_ref, own_ref, halo_ref, valid_ref = refs[:7]
+    outs = refs[7 : 7 + reps]
+    own_out, left_high, left_low, right_high, right_low, left, right, own = refs[7 + reps :]
+    here, cols = own_ref.shape
+    frames, feats = here * sides, shift_ref.shape[1]
     side = place_ref[1]
     shift = shift_ref[...]
-    every[0:HALO, :] = tail_ref[...]
-    place_pieces((size,), side, sides, pieces, every, HALO)
-    every[HALO : HALO + frames, :] = every[HALO : HALO + frames, :] - shift
-    own_columns(side, sides, every, own)
-    for s in range(sides):
-
-        @pl.when(side == s)
-        def _():
-            own[HALO + frames :, :] = halo_ref[...] - shift[:, s * cols : (s + 1) * cols]
-
-    own_out[...] = own[HALO : HALO + frames, :]
+    bases = [pl.multiple_of(lax.rem(side + sides - s, sides) * here, HALO) for s in range(sides)]
+    left[0:HALO, :] = tail_ref[...]
+    row = HALO
+    for s in range(1, sides):
+        for j, size in enumerate(sizes):
+            left[row : row + size, :] = decoded_piece(codes[j * (sides - 1) + s - 1], size) - shift
+            row += size
+    own[pl.ds(bases[0], here), :] = own_ref[...]
+
+    def keep_own(part):
+        own[frames:, :] = halo_ref[...] - shift[:, part]
+        for s in range(1, sides):
+            rows = slice(HALO + (s - 1) * here, HALO + s * here)
+            own[pl.ds(bases[s], here), :] = left[rows, part]
+
+    side_columns(side, sides, cols, keep_own)
+    own_out[...] = own[0:frames, :]
     valid_all = valid_ref[...]
     total = jnp.sum(valid_all)
     count = jnp.maximum(total, 1.0)
-    valid = valid_all[valid_all.shape[0] - frames :]
-    now = every[HALO : HALO + frames, :]
-    weighed = valid * now
-    sums = sums_ref[0:1, :] + row_sum(weighed)
-    squares = sums_ref[1:2, :] + row_sum(weighed * now)
-    later = own[HALO : HALO + frames + LAG, :]
-    weighed_later = valid_all[valid_all.shape[0] - frames - LAG :] * later
-    sums_next = sums_ref[2:3, 0:cols] + row_sum(weighed_later)
-    squares_next = sums_ref[3:4, 0:cols] + row_sum(weighed_later * later)
+    sums, squares = sums_ref[0:1, :], sums_ref[1:2, :]
+    sums_next, squares_next = sums_ref[2:3, 0:cols], sums_ref[3:4, 0:cols]
+    end = bases[0] + here - HALO
+    later = own[pl.ds(pl.multiple_of(end, HALO), 2 * HALO), :][LAG : LAG + HALO]
+    crossing = lax.broadcasted_iota(jnp.int32, (HALO, 1), 0) >= HALO - LAG
+    valid = valid_ref[pl.ds(pl.multiple_of(end, HALO), HALO), :]
+    weighed_later = jnp.where(crossing, valid * later, 0.0)
+    sums_next += row_sum(weighed_later)
+    squares_next += row_sum(weighed_later * later)
+    right[0:HALO, 0:cols] = jnp.zeros((HALO, cols), F32)
+    right[0:HALO, cols : 2 * cols] = weighed_later
+    for s in range(1, sides):
+        rows = slice(HALO + (s - 1) * here, HALO + s * here)
+        valid = valid_ref[pl.ds(bases[s], here), :]
+        weighed = valid * left[rows, :]
+        sums += row_sum(weighed)
+        squares += row_sum(weighed * left[rows, :])
+        around = own[pl.ds(bases[s], here + HALO), :]
+        right[rows, 0:cols] = valid * around[0:here]
+        later = around[LAG : LAG + here]
+        weighed_later = valid * later
+        right[rows, cols : 2 * cols] = weighed_later
+        sums_next += row_sum(weighed_later)
+        squares_next += row_sum(weighed_later * later)
     own_sums = jnp.zeros((1, cols), F32)
     own_shift = jnp.zeros((1, cols), F32)
     for s in range(sides):
@@ -336,29 +375,21 @@
         own_sums += mine * sums[:, s * cols : (s + 1) * cols]
         own_shift += mine * shift[:, s * cols : (s + 1) * cols]
     first = lax.broadcasted_iota(jnp.int32, (HALO, 1), 0) == 0
-    every[HALO + frames :, :] = jnp.where(first, sums, 0.0)
-    right[0:HALO, :] = jnp.zeros((HALO, 2 * cols), F32)
-    right[HALO : HALO + frames, 0:cols] = valid * own[HALO : HALO + frames, :]
-    right[HALO - LAG : HALO + frames, cols : 2 * cols] = weighed_later
-    right[HALO + frames :, 0:cols] = jnp.where(first, -own_sums / count, 0.0)
-    right[HALO + frames :, cols : 2 * cols] = jnp.where(first, -sums_next / count, 0.0)
-    high, low = split_in_two(every[...])
+    last = left.shape[0] - HALO
+    left[last:, :] = jnp.where(first, sums, 0.0)
+    right[last:, 0:cols] = jnp.where(first, -own_sums / count, 0.0)
+    right[last:, cols : 2 * cols] = jnp.where(first, -sums_next / count, 0.0)
+    high, low = split_in_two(left[...])
     left_high[...] = high.T
     left_low[...] = low.T
-    right_high, right_low = split_in_two(right[...])
-    for s in reversed(range(reps)):
-        rep = lax.rem(place_ref[2] + s, reps)
-        out = outs[s]
-        for z in range(groups):
-            at = pl.ds(pl.multiple_of((z * reps + rep) * rows, rows), rows)
-            part = before_ref[at, :]
-            part += jnp.dot(left_high[at, :], right_high, preferred_element_type=F32)
-            part += jnp.dot(left_high[at, :], right_low, preferred_element_type=F32)
-            part += jnp.dot(left_low[at, :], right_high, preferred_element_type=F32)
-            out[z * rows : (z + 1) * rows, :] = part
-        end = groups * rows
-        fold = feats // (2 * cols)
-        mean, square = shift + sums / count, squares - sums * sums / count
+    right_high[...], right_low[...] = split_in_two(right[...])
+    add_blocks(
+        place_ref, shifts, groups, before_ref, (left_high, left_low), (right_high, right_low), outs
+    )
+    fold = feats // (2 * cols)
+    mean, square = shift + sums / count, squares - sums * sums / count
+    for out in outs:
+        end = out.shape[0] - 8
         for f in range(fold):
             part = slice(2 * cols * f, 2 * cols * (f + 1))
             out[end + f : end + f + 1, :] = mean[:, part]
@@ -372,29 +403,56 @@
             out[end + 2 :, :] = jnp.zeros((spare, 2 * cols), F32)
 
 
-def late_moments(pieces, before, shift, sums, tail, halo, valid, place, sides, groups, reps):
-    size, feats = pieces[0].shape
-    cols = feats // sides
-    frames = sides * size
+def late_moments(codes, before, shift, sums, tail, own, halo, valid, place, sides, groups, reps, shifts):
+    sizes = tuple(chunk[0].shape[0] - HALO for chunk in codes)
+    codes = [code for chunk in codes for code in chunk]
+    here, cols = own.shape
+    feats = shift.shape[1]
+    depth = here * (sides - 1) + 2 * HALO
+    rows = feats // (groups * reps)
     vmem = pl.BlockSpec(memory_space=pltpu.VMEM)
     outs = pl.pallas_call(
-        functools.partial(late_kernel, size, sides, groups, reps),
-        in_specs=[pl.BlockSpec(memory_space=pltpu.SMEM)] + [vmem] * (len(pieces) + 6),
-        out_specs=[vmem] * (reps + 1),
-        out_shape=[jax.ShapeDtypeStruct((feats // reps + 8, 2 * cols), F32)] * reps
-        + [jax.ShapeDtypeStruct((frames, cols), F32)],
+        functools.partial(late_kernel, sizes, sides, groups, reps, shifts),
+        in_specs=[pl.BlockSpec(memory_space=pltpu.SMEM)] + [vmem] * (len(codes) + 7),
+        out_specs=[vmem] * (reps + 5),
+        out_shape=[jax.ShapeDtypeStruct((len(shifts) * rows + 8, 2 * cols), F32)] * reps
+        + [
+            jax.ShapeDtypeStruct((here * sides, cols), F32),
+            jax.ShapeDtypeStruct((feats, depth), BF16),
+            jax.ShapeDtypeStruct((feats, depth), BF16),
+            jax.ShapeDtypeStruct((depth, 2 * cols), BF16),
+            jax.ShapeDtypeStruct((depth, 2 * cols), BF16),
+        ],
         scratch_shapes=[
-            pltpu.VMEM((frames + 2 * HALO, feats), F32),
-            pltpu.VMEM((frames + 2 * HALO, cols), F32),
-            pltpu.VMEM((frames + 2 * HALO, 2 * cols), F32),
-            pltpu.VMEM((feats, frames + 2 * HALO), BF16),
-            pltpu.VMEM((feats, frames + 2 * HALO), BF16),
+            pltpu.VMEM((depth, feats), F32),
+            pltpu.VMEM((depth, 2 * cols), F32),
+            pltpu.VMEM((here * sides + HALO, cols), F32),
         ],
         compiler_params=params(),
         cost_estimate=SMALL,
         name="late_moments",
-    )(place, *pieces, before, shift, sums, tail, halo, valid)
-    return outs[:reps], outs[reps]
+    )(place, *codes, before, shift, sums, tail, own, halo, valid)
+    return outs[:reps], outs[reps], outs[reps + 1 :]
+
+
+def rest_kernel(groups, shifts, place_ref, before_ref, left_high, left_low, right_high, right_low, *outs):
+    add_blocks(
+        place_ref, shifts, groups, before_ref, (left_high, left_low), (right_high, right_low), outs
+    )
+
+
+def rest_moments(before, factors, place, groups, reps, shifts):
+    rows = before.shape[0] // (groups * reps)
+    vmem = pl.BlockSpec(memory_space=pltpu.VMEM)
+    return pl.pallas_call(
+        functools.partial(rest_kernel, groups, shifts),
+        in_specs=[pl.BlockSpec(memory_space=pltpu.SMEM)] + [vmem] * 5,
+        out_specs=[vmem] * reps,
+        out_shape=[jax.ShapeDtypeStruct((len(shifts) * rows, before.shape[1]), F32)] * reps,
+        compiler_params=params(),
+        cost_estimate=SMALL,
+        name="rest_moments",
+    )(place, before, *factors)
 
 
 def rolled(value, first):
@@ -407,81 +465,115 @@
     return jnp.broadcast_to(row, (8, row.shape[1])).T[:, 0:1]
 
 
-def share_kernel(groups, feats, place_ref, *refs):
-    parts, outs = refs[: -groups - 1], refs[-groups - 1 :]
-    reps, width = len(parts), outs[0].shape[1]
+def code_block(place_ref, groups, reps, s, i, parts, norms, out):
+    width = parts[0].shape[1]
     cols = width // 2
+    feats = norms.shape[1]
+    rows = feats // (groups * reps)
+    at = slice(i * rows, (i + 1) * rows)
+    total = parts[0][at, :]
+    for part in parts[1:]:
+        total += part[at, :]
+    if s == 0:
+        out[...] = total
+        return
+    there = lax.rem(place_ref[0] + s, groups)
+    first = (there * reps + place_ref[2]) * rows
+    inverse_cols = jnp.concatenate(
+        [rolled(norms[0:1, :], place_ref[1] * cols)[:, :cols], norms[1:2, :cols]], 1
+    )
+    ratio = total * as_column(rolled(norms[0:1, :], first)[:, :rows]) * inverse_cols
+    root = jnp.sqrt(jnp.minimum(jnp.abs(ratio), 1.001)) * CODE
+    root = jnp.where(ratio < 0.0, -root, root)
+    out[0:rows, :] = jnp.round(root).astype(jnp.int32).astype(jnp.int16)
+
+
+def first_share_kernel(groups, shifts, place_ref, *refs):
+    count = len(shifts)
+    parts, outs, codes_out, norms_out = refs[: -count - 2], refs[-count - 2 : -2], refs[-2], refs[-1]
+    reps, width = len(parts), parts[0].shape[1]
+    cols, feats = width // 2, norms_out.shape[1]
     fold = feats // width
-    rows = outs[0].shape[0]
-    end = groups * rows
+    end = parts[0].shape[0] - 8
     square = jnp.zeros((1, feats), F32)
     square_next = jnp.zeros((1, cols), F32)
     codes = []
     for part in parts:
         own = part[end : end + 8, :]
-        mean = [own[f : f + 1] for f in range(fold)]
         squares = [own[fold + f : fold + f + 1] for f in range(fold)]
         final = own[2 * fold : 2 * fold + 1]
         square += jnp.concatenate(squares, 1)
         square_next += final[:, cols:]
-        for line in mean:
-            codes += coded(line, MEAN_STEP)
+        for f in range(fold):
+            codes += coded(own[f : f + 1], MEAN_STEP)
         for line in squares:
             codes += coded(jnp.sqrt(jnp.maximum(line, 0.0)), ROOT_STEP)
-        codes += coded(final[:, :cols], MEAN_STEP)
-        codes[-2:] = [
-            jnp.concatenate(pair, 1)
-            for pair in zip(codes[-2:], coded(jnp.sqrt(jnp.maximum(final[:, cols:], 0.0)), ROOT_STEP))
-        ]
+        pair = coded(final[:, :cols], MEAN_STEP)
+        pair_next = coded(jnp.sqrt(jnp.maximum(final[:, cols:], 0.0)), ROOT_STEP)
+        codes += [jnp.concatenate(both, 1) for both in zip(pair, pair_next)]
         codes.append(own[2 * fold + 1 : 2 * fold + 2])
-    spare = outs[1].shape[0] - rows - len(codes)
+    spare = codes_out.shape[0] - len(codes)
     if spare:
         codes.append(jnp.zeros((spare, width), F32))
     codes = jnp.concatenate(codes, 0).astype(jnp.int32).astype(jnp.int16)
-    inverse = lax.rsqrt(jnp.maximum(square, TINY))
-    inverse_next = lax.rsqrt(jnp.maximum(square_next, TINY))
-    inverse_cols = jnp.concatenate(
-        [rolled(inverse, place_ref[1] * cols)[:, :cols], inverse_next], 1
-    )
-    for s in range(groups):
-        there = lax.rem(place_ref[0] + s, groups)
-        at = pl.ds(pl.multiple_of(there * rows, rows), rows)
-        total = parts[0][at, :]
-        for part in parts[1:]:
-            total += part[at, :]
-        if s == 0:
-            outs[0][...] = total
-            continue
-        first = (there * reps + place_ref[2]) * rows
-        ratio = total * as_column(rolled(inverse, first)[:, :rows]) * inverse_cols
-        root = jnp.sqrt(jnp.minimum(jnp.abs(ratio), 1.001)) * CODE
-        root = jnp.where(ratio < 0.0, -root, root)
-        outs[s][0:rows, :] = jnp.round(root).astype(jnp.int32).astype(jnp.int16)
-        outs[s][rows:, :] = codes
-    outs[groups][...] = codes
-
-
-def share(parts, place, groups, feats):
+    codes_out[...] = codes
+    norms_out[...] = jnp.zeros(norms_out.shape, F32)
+    norms_out[0:1, :] = lax.rsqrt(jnp.maximum(square, TINY))
+    norms_out[1:2, :cols] = lax.rsqrt(jnp.maximum(square_next, TINY))
+    for i, (s, out) in enumerate(zip(shifts, outs)):
+        code_block(place_ref, groups, reps, s, i, parts, norms_out, out)
+        out[out.shape[0] - codes.shape[0] :, :] = codes
+
+
+def rest_share_kernel(groups, shifts, place_ref, norms_ref, codes_ref, *refs):
+    count = len(shifts)
+    parts, outs = refs[:-count], refs[-count:]
+    for i, (s, out) in enumerate(zip(shifts, outs)):
+        code_block(place_ref, groups, len(parts), s, i, parts, norms_ref, out)
+        if s:
+            out[out.shape[0] - codes_ref.shape[0] :, :] = codes_ref[...]
+
+
+def first_share(parts, place, groups, shifts, feats):
+    width, reps = parts[0].shape[1], len(parts)
+    rows = feats // (groups * reps)
+    lines = -(-reps * (4 * (feats // width) + 3) // 16) * 16
+    vmem = pl.BlockSpec(memory_space=pltpu.VMEM)
+    outs = pl.pallas_call(
+        functools.partial(first_share_kernel, groups, shifts),
+        in_specs=[pl.BlockSpec(memory_space=pltpu.SMEM)] + [vmem] * reps,
+        out_specs=[vmem] * (len(shifts) + 2),
+        out_shape=[jax.ShapeDtypeStruct((rows + lines, width), jnp.int16)] * len(shifts)
+        + [
+            jax.ShapeDtypeStruct((lines, width), jnp.int16),
+            jax.ShapeDtypeStruct((8, feats), F32),
+        ],
+        compiler_params=params(),
+        cost_estimate=SMALL,
+        name="first_share",
+    )(place, *parts)
+    return outs[:-2], outs[-2], outs[-1]
+
+
+def rest_share(parts, norms, codes, place, groups, shifts):
     width = parts[0].shape[1]
-    rows = (parts[0].shape[0] - 8) // groups
-    lines = -(-len(parts) * (4 * (feats // width) + 3) // 16) * 16
+    rows = parts[0].shape[0] // len(shifts)
+    coded_shape = jax.ShapeDtypeStruct((rows + codes.shape[0], width), jnp.int16)
     vmem = pl.BlockSpec(memory_space=pltpu.VMEM)
     return pl.pallas_call(
-        functools.partial(share_kernel, groups, feats),
-        in_specs=[pl.BlockSpec(memory_space=pltpu.SMEM)] + [vmem] * len(parts),
-        out_specs=[vmem] * (groups + 1),
-        out_shape=[jax.ShapeDtypeStruct((rows, width), F32)]
-        + [jax.ShapeDtypeStruct((rows + lines, width), jnp.int16)] * (groups - 1)
-        + [jax.ShapeDtypeStruct((lines, width), jnp.int16)],
+        functools.partial(rest_share_kernel, groups, shifts),
+        in_specs=[pl.BlockSpec(memory_space=pltpu.SMEM)] + [vmem] * (len(parts) + 2),
+        out_specs=[vmem] * len(shifts),
+        out_shape=[coded_shape if s else jax.ShapeDtypeStruct((rows, width), F32) for s in shifts],
         compiler_params=params(),
         cost_estimate=SMALL,
-        name="share",
-    )(place, *parts)
+        name="rest_share",
+    )(place, norms, codes, *parts)
 
 
 def finish_kernel(reps, place_ref, kept_ref, codes_ref, *refs):
-    blocks = refs[:-6]
-    shift_ref, early_ref, late_ref, inst_out, lag_out, projections_out = refs[-6:]
+    blocks = refs[:-5]
+    shift_ref, own_ref, inst_out, lag_out, projections_out = refs[-5:]
     rows, cols = inst_out.shape
     feats = shift_ref.shape[1]
     width = 2 * cols
@@ -551,19 +643,16 @@
     inst_out[...] = moment[:, 0:cols] * scale_cols
     lag_out[...] = moment[:, cols : 2 * cols] * scale_next
     offset = rolled(shift_ref[...] - mean, first_col)[:, :cols]
-    split = early_ref.shape[0]
-    projections_out[0:split, :] = (early_ref[...] + offset) * scale_cols
-    projections_out[split:, :] = (late_ref[...] + offset) * scale_cols
-
-
-def finish(kept, codes, blocks, shift, early, late, place, reps):
+    projections_out[...] = (own_ref[...] + offset) * scale_cols
+
+
+def finish(kept, codes, blocks, shift, own, place, reps):
     rows = kept.shape[0]
-    cols = early.shape[1]
-    frames = early.shape[0] + late.shape[0]
+    frames, cols = own.shape
     vmem = pl.BlockSpec(memory_space=pltpu.VMEM)
     return pl.pallas_call(
         functools.partial(finish_kernel, reps),
-        in_specs=[pl.BlockSpec(memory_space=pltpu.SMEM)] + [vmem] * (len(blocks) + 5),
+        in_specs=[pl.BlockSpec(memory_space=pltpu.SMEM)] + [vmem] * (len(blocks) + 4),
         out_specs=[vmem] * 3,
         out_shape=[
             jax.ShapeDtypeStruct((rows, cols), F32),
@@ -573,7 +662,7 @@
         compiler_params=params(),
         cost_estimate=SMALL,
         name="finish",
-    )(place, kept, codes, *blocks, shift, early, late)
+    )(place, kept, codes, *blocks, shift, own)
 
 
 def upto(width):
@@ -636,7 +725,7 @@
             jax.ShapeDtypeStruct((1, 128), F32),
         ],
         compiler_params=params(),
-        cost_estimate=SMALL,
+        cost_estimate=LARGE,
         name="pair_signs",
     )(place, after, *pairs)
 
@@ -663,9 +752,9 @@
         if j:
             picked = pick(coords, chosen, arrived[-1][1], place, start, size, groups)
         arrived.append([picked[0]] + [rotated(picked[s], "atoms", s) for s in range(1, groups)])
-        start += sides * size
-
-    signs, most_used = pair_signs(pairs, arrived[-1][0], place, groups, width, cap)
+        start += size
+
+    signs, most_used = pair_signs(pairs, arrived[0][0], place, groups, width, cap)
 
     ids = jnp.concatenate([traj_ids[0], jnp.full((LAG,), -1, jnp.int32)])
     offset = atom_index * frames
@@ -673,31 +762,35 @@
     ids_later = lax.dynamic_slice_in_dim(ids, offset + LAG, frames)
     valid = (ids_now == ids_later).astype(F32)[:, None]
 
-    pieces, after = [], arrived[-1][0]
-    for blocks in arrived:
-        block, codes = distances(blocks, signs, after)
+    own_pieces, codes, after = [], [], arrived[-1][0]
+    for j, blocks in enumerate(arrived):
+        block, code = distances(blocks, signs, after)
         after = block
-        pieces.append([block] + [rotated(codes, "feat", s) for s in range(1, sides)])
-
-    opening = pieces[0][0][:HALO]
+        own_pieces.append(block)
+        codes.append([rotated(code, "feat", s) for s in range(1, sides)])
+        if j == 0:
+            opening = passed_down(block[:HALO], "atoms")
+    halo = lax.dynamic_slice_in_dim(opening, feat_index * cols, cols, 1)
     for s in range(1, sides):
-        first = lax.rem(feat_index + sides - s, sides) == 0
-        opening = jnp.where(first, decoded_piece(pieces[0][s], HALO), opening)
-    opening = lax.dynamic_slice_in_dim(opening, feat_index * cols, cols, 1)
-    halo = passed_down(opening, "atoms")
-
-    early = [piece for chunk in pieces[:-1] for piece in chunk]
-    before, own_early, shift, sums, tail = early_moments(early, valid, place, sizes[:-1], sides)
+        there = lax.rem(feat_index + s, sides)
+        sent = rotated(lax.dynamic_slice_in_dim(opening, there * cols, cols, 1), "feat", s)
+        halo = jnp.where(feat_index == s, sent, halo)
+
     reps = lax.axis_size("rep")
-    parts, own_late = late_moments(
-        pieces[-1], before, shift, sums, tail, halo, valid, place, sides, groups, reps
+    shifts = list(range(1, groups)) + [0]
+    shifts = tuple(shifts[: groups // 2]), tuple(shifts[groups // 2 :])
+    before, own, shift, sums, tail = early_moments(own_pieces, valid, place, sides)
+    parts, own, factors = late_moments(
+        codes, before, shift, sums, tail, own, halo, valid, place, sides, groups, reps, shifts[0]
     )
-    parts = [parts[0]] + [rotated(parts[s], "rep", s) for s in range(1, reps)]
-    kept, *blocks, codes = share(parts, place, groups, feats)
-    blocks = [rotated(block, "atoms", s + 1) for s, block in enumerate(blocks)]
-    corr_inst, corr_lag, projections = finish(
-        kept, codes, blocks, shift, own_early, own_late, place, reps
-    )
+    parts = [parts[0]] + [rotated(parts[r], "rep", r) for r in range(1, reps)]
+    rest = rest_moments(before, factors, place, groups, reps, shifts[1])
+    rest = [rest[0]] + [rotated(rest[r], "rep", r) for r in range(1, reps)]
+    blocks, stats, norms = first_share(parts, place, groups, shifts[0], feats)
+    blocks = [rotated(block, "atoms", s) for s, block in zip(shifts[0], blocks)]
+    *more, kept = rest_share(rest, norms, stats, place, groups, shifts[1])
+    blocks += [rotated(block, "atoms", s) for s, block in zip(shifts[1], more)]
+    corr_inst, corr_lag, projections = finish(kept, stats, blocks, shift, own, place, reps)
     return (corr_inst, corr_lag, projections[None]), most_used[0, 0]
 
 
@@ -707,7 +800,7 @@
     width = atom_coords.shape[3]
     coords = jnp.transpose(atom_coords[0], (1, 0, 2))
     pairs = [atom_pairs] + [rotated(atom_pairs, "feat", s) for s in range(1, lax.axis_size("feat"))]
-    cap = min(width, -(-(width * 9 // 16) // 64) * 64)
+    cap = min(width, packed(width * 5 // 9) // 3)
     outs, most_used = with_cap(cap, coords, pairs, traj_ids, place)
 
     def again(carry):

time: 127 us -> 119 us (0.937)
  starting transfers between devices: 18.7 us -> 15.6 us
  Pallas kernels: 34 us -> 31.5 us
  local copies, waits for them, and re-layouts: 4.12 us -> 2.18 us
    ppermute x1, waiting for transfers between devices: 0.01 us -> 6.4 us  [passed_down(): lax.ppermute(block, axis, [(i + 1, i) for i in range(lax.axis_size(axis)...]
    ppermute x13 -> x15, waiting for transfers between devices: 66.9 us -> 60.5 us  [rotated(): lax.ppermute(block, axis, [(i, (i + shift) % size) for i in range(size)])]
    ppermute x13 -> x15, starting transfers between devices: 16.8 us -> 13.7 us  [rotated(): lax.ppermute(block, axis, [(i, (i + shift) % size) for i in range(size)])]
    pallas_call x2, Pallas kernels: 6.2 us -> 3.8 us  [distances(): pl.pallas_call(distance_kernel, in_specs=[vmem] * (len(blocks) + 1) + [pl...]
    unnamed x18 -> x22, local copies, waits for them, and re-layouts: 3.81 us -> 2.02 us
    pallas_call x3 -> x5, Pallas kernels: 11 us -> 11.1 us  [the longest x1 3.32 us: late_moments(): pl.pallas_call(functools.partial(late_kernel, sizes, sides, groups, reps,...]
  transfers between devices with their start and end apart: 14 -> 16, of which waited for: 11 -> 8; matrix products, arithmetic and copies ran while one was open for 0% -> 0% of each run, Pallas kernels for 16% -> 18%
where the time goes in v4:
time: 119 us; the launch traced here: 118 us
  waiting for transfers between devices  66.9 us (56%)
  Pallas kernels  31.5 us (26%)
  starting transfers between devices  15.6 us (13%)
  local copies, waits for them, and re-layouts  2.18 us (2%)
    ppermute x15, waiting for transfers between devices, rotated(): lax.ppermute(block, axis, [(i, (i + shift) % size) for i in range(size)])  60.5 us
    ppermute x15, starting transfers between devices, rotated(): lax.ppermute(block, axis, [(i, (i + shift) % size) for i in range(size)])  13.7 us
    pallas_call x1, Pallas kernels, pair_signs(): pl.pallas_call(functools.partial(signs_kernel, groups, width, cap), in_sp...  6.49 us
    ppermute x1, waiting for transfers between devices, passed_down(): lax.ppermute(block, axis, [(i + 1, i) for i in range(lax.axis_size(axis)...  6.4 us
    pallas_call x1, Pallas kernels, first_pick(): pl.pallas_call(functools.partial(first_pick_kernel, len(pairs)), in_specs...  4.56 us
    pallas_call x2, Pallas kernels, distances(): pl.pallas_call(distance_kernel, in_specs=[vmem] * (len(blocks) + 1) + [pl...  3.8 us
    pallas_call x1, Pallas kernels, late_moments(): pl.pallas_call(functools.partial(late_kernel, sizes, sides, groups, reps,...  3.32 us
    pallas_call x1, Pallas kernels, finish(): pl.pallas_call(functools.partial(finish_kernel, reps), in_specs=[pl.Block...  2.82 us
  transfers between devices with their start and end apart: 16, of which 8 were waited for; matrix products, arithmetic and copies ran while one was open for 0% of the time, Pallas kernels for 18%

profile of v4, /device:TPU:9, one launch (start us, length us, event | category | flops | bytes accessed | tf_op | source)
XLA Modules:
  0.0 117.7 jit_solution(16040830482912370780)
XLA Ops:
  0.6 1.3 %collective-permute-start.15 = (s32[2,512]{1,0:T(2,128)}, s32[2,512]{1,0:T(2,128)S(1)}, u32[]{:S(2)}, u32[]{:S(2)}) collective-permute-start(s32[2,512]{1,0:T(2,128)} %refs_0_.1), channel_id=1, source_target_pairs={{0,2},{2,0},{1,3},{3,1},{4,6},{6,4},{5,7},{7,5},{8,10},{10,8},{9,1... | collective-permute-start | bytes 12296 | tf_op jit(solution)/shard_map/ppermute | solution.py:28
  1.9 0.1 pad_add_fusion.place_ref
  2.0 1.4 %collective-permute-done.15.refs_1_ = s32[2,512]{1,0:T(2,128)S(1)} collective-permute-done((s32[2,512]{1,0:T(2,128)}, s32[2,512]{1,0:T(2,128)S(1)}, u32[]{:S(2)}, u32[]{:S(2)}) %collective-permute-start.15) | collective-permute-done | bytes 4128 | tf_op jit(solution)/shard_map/ppermute | solution.py:28
  3.4 4.6 %first_pick.5 = (bf16[768,426]{1,0:T(8,128)(2,1)S(1)}, s32[1,2048]{1,0:T(1,128)S(1)}, s32[2,512]{1,0:T(2,128)S(1)}, s32[2,512]{1,0:T(2,128)S(1)}, bf16[160,1280]...) custom-call(s32[3]{0:T(128)S(1)} %pad_add_fusion.place_ref, ...), custom_call_target="tpu_custom_call" | custom-call | flops 1024 | bytes 1024 | tf_op jit(solution)/shard_map/first_pick/pallas_call | solution.py:99
  7.9 1.3 %collective-permute-start.16 = (bf16[160,1280]{1,0:T(8,128)(2,1)S(1)}, bf16[160,1280]{1,0:T(8,128)(2,1)S(1)}, u32[]{:S(2)}, u32[]{:S(2)}) collective-permute-start(bf16[160,1280]{1,0:T(8,128)(2,1)S(1)} %get-tuple-element.255), channel_id=1, source_target_pairs={{0,4},{4,8},{8,12},{12,0},{1,5},{5,9},{9,13},{13,1},{2,6},{6,10},{... | collective-permute-start | bytes 1228808 | tf_op jit(solution)/shard_map/ppermute | solution.py:28
  9.3 1.1 collective-permute-start.17
  10.4 1.4 %collective-permute-start.18 = (bf16[160,1280]{1,0:T(8,128)(2,1)S(1)}, bf16[160,1280]{1,0:T(8,128)(2,1)S(1)}, u32[]{:S(2)}, u32[]{:S(2)}) collective-permute-start(bf16[160,1280]{1,0:T(8,128)(2,1)S(1)} %get-tuple-element.257), channel_id=1, source_target_pairs={{0,12},{4,0},{8,4},{12,8},{1,13},{5,1},{9,5},{13,9},{2,14},{6,2},{... | collective-permute-start | bytes 1228808 | tf_op jit(solution)/shard_map/ppermute | solution.py:28
  11.8 6.5 %pair_signs.5 = (bf16[1704,1024]{1,0:T(8,128)(2,1)S(1)}, f32[1,128]{1,0:T(1,128)S(1)}) custom-call(s32[3]{0:T(128)S(1)} %pad_add_fusion.place_ref, bf16[160,1280]{1,0:T(8,128)(2,1)S(1)} %get-tuple-element.251.after_ref.refs_0_, s32[2,512]{1,0:T(2,128)S(1)} %get-tuple-element.252.refs_0_, s32[2,512]{1,0:T(2,128)S(1)} %get-tuple-element.253.refs_1_), custom_call_target="tpu_custom_call" | custom-call | flops 99999997952 | bytes 1024 | tf_op jit(solution)/shard_map/pair_signs/pallas_call | solution.py:718
  18.3 0.0 collective-permute-done.16.after_ref.refs_1_
  18.4 2.8 %pick.5 = (bf16[96,1280]{1,0:T(8,128)(2,1)S(1)}, bf16[96,1280]{1,0:T(8,128)(2,1)S(1)}, bf16[96,1280]{1,0:T(8,128)(2,1)S(1)}, bf16[96,1280]{1,0:T(8,128)(2,1)S(1)}) custom-call(s32[3]{0:T(128)S(1)} %pad_add_fusion.place_ref, bf16[3,2048,768]{2,1,0:T(8,128)(2,1)S(1)} %bitcast.27, bf16[768,426]{1,0:T(8,128)(2,1)S(1)} %get-tuple-element.259.chosen_ref, ...), custom_call_target="tpu_custom_call" | custom-call | flops 1024 | bytes 1024 | tf_op jit(solution)/shard_map/pick/pallas_call | solution.py:136
  21.2 0.3 collective-permute-start.20
  21.4 3.1 %collective-permute-start.21 = (bf16[96,1280]{1,0:T(8,128)(2,1)S(1)}, bf16[96,1280]{1,0:T(8,128)(2,1)S(1)}, u32[]{:S(2)}, u32[]{:S(2)}) collective-permute-start(bf16[96,1280]{1,0:T(8,128)(2,1)S(1)} %get-tuple-element.263), channel_id=1, source_target_pairs={{0,8},{4,12},{8,0},{12,4},{1,9},{5,13},{9,1},{13,5},{2,10},{6,14},... | collective-permute-start | bytes 737288 | tf_op jit(solution)/shard_map/ppermute | solution.py:28
  24.5 0.0 collective-permute-start.22
  24.5 28.6 %collective-permute-done.17.refs_2_ = bf16[160,1280]{1,0:T(8,128)(2,1)S(1)} collective-permute-done((bf16[160,1280]{1,0:T(8,128)(2,1)S(1)}, bf16[160,1280]{1,0:T(8,128)(2,1)S(1)}, u32[]{:S(2)}, u32[]{:S(2)}) %collective-permute-start.17) | collective-permute-done | bytes 409632 | tf_op jit(solution)/shard_map/ppermute | solution.py:28
  53.1 4.1 %collective-permute-done.18.refs_3_ = bf16[160,1280]{1,0:T(8,128)(2,1)S(1)} collective-permute-done((bf16[160,1280]{1,0:T(8,128)(2,1)S(1)}, bf16[160,1280]{1,0:T(8,128)(2,1)S(1)}, u32[]{:S(2)}, u32[]{:S(2)}) %collective-permute-start.18) | collective-permute-done | bytes 409632 | tf_op jit(solution)/shard_map/ppermute | solution.py:28
  57.2 2.3 %distances.10 = (f32[160,1024]{1,0:T(8,128)S(1)}, s16[176,1024]{1,0:T(8,128)(2,1)S(1)}) custom-call(bf16[160,1280]{1,0:T(8,128)(2,1)S(1)} %get-tuple-element.251.after_ref.refs_0_, bf16[160,1280]{1,0:T(8,128)(2,1)S(1)} %collective-permute-done.16.after_ref.refs_1_, bf16[160,1280]{1,0:T(8,128)(2,1)S(1)} %collective-permute-done.17.refs_2_, ...), custom_call_target="tpu_custom_call" | custom-call | flops 99999997952 | bytes 1024 | tf_op jit(solution)/shard_map/distances/pallas_call | solution.py:202
  59.5 1.9 %collective-permute-start.24 = (f32[16,1024]{1,0:T(8,128)S(1)}, f32[16,1024]{1,0:T(8,128)S(1)}, u32[]{:S(2)}, u32[]{:S(2)}) collective-permute-start(f32[16,1024]{1,0:T(8,128)S(1)} %slice.13), channel_id=1, source_target_pairs={{4,0},{8,4},{12,8},{5,1},{9,5},{13,9},{6,2},{10,6},{14,10},{7,3},{... | collective-permute-start | bytes 196616 | tf_op jit(solution)/shard_map/ppermute | solution.py:32
  61.5 1.3 %collective-permute-start.19 = (s16[176,1024]{1,0:T(8,128)(2,1)S(1)}, s16[176,1024]{1,0:T(8,128)(2,1)S(1)}, u32[]{:S(2)}, u32[]{:S(2)}) collective-permute-start(s16[176,1024]{1,0:T(8,128)(2,1)S(1)} %get-tuple-element.261), channel_id=1, source_target_pairs={{0,2},{2,0},{1,3},{3,1},{4,6},{6,4},{5,7},{7,5},{8,10},{10,8},{9,1... | collective-permute-start | bytes 1081352 | tf_op jit(solution)/shard_map/ppermute | solution.py:28
  62.7 6.4 %collective-permute-done.24 = f32[16,1024]{1,0:T(8,128)S(1)} collective-permute-done((f32[16,1024]{1,0:T(8,128)S(1)}, f32[16,1024]{1,0:T(8,128)S(1)}, u32[]{:S(2)}, u32[]{:S(2)}) %collective-permute-start.24) | collective-permute-done | bytes 65568 | tf_op jit(solution)/shard_map/ppermute | solution.py:32
  69.1 1.2 %collective-permute-start.25 = (f32[16,512]{1,0:T(8,128)S(1)}, f32[16,512]{1,0:T(8,128)S(1)}, u32[]{:S(2)}, u32[]{:S(2)}) collective-permute-start(f32[16,512]{1,0:T(8,128)S(1)} %constant_dynamic-slice_fusion.1), channel_id=1, source_target_pairs={{0,2},{2,0},{1,3},{3,1},{4,6},{6,4},{5,7},{7,5},{8,10},{10,8},{9,1... | collective-permute-start | bytes 98312 | tf_op jit(solution)/shard_map/ppermute | solution.py:28
  70.3 0.0 collective-permute-done.20.refs_1_
  70.3 0.0 collective-permute-done.21.refs_2_
  70.4 0.0 collective-permute-done.22.refs_3_
  70.4 2.0 %copy-done.1 = bf16[1704,1024]{1,0:T(8,128)(2,1)S(1)} copy-done((bf16[1704,1024]{1,0:T(8,128)(2,1)S(1)}, bf16[1704,1024]{1,0:T(8,128)(2,1)}, u32[]{:S(2)}) %copy-start.1) | copy-done | bytes 3489816
  72.3 1.5 %distances.11 = (f32[96,1024]{1,0:T(8,128)S(1)}, s16[112,1024]{1,0:T(8,128)(2,1)S(1)}) custom-call(bf16[96,1280]{1,0:T(8,128)(2,1)S(1)} %get-tuple-element.260.refs_5_.refs_0_, bf16[96,1280]{1,0:T(8,128)(2,1)S(1)} %collective-permute-done.20.refs_1_, bf16[96,1280]{1,0:T(8,128)(2,1)S(1)} %collective-permute-done.21.refs_2_, ...), custom_call_target="tpu_custom_call" | custom-call | flops 99999997952 | bytes 1024 | tf_op jit(solution)/shard_map/distances/pallas_call | solution.py:202
  73.9 0.3 collective-permute-start.23
  74.2 0.1 fusion.3
  74.3 0.2 copy.8.refs_2_.refs_8_
  74.4 0.0 collective-permute-done.25
  74.5 2.8 %early_moments.5 = (f32[1024,1024]{1,0:T(8,128)S(1)}, f32[256,512]{1,0:T(8,128)S(1)}, f32[1,1024]{1,0:T(1,128)S(1)}, f32[4,1024]{1,0:T(4,128)S(1)}, f32[16,1024]{1,0:T(8,128)S(1)}) custom-call(s32[3]{0:T(128)S(1)} %copy-done.3, f32[160,1024]{1,0:T(8,128)S(1)} %get-tuple-element.265.refs_5_.refs_0_, f32[96,1024]{1,0:T(8,128)S(1)} %get-tuple-element.267.refs_1_, ...), custom_call_target="tpu_custom_call" | custom-call | flops 1024 | bytes 1024 | tf_op jit(solution)/shard_map/early_moments/pallas_call | solution.py:281
  77.3 0.0 collective-permute-done.19.refs_0_
  77.3 3.0 %collective-permute-done.23.refs_1_ = s16[112,1024]{1,0:T(8,128)(2,1)S(1)} collective-permute-done((s16[112,1024]{1,0:T(8,128)(2,1)S(1)}, s16[112,1024]{1,0:T(8,128)(2,1)S(1)}, u32[]{:S(2)}, u32[]{:S(2)}) %collective-permute-start.23) | collective-permute-done | bytes 229408 | tf_op jit(solution)/shard_map/ppermute | solution.py:28
  80.3 3.3 %late_moments.5 = (f32[264,1024]{1,0:T(8,128)S(1)}, f32[264,1024]{1,0:T(8,128)S(1)}, f32[512,512]{1,0:T(8,128)S(1)}, bf16[1024,288]{1,0:T(8,128)(2,1)S(1)}, bf16...) custom-call(s32[3]{0:T(128)S(1)} %copy-done.3, ...), custom_call_target="tpu_custom_call" | custom-call | flops 1024 | bytes 1024 | tf_op jit(solution)/shard_map/late_moments/pallas_call | solution.py:414
  83.6 1.7 %collective-permute-start.26 = (f32[264,1024]{1,0:T(8,128)S(1)}, f32[264,1024]{1,0:T(8,128)S(1)}, u32[]{:S(2)}, u32[]{:S(2)}) collective-permute-start(f32[264,1024]{1,0:T(8,128)S(1)} %get-tuple-element.275), channel_id=1, source_target_pairs={{0,1},{1,0},{2,3},{3,2},{4,5},{5,4},{6,7},{7,6},{8,9},{9,8},{10,11... | collective-permute-start | bytes 3244040 | tf_op jit(solution)/shard_map/ppermute | solution.py:28
  85.3 2.3 %rest_moments.5 = (f32[256,1024]{1,0:T(8,128)S(1)}, f32[256,1024]{1,0:T(8,128)S(1)}) custom-call(s32[3]{0:T(128)S(1)} %copy-done.3, f32[1024,1024]{1,0:T(8,128)S(1)} %get-tuple-element.269.refs_2_.before_ref, bf16[1024,288]{1,0:T(8,128)(2,1)S(1)} %get-tuple-element.278.left_high, bf16[1024,288]{1,0:T(8,128)(2,1)S(1)} %get-tuple-element.279.left_low, ...), custom_call_target="tpu_custom_call" | custom-call | flops 1024 | bytes 1024 | tf_op jit(solution)/shard_map/rest_moments/pallas_call | solution.py:447
  87.7 0.1 collective-permute-start.27
  87.8 0.0 collective-permute-done.26.refs_1_
  87.8 1.5 %first_share.5 = (s16[144,1024]{1,0:T(8,128)(2,1)S(1)}, s16[144,1024]{1,0:T(8,128)(2,1)S(1)}, s16[16,1024]{1,0:T(8,128)(2,1)S(1)}, f32[8,1024]{1,0:T(8,128)S(1)}) custom-call(s32[3]{0:T(128)S(1)} %copy-done.3, f32[264,1024]{1,0:T(8,128)S(1)} %get-tuple-element.274.refs_0_, f32[264,1024]{1,0:T(8,128)S(1)} %collective-permute-done.26.refs_1_), custom_call_target="tpu_custom_call" | custom-call | flops 1024 | bytes 1024 | tf_op jit(solution)/shard_map/first_share/pallas_call | solution.py:542
  89.3 0.1 collective-permute-start.28
  89.3 0.1 collective-permute-start.29
  89.4 1.0 collective-permute-done.27.refs_1_
  90.4 1.1 rest_share.5
  91.5 0.4 collective-permute-start.30
  92.0 5.4 %collective-permute-done.28.refs_0_ = s16[144,1024]{1,0:T(8,128)(2,1)S(1)} collective-permute-done((s16[144,1024]{1,0:T(8,128)(2,1)S(1)}, s16[144,1024]{1,0:T(8,128)(2,1)S(1)}, u32[]{:S(2)}, u32[]{:S(2)}) %collective-permute-start.28) | collective-permute-done | bytes 294944 | tf_op jit(solution)/shard_map/ppermute | solution.py:28
  97.4 17.1 %collective-permute-done.29.refs_1_ = s16[144,1024]{1,0:T(8,128)(2,1)S(1)} collective-permute-done((s16[144,1024]{1,0:T(8,128)(2,1)S(1)}, s16[144,1024]{1,0:T(8,128)(2,1)S(1)}, u32[]{:S(2)}, u32[]{:S(2)}) %collective-permute-start.29) | collective-permute-done | bytes 294944 | tf_op jit(solution)/shard_map/ppermute | solution.py:28
  114.5 0.0 collective-permute-done.30.refs_2_
  114.5 2.8 %finish.5 = (f32[128,512]{1,0:T(8,128)}, f32[128,512]{1,0:T(8,128)}, f32[512,512]{1,0:T(8,128)}) custom-call(s32[3]{0:T(128)S(1)} %copy-done.3, f32[128,1024]{1,0:T(8,128)S(1)} %get-tuple-element.284.kept_ref, s16[16,1024]{1,0:T(8,128)(2,1)S(1)} %get-tuple-element.277.codes_ref, s16[144,1024]{1,0:T(8,128)(2,1)S(1)} %collective-permute-done.28.refs_0_, ...), custom_call_target="tpu_custom_call" | custom-call | flops 1024 | bytes 1024 | tf_op jit(solution)/shard_map/finish/pallas_call | solution.py:653
  117.3 0.2 while.16
  (25 shorter events, 0.1 us)
Async XLA Ops:
  0.6 2.7 %collective-permute-start.15 = (s32[2,512]{1,0:T(2,128)}, s32[2,512]{1,0:T(2,128)S(1)}, u32[]{:S(2)}, u32[]{:S(2)}) collective-permute-start(s32[2,512]{1,0:T(2,128)} %refs_0_.1), channel_id=1, source_target_pairs={{0,2},{2,0},{1,3},{3,1},{4,6},{6,4},{5,7},{7,5},{8,10},{10,8},{9,1... | collective-permute-start | bytes 12296 | tf_op jit(solution)/shard_map/ppermute | solution.py:28
  2.0 16.3 %copy-start.2 = (s32[3]{0:T(128)}, s32[3]{0:T(128)S(1)}, u32[]{:S(2)}) copy-start(s32[3]{0:T(128)S(1)} %pad_add_fusion.place_ref) | copy-start | bytes 40
  3.4 4.6 %copy-start.9 = (s32[2,512]{1,0:T(2,128)}, s32[2,512]{1,0:T(2,128)S(1)}, u32[]{:S(2)}) copy-start(s32[2,512]{1,0:T(2,128)S(1)} %collective-permute-done.15.refs_1_) | copy-start | bytes 12292
  7.9 10.3 %collective-permute-start.16 = (bf16[160,1280]{1,0:T(8,128)(2,1)S(1)}, bf16[160,1280]{1,0:T(8,128)(2,1)S(1)}, u32[]{:S(2)}, u32[]{:S(2)}) collective-permute-start(bf16[160,1280]{1,0:T(8,128)(2,1)S(1)} %get-tuple-element.255), channel_id=1, source_target_pairs={{0,4},{4,8},{8,12},{12,0},{1,5},{5,9},{9,13},{13,1},{2,6},{6,10},{... | collective-permute-start | bytes 1228808 | tf_op jit(solution)/shard_map/ppermute | solution.py:28
  9.3 43.8 %collective-permute-start.17 = (bf16[160,1280]{1,0:T(8,128)(2,1)S(1)}, bf16[160,1280]{1,0:T(8,128)(2,1)S(1)}, u32[]{:S(2)}, u32[]{:S(2)}) collective-permute-start(bf16[160,1280]{1,0:T(8,128)(2,1)S(1)} %get-tuple-element.256), channel_id=1, source_target_pairs={{0,8},{4,12},{8,0},{12,4},{1,9},{5,13},{9,1},{13,5},{2,10},{6,14},... | collective-permute-start | bytes 1228808 | tf_op jit(solution)/shard_map/ppermute | solution.py:28
  10.4 46.8 %collective-permute-start.18 = (bf16[160,1280]{1,0:T(8,128)(2,1)S(1)}, bf16[160,1280]{1,0:T(8,128)(2,1)S(1)}, u32[]{:S(2)}, u32[]{:S(2)}) collective-permute-start(bf16[160,1280]{1,0:T(8,128)(2,1)S(1)} %get-tuple-element.257), channel_id=1, source_target_pairs={{0,12},{4,0},{8,4},{12,8},{1,13},{5,1},{9,5},{13,9},{2,14},{6,2},{... | collective-permute-start | bytes 1228808 | tf_op jit(solution)/shard_map/ppermute | solution.py:28
  11.8 6.5 %slice-start = ((s8[9437184]{0:T(1024)(128)(4,1)}), s8[4194304]{0:T(1024)(128)(4,1)S(1)}, s32[]{:S(2)}) async-start(s8[9437184]{0:T(1024)(128)(4,1)} %bitcast.25), calls=%async_computation | async-start | bytes 8388608
  11.8 6.5 %slice-start.1 = ((s8[9437184]{0:T(1024)(128)(4,1)}), s8[4194304]{0:T(1024)(128)(4,1)S(1)}, s32[]{:S(2)}) async-start(s8[9437184]{0:T(1024)(128)(4,1)} %bitcast.25), calls=%async_computation.1 | async-start | bytes 8388608
  11.8 6.6 %slice-start.2 = ((s8[9437184]{0:T(1024)(128)(4,1)}), s8[1048576]{0:T(1024)(128)(4,1)S(1)}, s32[]{:S(2)}) async-start(s8[9437184]{0:T(1024)(128)(4,1)} %bitcast.25), calls=%async_computation.2 | async-start | bytes 2097152
  18.3 38.9 %copy-start = (bf16[1704,1024]{1,0:T(8,128)(2,1)}, bf16[1704,1024]{1,0:T(8,128)(2,1)S(1)}, u32[]{:S(2)}) copy-start(bf16[1704,1024]{1,0:T(8,128)(2,1)S(1)} %get-tuple-element.258.refs_4_) | copy-start | bytes 10469380
  21.2 49.2 %collective-permute-start.20 = (bf16[96,1280]{1,0:T(8,128)(2,1)S(1)}, bf16[96,1280]{1,0:T(8,128)(2,1)S(1)}, u32[]{:S(2)}, u32[]{:S(2)}) collective-permute-start(bf16[96,1280]{1,0:T(8,128)(2,1)S(1)} %get-tuple-element.262), channel_id=1, source_target_pairs={{0,4},{4,8},{8,12},{12,0},{1,5},{5,9},{9,13},{13,1},{2,6},{6,10},{... | collective-permute-start | bytes 737288 | tf_op jit(solution)/shard_map/ppermute | solution.py:28
  21.4 48.9 %collective-permute-start.21 = (bf16[96,1280]{1,0:T(8,128)(2,1)S(1)}, bf16[96,1280]{1,0:T(8,128)(2,1)S(1)}, u32[]{:S(2)}, u32[]{:S(2)}) collective-permute-start(bf16[96,1280]{1,0:T(8,128)(2,1)S(1)} %get-tuple-element.263), channel_id=1, source_target_pairs={{0,8},{4,12},{8,0},{12,4},{1,9},{5,13},{9,1},{13,5},{2,10},{6,14},... | collective-permute-start | bytes 737288 | tf_op jit(solution)/shard_map/ppermute | solution.py:28
  24.5 45.8 %collective-permute-start.22 = (bf16[96,1280]{1,0:T(8,128)(2,1)S(1)}, bf16[96,1280]{1,0:T(8,128)(2,1)S(1)}, u32[]{:S(2)}, u32[]{:S(2)}) collective-permute-start(bf16[96,1280]{1,0:T(8,128)(2,1)S(1)} %get-tuple-element.264), channel_id=1, source_target_pairs={{0,12},{4,0},{8,4},{12,8},{1,13},{5,1},{9,5},{13,9},{2,14},{6,2},{... | collective-permute-start | bytes 737288 | tf_op jit(solution)/shard_map/ppermute | solution.py:28
  59.5 9.6 %collective-permute-start.24 = (f32[16,1024]{1,0:T(8,128)S(1)}, f32[16,1024]{1,0:T(8,128)S(1)}, u32[]{:S(2)}, u32[]{:S(2)}) collective-permute-start(f32[16,1024]{1,0:T(8,128)S(1)} %slice.13), channel_id=1, source_target_pairs={{4,0},{8,4},{12,8},{5,1},{9,5},{13,9},{6,2},{10,6},{14,10},{7,3},{... | collective-permute-start | bytes 196616 | tf_op jit(solution)/shard_map/ppermute | solution.py:32
  61.5 15.8 %collective-permute-start.19 = (s16[176,1024]{1,0:T(8,128)(2,1)S(1)}, s16[176,1024]{1,0:T(8,128)(2,1)S(1)}, u32[]{:S(2)}, u32[]{:S(2)}) collective-permute-start(s16[176,1024]{1,0:T(8,128)(2,1)S(1)} %get-tuple-element.261), channel_id=1, source_target_pairs={{0,2},{2,0},{1,3},{3,1},{4,6},{6,4},{5,7},{7,5},{8,10},{10,8},{9,1... | collective-permute-start | bytes 1081352 | tf_op jit(solution)/shard_map/ppermute | solution.py:28
  69.1 5.3 %copy-start.3 = (s32[3]{0:T(128)S(1)}, s32[3]{0:T(128)}, u32[]{:S(2)}) copy-start(s32[3]{0:T(128)} %copy-done.2) | copy-start | bytes 40
  69.1 5.3 %collective-permute-start.25 = (f32[16,512]{1,0:T(8,128)S(1)}, f32[16,512]{1,0:T(8,128)S(1)}, u32[]{:S(2)}, u32[]{:S(2)}) collective-permute-start(f32[16,512]{1,0:T(8,128)S(1)} %constant_dynamic-slice_fusion.1), channel_id=1, source_target_pairs={{0,2},{2,0},{1,3},{3,1},{4,6},{6,4},{5,7},{7,5},{8,10},{10,8},{9,1... | collective-permute-start | bytes 98312 | tf_op jit(solution)/shard_map/ppermute | solution.py:28
  70.4 2.0 %copy-start.1 = (bf16[1704,1024]{1,0:T(8,128)(2,1)S(1)}, bf16[1704,1024]{1,0:T(8,128)(2,1)}, u32[]{:S(2)}) copy-start(bf16[1704,1024]{1,0:T(8,128)(2,1)} %copy-done) | copy-start | bytes 10469380
  73.9 6.4 %collective-permute-start.23 = (s16[112,1024]{1,0:T(8,128)(2,1)S(1)}, s16[112,1024]{1,0:T(8,128)(2,1)S(1)}, u32[]{:S(2)}, u32[]{:S(2)}) collective-permute-start(s16[112,1024]{1,0:T(8,128)(2,1)S(1)} %get-tuple-element.266), channel_id=1, source_target_pairs={{0,2},{2,0},{1,3},{3,1},{4,6},{6,4},{5,7},{7,5},{8,10},{10,8},{9,1... | collective-permute-start | bytes 688136 | tf_op jit(solution)/shard_map/ppermute | solution.py:28
  83.6 4.2 %collective-permute-start.26 = (f32[264,1024]{1,0:T(8,128)S(1)}, f32[264,1024]{1,0:T(8,128)S(1)}, u32[]{:S(2)}, u32[]{:S(2)}) collective-permute-start(f32[264,1024]{1,0:T(8,128)S(1)} %get-tuple-element.275), channel_id=1, source_target_pairs={{0,1},{1,0},{2,3},{3,2},{4,5},{5,4},{6,7},{7,6},{8,9},{9,8},{10,11... | collective-permute-start | bytes 3244040 | tf_op jit(solution)/shard_map/ppermute | solution.py:28
  87.7 2.7 %collective-permute-start.27 = (f32[256,1024]{1,0:T(8,128)S(1)}, f32[256,1024]{1,0:T(8,128)S(1)}, u32[]{:S(2)}, u32[]{:S(2)}) collective-permute-start(f32[256,1024]{1,0:T(8,128)S(1)} %get-tuple-element.283), channel_id=1, source_target_pairs={{0,1},{1,0},{2,3},{3,2},{4,5},{5,4},{6,7},{7,6},{8,9},{9,8},{10,11... | collective-permute-start | bytes 3145736 | tf_op jit(solution)/shard_map/ppermute | solution.py:28
  89.3 8.1 %collective-permute-start.28 = (s16[144,1024]{1,0:T(8,128)(2,1)S(1)}, s16[144,1024]{1,0:T(8,128)(2,1)S(1)}, u32[]{:S(2)}, u32[]{:S(2)}) collective-permute-start(s16[144,1024]{1,0:T(8,128)(2,1)S(1)} %get-tuple-element.285), channel_id=1, source_target_pairs={{0,4},{4,8},{8,12},{12,0},{1,5},{5,9},{9,13},{13,1},{2,6},{6,10},{... | collective-permute-start | bytes 884744 | tf_op jit(solution)/shard_map/ppermute | solution.py:28
  89.3 25.2 %collective-permute-start.29 = (s16[144,1024]{1,0:T(8,128)(2,1)S(1)}, s16[144,1024]{1,0:T(8,128)(2,1)S(1)}, u32[]{:S(2)}, u32[]{:S(2)}) collective-permute-start(s16[144,1024]{1,0:T(8,128)(2,1)S(1)} %get-tuple-element.286), channel_id=1, source_target_pairs={{0,8},{4,12},{8,0},{12,4},{1,9},{5,13},{9,1},{13,5},{2,10},{6,14},... | collective-permute-start | bytes 884744 | tf_op jit(solution)/shard_map/ppermute | solution.py:28
  91.5 23.0 %collective-permute-start.30 = (s16[144,1024]{1,0:T(8,128)(2,1)S(1)}, s16[144,1024]{1,0:T(8,128)(2,1)S(1)}, u32[]{:S(2)}, u32[]{:S(2)}) collective-permute-start(s16[144,1024]{1,0:T(8,128)(2,1)S(1)} %get-tuple-element.287), channel_id=1, source_target_pairs={{0,12},{4,0},{8,4},{12,8},{1,13},{5,1},{9,5},{13,9},{2,14},{6,2},{... | collective-permute-start | bytes 884744 | tf_op jit(solution)/shard_map/ppermute | solution.py:28
  114.5 2.8 %copy-start.5 = (s32[1,2048]{1,0:T(1,128)S(1)}, s32[1,2048]{1,0:T(1,128)}, u32[]{:S(2)}) copy-start(s32[1,2048]{1,0:T(1,128)} %ids_ref.1) | copy-start | bytes 24580
  114.5 2.8 %copy-start.7 = (s32[2,512]{1,0:T(2,128)S(1)}, s32[2,512]{1,0:T(2,128)}, u32[]{:S(2)}) copy-start(s32[2,512]{1,0:T(2,128)} %refs_0_.1) | copy-start | bytes 12292
  114.5 2.8 %copy-start.10 = (s32[2,512]{1,0:T(2,128)S(1)}, s32[2,512]{1,0:T(2,128)}, u32[]{:S(2)}) copy-start(s32[2,512]{1,0:T(2,128)} %copy-done.9) | copy-start | bytes 12292

commit v5 on v4

--- a/solution.py
+++ b/solution.py
@@ -16,7 +16,7 @@
 ROOT_STEP = 0.02
 TINY = 1e-30
 REACH = 1e-6
-VMEM_LIMIT = 32 * 1024 * 1024
+VMEM_LIMIT = 24 * 1024 * 1024
 F32 = jnp.float32
 BF16 = jnp.bfloat16
 LARGE = pl.CostEstimate(flops=10**11, bytes_accessed=1024, transcendentals=0)
@@ -26,6 +26,16 @@
 def rotated(block, axis, shift):
     size = lax.axis_size(axis)
     return lax.ppermute(block, axis, [(i, (i + shift) % size) for i in range(size)])
+
+
+def shifts_of(axis):
+    size = lax.axis_size(axis)
+    return sorted(range(1, size), key=lambda s: -min(s, size - s))
+
+
+def sent_around(blocks):
+    moved = {s: rotated(blocks[s], "atoms", s) for s in shifts_of("atoms")}
+    return [blocks[0]] + [moved[s] for s in range(1, len(blocks))]
 
 
 def passed_down(block, axis):
@@ -76,9 +86,10 @@
 def first_pick_kernel(sides, place_ref, coords_ref, ids_ref, *refs):
     pairs, refs = refs[:sides], refs[sides:]
     chosen_ref, ids_out, pairs_out, refs = refs[0], refs[1], refs[2 : 2 + sides], refs[2 + sides :]
-    outs, rows_ref, sems = refs[:-2], refs[-2], refs[-1]
+    later_out, outs, rows_ref, sems = refs[0], refs[1:-2], refs[-2], refs[-1]
     width, cap = chosen_ref.shape
-    copies = start_rows((rows_ref.shape[2],), 0, place_ref, coords_ref, [rows_ref], sems)
+    sizes = (rows_ref.shape[2], later_out.shape[2])
+    copies = start_rows(sizes, 0, place_ref, coords_ref, [rows_ref, later_out], sems)
     ids_out[...] = ids_ref[...]
     for block, copy in zip(pairs, pairs_out):
         copy[...] = block[...]
@@ -91,10 +102,13 @@
     for s, out in enumerate(outs):
         copies[s].wait()
         pick_rows(rows_ref.at[s], chosen_ref[...], out)
-
-
-def first_pick(coords, ids, pairs, cap, place, size, groups):
+    for copy in copies[len(outs) :]:
+        copy.wait()
+
+
+def first_pick(coords, ids, pairs, cap, place, sizes, groups):
     width = coords.shape[2]
+    size, later = sizes
     vmem = pl.BlockSpec(memory_space=pltpu.VMEM)
     outs = pl.pallas_call(
         functools.partial(first_pick_kernel, len(pairs)),
@@ -103,54 +117,44 @@
             pl.BlockSpec(memory_space=pltpu.HBM),
         ]
         + [vmem] * (len(pairs) + 1),
-        out_specs=[vmem] * (2 + len(pairs) + groups),
+        out_specs=[vmem] * (3 + len(pairs) + groups),
         out_shape=[
             jax.ShapeDtypeStruct((width, cap), BF16),
             jax.ShapeDtypeStruct(ids.shape, ids.dtype),
         ]
         + [jax.ShapeDtypeStruct(block.shape, block.dtype) for block in pairs]
+        + [jax.ShapeDtypeStruct((groups, 3, later, width), BF16)]
         + [jax.ShapeDtypeStruct((size, packed(cap)), BF16)] * groups,
         scratch_shapes=[
             pltpu.VMEM((groups, 3, size, width), BF16),
-            pltpu.SemaphoreType.DMA((1, groups)),
+            pltpu.SemaphoreType.DMA((2, groups)),
         ],
         compiler_params=params(),
         cost_estimate=SMALL,
         name="first_pick",
     )(place, coords, ids, *pairs)
-    sides = len(pairs)
-    return outs[0], outs[1], outs[2 : 2 + sides], outs[2 + sides :]
-
-
-def pick_kernel(start, place_ref, coords_ref, chosen_ref, after_ref, *refs):
-    outs, rows_ref, sems = refs[:-2], refs[-2], refs[-1]
-    copies = start_rows((rows_ref.shape[2],), start, place_ref, coords_ref, [rows_ref], sems)
+    last = 2 + len(pairs)
+    return outs[0], outs[1], outs[2:last], outs[last], outs[last + 1 :]
+
+
+def pick_kernel(rows_ref, chosen_ref, after_ref, *outs):
     for s, out in enumerate(outs):
-        copies[s].wait()
         pick_rows(rows_ref.at[s], chosen_ref[...], out)
 
 
-def pick(coords, chosen, after, place, start, size, groups):
-    width, cap = chosen.shape
+def pick(rows, chosen, after):
+    groups, _, size, _ = rows.shape
+    cap = chosen.shape[1]
     vmem = pl.BlockSpec(memory_space=pltpu.VMEM)
     return pl.pallas_call(
-        functools.partial(pick_kernel, start),
-        in_specs=[
-            pl.BlockSpec(memory_space=pltpu.SMEM),
-            pl.BlockSpec(memory_space=pltpu.HBM),
-            vmem,
-            pl.BlockSpec(memory_space=pl.ANY),
-        ],
+        pick_kernel,
+        in_specs=[vmem, vmem, pl.BlockSpec(memory_space=pl.ANY)],
         out_specs=[vmem] * groups,
         out_shape=[jax.ShapeDtypeStruct((size, packed(cap)), BF16)] * groups,
-        scratch_shapes=[
-            pltpu.VMEM((groups, 3, size, width), BF16),
-            pltpu.SemaphoreType.DMA((1, groups)),
-        ],
         compiler_params=params(),
         cost_estimate=SMALL,
         name="pick",
-    )(place, coords, chosen, after)
+    )(rows, chosen, after)
 
 
 def coded(value, step):
@@ -744,17 +748,13 @@
     feats = cols * sides
     sizes = chunk_sizes(frames // sides)
 
-    chosen, traj_ids, pairs, picked = first_pick(
-        coords, traj_ids, pairs, cap, place, sizes[0], groups
+    chosen, traj_ids, pairs, later, picked = first_pick(
+        coords, traj_ids, pairs, cap, place, sizes, groups
     )
-    arrived, start = [], 0
-    for j, size in enumerate(sizes):
-        if j:
-            picked = pick(coords, chosen, arrived[-1][1], place, start, size, groups)
-        arrived.append([picked[0]] + [rotated(picked[s], "atoms", s) for s in range(1, groups)])
-        start += size
-
-    signs, most_used = pair_signs(pairs, arrived[0][0], place, groups, width, cap)
+    arrived = [sent_around(picked)]
+    signs, most_used = pair_signs(pairs, picked[0], place, groups, width, cap)
+    picked = pick(later, chosen, most_used)
+    arrived.append(sent_around(picked))
 
     ids = jnp.concatenate([traj_ids[0], jnp.full((LAG,), -1, jnp.int32)])
     offset = atom_index * frames
@@ -777,7 +777,7 @@
         halo = jnp.where(feat_index == s, sent, halo)
 
     reps = lax.axis_size("rep")
-    shifts = list(range(1, groups)) + [0]
+    shifts = shifts_of("atoms") + [0]
     shifts = tuple(shifts[: groups // 2]), tuple(shifts[groups // 2 :])
     before, own, shift, sums, tail = early_moments(own_pieces, valid, place, sides)
     parts, own, factors = late_moments(

time: 119 us -> 116 us (0.975)
  local copies, waits for them, and re-layouts: 2.18 us -> 0.2 us
  Pallas kernels: 31.5 us -> 30.2 us
    ppermute x15, waiting for transfers between devices: 60.5 us -> 67.1 us  [rotated(): lax.ppermute(block, axis, [(i, (i + shift) % size) for i in range(size)])]
    ppermute x1, waiting for transfers between devices: 6.4 us -> 0.01 us  [passed_down(): lax.ppermute(block, axis, [(i + 1, i) for i in range(lax.axis_size(axis)...]
    unnamed x22 -> x16, local copies, waits for them, and re-layouts: 2.02 us -> 0.04 us
    pallas_call x1, Pallas kernels: 2.8 us -> 1.15 us  [pick(): pl.pallas_call(pick_kernel, in_specs=[vmem, vmem, pl.BlockSpec(memory_spa...]
  transfers between devices with their start and end apart: 16 -> 16, of which waited for: 8 -> 9; matrix products, arithmetic and copies ran while one was open for 0% -> 0% of each run, Pallas kernels for 18% -> 17%
where the time goes in v5:
time: 116 us; the launch traced here: 115 us
  waiting for transfers between devices  67.1 us (58%)
  Pallas kernels  30.2 us (26%)
  starting transfers between devices  15.5 us (13%)
    ppermute x15, waiting for transfers between devices, rotated(): lax.ppermute(block, axis, [(i, (i + shift) % size) for i in range(size)])  67.1 us
    ppermute x15, starting transfers between devices, rotated(): lax.ppermute(block, axis, [(i, (i + shift) % size) for i in range(size)])  13.3 us
    pallas_call x1, Pallas kernels, pair_signs(): pl.pallas_call(functools.partial(signs_kernel, groups, width, cap), in_sp...  6.52 us
    pallas_call x1, Pallas kernels, first_pick(): pl.pallas_call(functools.partial(first_pick_kernel, len(pairs)), in_specs...  4.81 us
    pallas_call x2, Pallas kernels, distances(): pl.pallas_call(distance_kernel, in_specs=[vmem] * (len(blocks) + 1) + [pl...  3.86 us
    pallas_call x1, Pallas kernels, late_moments(): pl.pallas_call(functools.partial(late_kernel, sizes, sides, groups, reps,...  3.31 us
    pallas_call x1, Pallas kernels, finish(): pl.pallas_call(functools.partial(finish_kernel, reps), in_specs=[pl.Block...  2.84 us
    pallas_call x1, Pallas kernels, early_moments(): pl.pallas_call(functools.partial(early_kernel, len(pieces), sides), in_sp...  2.8 us
  transfers between devices with their start and end apart: 16, of which 9 were waited for; matrix products, arithmetic and copies ran while one was open for 0% of the time, Pallas kernels for 17%

profile of v5, /device:TPU:9, one launch (start us, length us, event | category | flops | bytes accessed | tf_op | source)
XLA Modules:
  0.0 114.5 jit_solution(10954130438963646208)
XLA Ops:
  0.6 1.3 %collective-permute-start.15 = (s32[2,512]{1,0:T(2,128)}, s32[2,512]{1,0:T(2,128)S(1)}, u32[]{:S(2)}, u32[]{:S(2)}) collective-permute-start(s32[2,512]{1,0:T(2,128)} %refs_0_.1), channel_id=1, source_target_pairs={{0,2},{2,0},{1,3},{3,1},{4,6},{6,4},{5,7},{7,5},{8,10},{10,8},{9,1... | collective-permute-start | bytes 12296 | tf_op jit(solution)/shard_map/ppermute | solution.py:28
  1.9 0.1 pad_add_fusion.place_ref
  2.0 1.4 %collective-permute-done.15.refs_1_ = s32[2,512]{1,0:T(2,128)S(1)} collective-permute-done((s32[2,512]{1,0:T(2,128)}, s32[2,512]{1,0:T(2,128)S(1)}, u32[]{:S(2)}, u32[]{:S(2)}) %collective-permute-start.15) | collective-permute-done | bytes 4128 | tf_op jit(solution)/shard_map/ppermute | solution.py:28
  3.4 4.8 %first_pick.5 = (bf16[768,426]{1,0:T(8,128)(2,1)S(1)}, s32[1,2048]{1,0:T(1,128)S(1)}, s32[2,512]{1,0:T(2,128)S(1)}, s32[2,512]{1,0:T(2,128)S(1)}, bf16[4,3,96,76...) custom-call(s32[3]{0:T(128)S(1)} %pad_add_fusion.place_ref, ...), custom_call_target="tpu_custom_call" | custom-call | flops 1024 | bytes 1024 | tf_op jit(solution)/shard_map/first_pick/pallas_call | solution.py:113
  8.2 1.4 %collective-permute-start.16 = (bf16[160,1280]{1,0:T(8,128)(2,1)S(1)}, bf16[160,1280]{1,0:T(8,128)(2,1)S(1)}, u32[]{:S(2)}, u32[]{:S(2)}) collective-permute-start(bf16[160,1280]{1,0:T(8,128)(2,1)S(1)} %get-tuple-element.258), channel_id=1, source_target_pairs={{0,4},{4,8},{8,12},{12,0},{1,5},{5,9},{9,13},{13,1},{2,6},{6,10},{... | collective-permute-start | bytes 1228808 | tf_op jit(solution)/shard_map/ppermute | solution.py:28
  9.5 1.1 collective-permute-start.17
  10.6 1.4 %collective-permute-start.18 = (bf16[160,1280]{1,0:T(8,128)(2,1)S(1)}, bf16[160,1280]{1,0:T(8,128)(2,1)S(1)}, u32[]{:S(2)}, u32[]{:S(2)}) collective-permute-start(bf16[160,1280]{1,0:T(8,128)(2,1)S(1)} %get-tuple-element.260), channel_id=1, source_target_pairs={{0,12},{4,0},{8,4},{12,8},{1,13},{5,1},{9,5},{13,9},{2,14},{6,2},{... | collective-permute-start | bytes 1228808 | tf_op jit(solution)/shard_map/ppermute | solution.py:28
  12.0 6.5 %pair_signs.5 = (bf16[1704,1024]{1,0:T(8,128)(2,1)S(1)}, f32[1,128]{1,0:T(1,128)S(1)}) custom-call(s32[3]{0:T(128)S(1)} %pad_add_fusion.place_ref, bf16[160,1280]{1,0:T(8,128)(2,1)S(1)} %get-tuple-element.254.after_ref.refs_0_, s32[2,512]{1,0:T(2,128)S(1)} %get-tuple-element.255.refs_0_, s32[2,512]{1,0:T(2,128)S(1)} %get-tuple-element.256.refs_1_), custom_call_target="tpu_custom_call" | custom-call | flops 99999997952 | bytes 1024 | tf_op jit(solution)/shard_map/pair_signs/pallas_call | solution.py:722
  18.6 0.0 copy-start
  18.6 1.2 %pick.5 = (bf16[96,1280]{1,0:T(8,128)(2,1)S(1)}, bf16[96,1280]{1,0:T(8,128)(2,1)S(1)}, bf16[96,1280]{1,0:T(8,128)(2,1)S(1)}, bf16[96,1280]{1,0:T(8,128)(2,1)S(1)}) custom-call(bf16[4,3,96,768]{3,2,1,0:T(8,128)(2,1)S(1)} %get-tuple-element.262.rows_ref, bf16[768,426]{1,0:T(8,128)(2,1)S(1)} %get-tuple-element.263.chosen_ref, ...), custom_call_target="tpu_custom_call" | custom-call | flops 1024 | bytes 1024 | tf_op jit(solution)/shard_map/pick/pallas_call | solution.py:149
  19.7 0.1 collective-permute-start.20
  19.8 3.1 %collective-permute-start.21 = (bf16[96,1280]{1,0:T(8,128)(2,1)S(1)}, bf16[96,1280]{1,0:T(8,128)(2,1)S(1)}, u32[]{:S(2)}, u32[]{:S(2)}) collective-permute-start(bf16[96,1280]{1,0:T(8,128)(2,1)S(1)} %get-tuple-element.267), channel_id=1, source_target_pairs={{0,8},{4,12},{8,0},{12,4},{1,9},{5,13},{9,1},{13,5},{2,10},{6,14},... | collective-permute-start | bytes 737288 | tf_op jit(solution)/shard_map/ppermute | solution.py:28
  22.9 0.0 collective-permute-done.16.refs_1_
  22.9 0.0 collective-permute-start.22
  22.9 30.4 %collective-permute-done.17.refs_2_ = bf16[160,1280]{1,0:T(8,128)(2,1)S(1)} collective-permute-done((bf16[160,1280]{1,0:T(8,128)(2,1)S(1)}, bf16[160,1280]{1,0:T(8,128)(2,1)S(1)}, u32[]{:S(2)}, u32[]{:S(2)}) %collective-permute-start.17) | collective-permute-done | bytes 409632 | tf_op jit(solution)/shard_map/ppermute | solution.py:28
  53.3 4.1 %collective-permute-done.18.refs_3_ = bf16[160,1280]{1,0:T(8,128)(2,1)S(1)} collective-permute-done((bf16[160,1280]{1,0:T(8,128)(2,1)S(1)}, bf16[160,1280]{1,0:T(8,128)(2,1)S(1)}, u32[]{:S(2)}, u32[]{:S(2)}) %collective-permute-start.18) | collective-permute-done | bytes 409632 | tf_op jit(solution)/shard_map/ppermute | solution.py:28
  57.4 2.3 %distances.10 = (f32[160,1024]{1,0:T(8,128)S(1)}, s16[176,1024]{1,0:T(8,128)(2,1)S(1)}) custom-call(bf16[160,1280]{1,0:T(8,128)(2,1)S(1)} %get-tuple-element.254.after_ref.refs_0_, bf16[160,1280]{1,0:T(8,128)(2,1)S(1)} %collective-permute-done.16.refs_1_, bf16[160,1280]{1,0:T(8,128)(2,1)S(1)} %collective-permute-done.17.refs_2_, ...), custom_call_target="tpu_custom_call" | custom-call | flops 99999997952 | bytes 1024 | tf_op jit(solution)/shard_map/distances/pallas_call | solution.py:206
  59.8 1.3 %collective-permute-start.19 = (s16[176,1024]{1,0:T(8,128)(2,1)S(1)}, s16[176,1024]{1,0:T(8,128)(2,1)S(1)}, u32[]{:S(2)}, u32[]{:S(2)}) collective-permute-start(s16[176,1024]{1,0:T(8,128)(2,1)S(1)} %get-tuple-element.265), channel_id=1, source_target_pairs={{0,2},{2,0},{1,3},{3,1},{4,6},{6,4},{5,7},{7,5},{8,10},{10,8},{9,1... | collective-permute-start | bytes 1081352 | tf_op jit(solution)/shard_map/ppermute | solution.py:28
  61.1 2.2 %collective-permute-start.24 = (f32[16,1024]{1,0:T(8,128)S(1)}, f32[16,1024]{1,0:T(8,128)S(1)}, u32[]{:S(2)}, u32[]{:S(2)}) collective-permute-start(f32[16,1024]{1,0:T(8,128)S(1)} %slice.13), channel_id=1, source_target_pairs={{4,0},{8,4},{12,8},{5,1},{9,5},{13,9},{6,2},{10,6},{14,10},{7,3},{... | collective-permute-start | bytes 196616 | tf_op jit(solution)/shard_map/ppermute | solution.py:42
  63.3 0.0 collective-permute-done.20.refs_1_
  63.3 0.6 collective-permute-done.21.refs_2_
  63.9 4.1 %collective-permute-done.22.refs_3_ = bf16[96,1280]{1,0:T(8,128)(2,1)S(1)} collective-permute-done((bf16[96,1280]{1,0:T(8,128)(2,1)S(1)}, bf16[96,1280]{1,0:T(8,128)(2,1)S(1)}, u32[]{:S(2)}, u32[]{:S(2)}) %collective-permute-start.22) | collective-permute-done | bytes 245792 | tf_op jit(solution)/shard_map/ppermute | solution.py:28
  68.0 1.5 %distances.11 = (f32[96,1024]{1,0:T(8,128)S(1)}, s16[112,1024]{1,0:T(8,128)(2,1)S(1)}) custom-call(bf16[96,1280]{1,0:T(8,128)(2,1)S(1)} %get-tuple-element.264.refs_5_.refs_0_, bf16[96,1280]{1,0:T(8,128)(2,1)S(1)} %collective-permute-done.20.refs_1_, bf16[96,1280]{1,0:T(8,128)(2,1)S(1)} %collective-permute-done.21.refs_2_, ...), custom_call_target="tpu_custom_call" | custom-call | flops 99999997952 | bytes 1024 | tf_op jit(solution)/shard_map/distances/pallas_call | solution.py:206
  69.5 1.3 %collective-permute-start.23 = (s16[112,1024]{1,0:T(8,128)(2,1)S(1)}, s16[112,1024]{1,0:T(8,128)(2,1)S(1)}, u32[]{:S(2)}, u32[]{:S(2)}) collective-permute-start(s16[112,1024]{1,0:T(8,128)(2,1)S(1)} %get-tuple-element.270), channel_id=1, source_target_pairs={{0,2},{2,0},{1,3},{3,1},{4,6},{6,4},{5,7},{7,5},{8,10},{10,8},{9,1... | collective-permute-start | bytes 688136 | tf_op jit(solution)/shard_map/ppermute | solution.py:28
  70.8 0.3 collective-permute-start.25
  71.0 0.1 fusion.3
  71.1 0.2 copy.8.refs_2_.refs_8_
  71.3 2.8 %early_moments.5 = (f32[1024,1024]{1,0:T(8,128)S(1)}, f32[256,512]{1,0:T(8,128)S(1)}, f32[1,1024]{1,0:T(1,128)S(1)}, f32[4,1024]{1,0:T(4,128)S(1)}, f32[16,1024]{1,0:T(8,128)S(1)}) custom-call(s32[3]{0:T(128)S(1)} %copy-done.3, f32[160,1024]{1,0:T(8,128)S(1)} %get-tuple-element.269.refs_5_.refs_0_, f32[96,1024]{1,0:T(8,128)S(1)} %get-tuple-element.271.refs_1_, ...), custom_call_target="tpu_custom_call" | custom-call | flops 1024 | bytes 1024 | tf_op jit(solution)/shard_map/early_moments/pallas_call | solution.py:285
  74.1 2.7 %collective-permute-done.25 = f32[16,512]{1,0:T(8,128)S(1)} collective-permute-done((f32[16,512]{1,0:T(8,128)S(1)}, f32[16,512]{1,0:T(8,128)S(1)}, u32[]{:S(2)}, u32[]{:S(2)}) %collective-permute-start.25) | collective-permute-done | bytes 32800 | tf_op jit(solution)/shard_map/ppermute | solution.py:28
  76.9 0.0 collective-permute-done.23.refs_1_
  76.9 3.3 %late_moments.5 = (f32[264,1024]{1,0:T(8,128)S(1)}, f32[264,1024]{1,0:T(8,128)S(1)}, f32[512,512]{1,0:T(8,128)S(1)}, bf16[1024,288]{1,0:T(8,128)(2,1)S(1)}, bf16...) custom-call(s32[3]{0:T(128)S(1)} %copy-done.3, ...), custom_call_target="tpu_custom_call" | custom-call | flops 1024 | bytes 1024 | tf_op jit(solution)/shard_map/late_moments/pallas_call | solution.py:418
  80.2 1.5 %collective-permute-start.26 = (f32[264,1024]{1,0:T(8,128)S(1)}, f32[264,1024]{1,0:T(8,128)S(1)}, u32[]{:S(2)}, u32[]{:S(2)}) collective-permute-start(f32[264,1024]{1,0:T(8,128)S(1)} %get-tuple-element.279), channel_id=1, source_target_pairs={{0,1},{1,0},{2,3},{3,2},{4,5},{5,4},{6,7},{7,6},{8,9},{9,8},{10,11... | collective-permute-start | bytes 3244040 | tf_op jit(solution)/shard_map/ppermute | solution.py:28
  81.7 2.3 %rest_moments.5 = (f32[256,1024]{1,0:T(8,128)S(1)}, f32[256,1024]{1,0:T(8,128)S(1)}) custom-call(s32[3]{0:T(128)S(1)} %copy-done.3, f32[1024,1024]{1,0:T(8,128)S(1)} %get-tuple-element.273.refs_2_.before_ref, bf16[1024,288]{1,0:T(8,128)(2,1)S(1)} %get-tuple-element.282.left_high, bf16[1024,288]{1,0:T(8,128)(2,1)S(1)} %get-tuple-element.283.left_low, ...), custom_call_target="tpu_custom_call" | custom-call | flops 1024 | bytes 1024 | tf_op jit(solution)/shard_map/rest_moments/pallas_call | solution.py:451
  84.0 0.1 collective-permute-start.27
  84.1 0.0 copy-start.1
  84.1 1.5 %first_share.5 = (s16[144,1024]{1,0:T(8,128)(2,1)S(1)}, s16[144,1024]{1,0:T(8,128)(2,1)S(1)}, s16[16,1024]{1,0:T(8,128)(2,1)S(1)}, f32[8,1024]{1,0:T(8,128)S(1)}) custom-call(s32[3]{0:T(128)S(1)} %copy-done.3, f32[264,1024]{1,0:T(8,128)S(1)} %get-tuple-element.278.refs_0_, f32[264,1024]{1,0:T(8,128)S(1)} %collective-permute-done.26.refs_1_), custom_call_target="tpu_custom_call" | custom-call | flops 1024 | bytes 1024 | tf_op jit(solution)/shard_map/first_share/pallas_call | solution.py:546
  85.6 0.1 collective-permute-start.28
  85.7 0.1 collective-permute-start.29
  85.8 1.0 collective-permute-done.27.refs_1_
  86.8 1.1 rest_share.5
  87.9 0.0 copy-start.5
  87.9 0.0 copy-start.7
  87.9 0.5 collective-permute-start.30
  88.5 10.2 %collective-permute-done.28.refs_0_ = s16[144,1024]{1,0:T(8,128)(2,1)S(1)} collective-permute-done((s16[144,1024]{1,0:T(8,128)(2,1)S(1)}, s16[144,1024]{1,0:T(8,128)(2,1)S(1)}, u32[]{:S(2)}, u32[]{:S(2)}) %collective-permute-start.28) | collective-permute-done | bytes 294944 | tf_op jit(solution)/shard_map/ppermute | solution.py:28
  98.6 12.6 %collective-permute-done.29.refs_1_ = s16[144,1024]{1,0:T(8,128)(2,1)S(1)} collective-permute-done((s16[144,1024]{1,0:T(8,128)(2,1)S(1)}, s16[144,1024]{1,0:T(8,128)(2,1)S(1)}, u32[]{:S(2)}, u32[]{:S(2)}) %collective-permute-start.29) | collective-permute-done | bytes 294944 | tf_op jit(solution)/shard_map/ppermute | solution.py:28
  111.3 0.0 collective-permute-done.30.refs_2_
  111.3 2.8 %finish.5 = (f32[128,512]{1,0:T(8,128)}, f32[128,512]{1,0:T(8,128)}, f32[512,512]{1,0:T(8,128)}) custom-call(s32[3]{0:T(128)S(1)} %copy-done.3, f32[128,1024]{1,0:T(8,128)S(1)} %get-tuple-element.288.kept_ref, s16[16,1024]{1,0:T(8,128)(2,1)S(1)} %get-tuple-element.281.codes_ref, s16[144,1024]{1,0:T(8,128)(2,1)S(1)} %collective-permute-done.28.refs_0_, ...), custom_call_target="tpu_custom_call" | custom-call | flops 1024 | bytes 1024 | tf_op jit(solution)/shard_map/finish/pallas_call | solution.py:657
  114.1 0.2 while.16
  (18 shorter events, 0.0 us)
Async XLA Ops:
  0.6 2.7 %collective-permute-start.15 = (s32[2,512]{1,0:T(2,128)}, s32[2,512]{1,0:T(2,128)S(1)}, u32[]{:S(2)}, u32[]{:S(2)}) collective-permute-start(s32[2,512]{1,0:T(2,128)} %refs_0_.1), channel_id=1, source_target_pairs={{0,2},{2,0},{1,3},{3,1},{4,6},{6,4},{5,7},{7,5},{8,10},{10,8},{9,1... | collective-permute-start | bytes 12296 | tf_op jit(solution)/shard_map/ppermute | solution.py:28
  2.0 10.0 %copy-start.2 = (s32[3]{0:T(128)}, s32[3]{0:T(128)S(1)}, u32[]{:S(2)}) copy-start(s32[3]{0:T(128)S(1)} %pad_add_fusion.place_ref) | copy-start | bytes 40
  3.4 4.8 %copy-start.9 = (s32[2,512]{1,0:T(2,128)}, s32[2,512]{1,0:T(2,128)S(1)}, u32[]{:S(2)}) copy-start(s32[2,512]{1,0:T(2,128)S(1)} %collective-permute-done.15.refs_1_) | copy-start | bytes 12292
  8.2 14.7 %collective-permute-start.16 = (bf16[160,1280]{1,0:T(8,128)(2,1)S(1)}, bf16[160,1280]{1,0:T(8,128)(2,1)S(1)}, u32[]{:S(2)}, u32[]{:S(2)}) collective-permute-start(bf16[160,1280]{1,0:T(8,128)(2,1)S(1)} %get-tuple-element.258), channel_id=1, source_target_pairs={{0,4},{4,8},{8,12},{12,0},{1,5},{5,9},{9,13},{13,1},{2,6},{6,10},{... | collective-permute-start | bytes 1228808 | tf_op jit(solution)/shard_map/ppermute | solution.py:28
  9.5 43.8 %collective-permute-start.17 = (bf16[160,1280]{1,0:T(8,128)(2,1)S(1)}, bf16[160,1280]{1,0:T(8,128)(2,1)S(1)}, u32[]{:S(2)}, u32[]{:S(2)}) collective-permute-start(bf16[160,1280]{1,0:T(8,128)(2,1)S(1)} %get-tuple-element.259), channel_id=1, source_target_pairs={{0,8},{4,12},{8,0},{12,4},{1,9},{5,13},{9,1},{13,5},{2,10},{6,14},... | collective-permute-start | bytes 1228808 | tf_op jit(solution)/shard_map/ppermute | solution.py:28
  10.6 46.8 %collective-permute-start.18 = (bf16[160,1280]{1,0:T(8,128)(2,1)S(1)}, bf16[160,1280]{1,0:T(8,128)(2,1)S(1)}, u32[]{:S(2)}, u32[]{:S(2)}) collective-permute-start(bf16[160,1280]{1,0:T(8,128)(2,1)S(1)} %get-tuple-element.260), channel_id=1, source_target_pairs={{0,12},{4,0},{8,4},{12,8},{1,13},{5,1},{9,5},{13,9},{2,14},{6,2},{... | collective-permute-start | bytes 1228808 | tf_op jit(solution)/shard_map/ppermute | solution.py:28
  18.6 38.9 %copy-start = (f32[1,128]{1,0:T(1,128)}, f32[1,128]{1,0:T(1,128)S(1)}, u32[]{:S(2)}) copy-start(f32[1,128]{1,0:T(1,128)S(1)} %get-tuple-element.257.after_ref) | copy-start | bytes 1540
  19.7 43.6 %collective-permute-start.20 = (bf16[96,1280]{1,0:T(8,128)(2,1)S(1)}, bf16[96,1280]{1,0:T(8,128)(2,1)S(1)}, u32[]{:S(2)}, u32[]{:S(2)}) collective-permute-start(bf16[96,1280]{1,0:T(8,128)(2,1)S(1)} %get-tuple-element.266), channel_id=1, source_target_pairs={{0,4},{4,8},{8,12},{12,0},{1,5},{5,9},{9,13},{13,1},{2,6},{6,10},{... | collective-permute-start | bytes 737288 | tf_op jit(solution)/shard_map/ppermute | solution.py:28
  19.8 44.0 %collective-permute-start.21 = (bf16[96,1280]{1,0:T(8,128)(2,1)S(1)}, bf16[96,1280]{1,0:T(8,128)(2,1)S(1)}, u32[]{:S(2)}, u32[]{:S(2)}) collective-permute-start(bf16[96,1280]{1,0:T(8,128)(2,1)S(1)} %get-tuple-element.267), channel_id=1, source_target_pairs={{0,8},{4,12},{8,0},{12,4},{1,9},{5,13},{9,1},{13,5},{2,10},{6,14},... | collective-permute-start | bytes 737288 | tf_op jit(solution)/shard_map/ppermute | solution.py:28
  22.9 45.0 %collective-permute-start.22 = (bf16[96,1280]{1,0:T(8,128)(2,1)S(1)}, bf16[96,1280]{1,0:T(8,128)(2,1)S(1)}, u32[]{:S(2)}, u32[]{:S(2)}) collective-permute-start(bf16[96,1280]{1,0:T(8,128)(2,1)S(1)} %get-tuple-element.268), channel_id=1, source_target_pairs={{0,12},{4,0},{8,4},{12,8},{1,13},{5,1},{9,5},{13,9},{2,14},{6,2},{... | collective-permute-start | bytes 737288 | tf_op jit(solution)/shard_map/ppermute | solution.py:28
  59.8 17.1 %collective-permute-start.19 = (s16[176,1024]{1,0:T(8,128)(2,1)S(1)}, s16[176,1024]{1,0:T(8,128)(2,1)S(1)}, u32[]{:S(2)}, u32[]{:S(2)}) collective-permute-start(s16[176,1024]{1,0:T(8,128)(2,1)S(1)} %get-tuple-element.265), channel_id=1, source_target_pairs={{0,2},{2,0},{1,3},{3,1},{4,6},{6,4},{5,7},{7,5},{8,10},{10,8},{9,1... | collective-permute-start | bytes 1081352 | tf_op jit(solution)/shard_map/ppermute | solution.py:28
  61.1 10.2 %copy-start.3 = (s32[3]{0:T(128)S(1)}, s32[3]{0:T(128)}, u32[]{:S(2)}) copy-start(s32[3]{0:T(128)} %copy-done.2) | copy-start | bytes 40
  61.1 9.7 %collective-permute-start.24 = (f32[16,1024]{1,0:T(8,128)S(1)}, f32[16,1024]{1,0:T(8,128)S(1)}, u32[]{:S(2)}, u32[]{:S(2)}) collective-permute-start(f32[16,1024]{1,0:T(8,128)S(1)} %slice.13), channel_id=1, source_target_pairs={{4,0},{8,4},{12,8},{5,1},{9,5},{13,9},{6,2},{10,6},{14,10},{7,3},{... | collective-permute-start | bytes 196616 | tf_op jit(solution)/shard_map/ppermute | solution.py:42
  69.5 7.3 %collective-permute-start.23 = (s16[112,1024]{1,0:T(8,128)(2,1)S(1)}, s16[112,1024]{1,0:T(8,128)(2,1)S(1)}, u32[]{:S(2)}, u32[]{:S(2)}) collective-permute-start(s16[112,1024]{1,0:T(8,128)(2,1)S(1)} %get-tuple-element.270), channel_id=1, source_target_pairs={{0,2},{2,0},{1,3},{3,1},{4,6},{6,4},{5,7},{7,5},{8,10},{10,8},{9,1... | collective-permute-start | bytes 688136 | tf_op jit(solution)/shard_map/ppermute | solution.py:28
  70.8 6.1 %collective-permute-start.25 = (f32[16,512]{1,0:T(8,128)S(1)}, f32[16,512]{1,0:T(8,128)S(1)}, u32[]{:S(2)}, u32[]{:S(2)}) collective-permute-start(f32[16,512]{1,0:T(8,128)S(1)} %constant_dynamic-slice_fusion.1), channel_id=1, source_target_pairs={{0,2},{2,0},{1,3},{3,1},{4,6},{6,4},{5,7},{7,5},{8,10},{10,8},{9,1... | collective-permute-start | bytes 98312 | tf_op jit(solution)/shard_map/ppermute | solution.py:28
  80.2 3.9 %collective-permute-start.26 = (f32[264,1024]{1,0:T(8,128)S(1)}, f32[264,1024]{1,0:T(8,128)S(1)}, u32[]{:S(2)}, u32[]{:S(2)}) collective-permute-start(f32[264,1024]{1,0:T(8,128)S(1)} %get-tuple-element.279), channel_id=1, source_target_pairs={{0,1},{1,0},{2,3},{3,2},{4,5},{5,4},{6,7},{7,6},{8,9},{9,8},{10,11... | collective-permute-start | bytes 3244040 | tf_op jit(solution)/shard_map/ppermute | solution.py:28
  84.0 2.7 %collective-permute-start.27 = (f32[256,1024]{1,0:T(8,128)S(1)}, f32[256,1024]{1,0:T(8,128)S(1)}, u32[]{:S(2)}, u32[]{:S(2)}) collective-permute-start(f32[256,1024]{1,0:T(8,128)S(1)} %get-tuple-element.287), channel_id=1, source_target_pairs={{0,1},{1,0},{2,3},{3,2},{4,5},{5,4},{6,7},{7,6},{8,9},{9,8},{10,11... | collective-permute-start | bytes 3145736 | tf_op jit(solution)/shard_map/ppermute | solution.py:28
  84.1 4.3 %copy-start.1 = (f32[1,128]{1,0:T(1,128)S(1)}, f32[1,128]{1,0:T(1,128)}, u32[]{:S(2)}) copy-start(f32[1,128]{1,0:T(1,128)} %copy-done) | copy-start | bytes 1540
  85.6 13.0 %collective-permute-start.28 = (s16[144,1024]{1,0:T(8,128)(2,1)S(1)}, s16[144,1024]{1,0:T(8,128)(2,1)S(1)}, u32[]{:S(2)}, u32[]{:S(2)}) collective-permute-start(s16[144,1024]{1,0:T(8,128)(2,1)S(1)} %get-tuple-element.289), channel_id=1, source_target_pairs={{0,8},{4,12},{8,0},{12,4},{1,9},{5,13},{9,1},{13,5},{2,10},{6,14},... | collective-permute-start | bytes 884744 | tf_op jit(solution)/shard_map/ppermute | solution.py:28
  85.7 25.6 %collective-permute-start.29 = (s16[144,1024]{1,0:T(8,128)(2,1)S(1)}, s16[144,1024]{1,0:T(8,128)(2,1)S(1)}, u32[]{:S(2)}, u32[]{:S(2)}) collective-permute-start(s16[144,1024]{1,0:T(8,128)(2,1)S(1)} %get-tuple-element.290), channel_id=1, source_target_pairs={{0,4},{4,8},{8,12},{12,0},{1,5},{5,9},{9,13},{13,1},{2,6},{6,10},{... | collective-permute-start | bytes 884744 | tf_op jit(solution)/shard_map/ppermute | solution.py:28
  87.9 26.2 %copy-start.5 = (s32[1,2048]{1,0:T(1,128)S(1)}, s32[1,2048]{1,0:T(1,128)}, u32[]{:S(2)}) copy-start(s32[1,2048]{1,0:T(1,128)} %ids_ref.1) | copy-start | bytes 24580
  87.9 26.2 %copy-start.7 = (s32[2,512]{1,0:T(2,128)S(1)}, s32[2,512]{1,0:T(2,128)}, u32[]{:S(2)}) copy-start(s32[2,512]{1,0:T(2,128)} %refs_0_.1) | copy-start | bytes 12292
  87.9 26.2 %copy-start.10 = (s32[2,512]{1,0:T(2,128)S(1)}, s32[2,512]{1,0:T(2,128)}, u32[]{:S(2)}) copy-start(s32[2,512]{1,0:T(2,128)} %copy-done.9) | copy-start | bytes 12292
  87.9 23.3 %collective-permute-start.30 = (s16[144,1024]{1,0:T(8,128)(2,1)S(1)}, s16[144,1024]{1,0:T(8,128)(2,1)S(1)}, u32[]{:S(2)}, u32[]{:S(2)}) collective-permute-start(s16[144,1024]{1,0:T(8,128)(2,1)S(1)} %get-tuple-element.291), channel_id=1, source_target_pairs={{0,12},{4,0},{8,4},{12,8},{1,13},{5,1},{9,5},{13,9},{2,14},{6,2},{... | collective-permute-start | bytes 884744 | tf_op jit(solution)/shard_map/ppermute | solution.py:28

commit v6 on v5

--- a/solution.py
+++ b/solution.py
@@ -16,7 +16,7 @@
 ROOT_STEP = 0.02
 TINY = 1e-30
 REACH = 1e-6
-VMEM_LIMIT = 24 * 1024 * 1024
+VMEM_LIMIT = 20 * 1024 * 1024
 F32 = jnp.float32
 BF16 = jnp.bfloat16
 LARGE = pl.CostEstimate(flops=10**11, bytes_accessed=1024, transcendentals=0)
@@ -33,11 +33,6 @@
     return sorted(range(1, size), key=lambda s: -min(s, size - s))
 
 
-def sent_around(blocks):
-    moved = {s: rotated(blocks[s], "atoms", s) for s in shifts_of("atoms")}
-    return [blocks[0]] + [moved[s] for s in range(1, len(blocks))]
-
-
 def passed_down(block, axis):
     return lax.ppermute(block, axis, [(i + 1, i) for i in range(lax.axis_size(axis) - 1)])
 
@@ -46,29 +41,27 @@
     return pltpu.CompilerParams(vmem_limit_bytes=VMEM_LIMIT)
 
 
-def start_rows(sizes, start, place_ref, coords_ref, rows_refs, sems):
-    groups, sides = rows_refs[0].shape[0], lax.axis_size("feat")
+def start_rows(shifts, start, place_ref, coords_ref, rows_ref, sems):
+    groups, sides = lax.axis_size("atoms"), lax.axis_size("feat")
     frames = coords_ref.shape[1] // groups
     copies = []
-    for j, size in enumerate(sizes):
-        for s in range(groups):
-            there = lax.rem(place_ref[0] + s, groups)
-            row = there * frames + place_ref[1] * (frames // sides) + start
-            copies.append(
-                pltpu.make_async_copy(
-                    coords_ref.at[:, pl.ds(pl.multiple_of(row, HALO), size), :],
-                    rows_refs[j].at[s],
-                    sems.at[j, s],
-                )
-            )
-        start += size
-    for copy in copies:
-        copy.start()
+    for i, s in enumerate(shifts):
+        there = lax.rem(place_ref[0] + s, groups)
+        row = there * frames + place_ref[1] * (frames // sides) + start
+        rows = pl.ds(pl.multiple_of(row, HALO), rows_ref.shape[2])
+        copies.append(
+            pltpu.make_async_copy(coords_ref.at[:, rows, :], rows_ref.at[i], sems.at[i])
+        )
+        copies[-1].start()
     return copies
 
 
 def packed(cap):
     return -(-3 * cap // 128) * 128
+
+
+def slot_rows(cap):
+    return -(-cap // HALO) * HALO
 
 
 def pick_rows(rows, chosen, out):
@@ -83,13 +76,15 @@
         out[:, 3 * cap :] = jnp.zeros((size, out.shape[1] - 3 * cap), BF16)
 
 
-def first_pick_kernel(sides, place_ref, coords_ref, ids_ref, *refs):
+def first_pick_kernel(sides, near, far, place_ref, coords_ref, ids_ref, *refs):
     pairs, refs = refs[:sides], refs[sides:]
     chosen_ref, ids_out, pairs_out, refs = refs[0], refs[1], refs[2 : 2 + sides], refs[2 + sides :]
-    later_out, outs, rows_ref, sems = refs[0], refs[1:-2], refs[-2], refs[-1]
+    near_out, later_out, out, rows_ref, sems = refs
     width, cap = chosen_ref.shape
-    sizes = (rows_ref.shape[2], later_out.shape[2])
-    copies = start_rows(sizes, 0, place_ref, coords_ref, [rows_ref, later_out], sems)
+    size = rows_ref.shape[2]
+    first = start_rows([far], 0, place_ref, coords_ref, rows_ref, sems.at[0])
+    others = start_rows(near + [0], 0, place_ref, coords_ref, near_out, sems.at[1])
+    others += start_rows([far] + near + [0], size, place_ref, coords_ref, later_out, sems.at[2])
     ids_out[...] = ids_ref[...]
     for block, copy in zip(pairs, pairs_out):
         copy[...] = block[...]
@@ -99,62 +94,70 @@
         some = min(128, cap - l)
         here = (rank == (lanes + l).astype(F32)).astype(F32).astype(BF16)
         chosen_ref[:, l : l + some] = here[:, :some]
-    for s, out in enumerate(outs):
-        copies[s].wait()
-        pick_rows(rows_ref.at[s], chosen_ref[...], out)
-    for copy in copies[len(outs) :]:
+    first[0].wait()
+    pick_rows(rows_ref.at[0], chosen_ref[...], out)
+    for copy in others:
         copy.wait()
 
 
-def first_pick(coords, ids, pairs, cap, place, sizes, groups):
+def first_pick(coords, ids, pairs, cap, place, sizes, near, far):
     width = coords.shape[2]
     size, later = sizes
     vmem = pl.BlockSpec(memory_space=pltpu.VMEM)
     outs = pl.pallas_call(
-        functools.partial(first_pick_kernel, len(pairs)),
+        functools.partial(first_pick_kernel, len(pairs), near, far),
         in_specs=[
             pl.BlockSpec(memory_space=pltpu.SMEM),
             pl.BlockSpec(memory_space=pltpu.HBM),
         ]
         + [vmem] * (len(pairs) + 1),
-        out_specs=[vmem] * (3 + len(pairs) + groups),
+        out_specs=[vmem] * (5 + len(pairs)),
         out_shape=[
             jax.ShapeDtypeStruct((width, cap), BF16),
             jax.ShapeDtypeStruct(ids.shape, ids.dtype),
         ]
         + [jax.ShapeDtypeStruct(block.shape, block.dtype) for block in pairs]
-        + [jax.ShapeDtypeStruct((groups, 3, later, width), BF16)]
-        + [jax.ShapeDtypeStruct((size, packed(cap)), BF16)] * groups,
+        + [
+            jax.ShapeDtypeStruct((len(near) + 1, 3, size, width), BF16),
+            jax.ShapeDtypeStruct((len(near) + 2, 3, later, width), BF16),
+            jax.ShapeDtypeStruct((size, packed(cap)), BF16),
+        ],
         scratch_shapes=[
-            pltpu.VMEM((groups, 3, size, width), BF16),
-            pltpu.SemaphoreType.DMA((2, groups)),
+            pltpu.VMEM((1, 3, size, width), BF16),
+            pltpu.SemaphoreType.DMA((3, len(near) + 2)),
         ],
         compiler_params=params(),
         cost_estimate=SMALL,
         name="first_pick",
     )(place, coords, ids, *pairs)
     last = 2 + len(pairs)
-    return outs[0], outs[1], outs[2:last], outs[last], outs[last + 1 :]
-
-
-def pick_kernel(rows_ref, chosen_ref, after_ref, *outs):
-    for s, out in enumerate(outs):
-        pick_rows(rows_ref.at[s], chosen_ref[...], out)
+    return outs[0], outs[1], outs[2:last], outs[last], outs[last + 1], outs[last + 2]
+
+
+def pick_kernel(counts, chosen_ref, after_ref, *refs):
+    rows_refs, outs = refs[: len(counts)], list(refs[len(counts) :])
+    for rows_ref, count in zip(rows_refs, counts):
+        for i in range(count):
+            pick_rows(rows_ref.at[i], chosen_ref[...], outs.pop(0))
 
 
 def pick(rows, chosen, after):
-    groups, _, size, _ = rows.shape
     cap = chosen.shape[1]
+    counts = [some.shape[0] for some in rows]
     vmem = pl.BlockSpec(memory_space=pltpu.VMEM)
     return pl.pallas_call(
-        pick_kernel,
-        in_specs=[vmem, vmem, pl.BlockSpec(memory_space=pl.ANY)],
-        out_specs=[vmem] * groups,
-        out_shape=[jax.ShapeDtypeStruct((size, packed(cap)), BF16)] * groups,
+        functools.partial(pick_kernel, counts),
+        in_specs=[vmem, pl.BlockSpec(memory_space=pl.ANY)] + [vmem] * len(rows),
+        out_specs=[vmem] * sum(counts),
+        out_shape=[
+            jax.ShapeDtypeStruct((some.shape[2], packed(cap)), BF16)
+            for some in rows
+            for _ in range(some.shape[0])
+        ],
         compiler_params=params(),
         cost_estimate=SMALL,
         name="pick",
-    )(rows, chosen, after)
+    )(chosen, after, *rows)
 
 
 def coded(value, step):
@@ -175,15 +178,16 @@
     return middle + codes[0:rows, :].astype(jnp.int32).astype(F32) * (reach * (1.0 / CODE))
 
 
-def distance_kernel(*refs):
+def distance_kernel(cap, *refs):
     blocks, (signs_ref, after_ref, out, codes_out, joined) = refs[:-5], refs[-5:]
     size = blocks[0].shape[0]
-    cap = signs_ref.shape[0] // len(blocks)
+    slots = signs_ref.shape[0] // len(blocks)
     for s, block in enumerate(blocks):
         for k in range(3):
-            joined[k * size : (k + 1) * size, s * cap : (s + 1) * cap] = block[
-                :, k * cap : (k + 1) * cap
-            ]
+            rows = slice(k * size, (k + 1) * size)
+            joined[rows, s * slots : s * slots + cap] = block[:, k * cap : (k + 1) * cap]
+        if slots > cap:
+            joined[:, s * slots + cap : (s + 1) * slots] = jnp.zeros((3 * size, slots - cap), BF16)
     delta = jnp.dot(joined[...], signs_ref[...], preferred_element_type=F32)
     square = delta * delta
     total = square[:size] + square[size : 2 * size] + square[2 * size :]
@@ -200,11 +204,11 @@
     codes_out[size:, :] = ends.astype(jnp.int32).astype(jnp.int16)
 
 
-def distances(blocks, signs, after):
+def distances(blocks, signs, after, cap):
     size = blocks[0].shape[0]
     vmem = pl.BlockSpec(memory_space=pltpu.VMEM)
     return pl.pallas_call(
-        distance_kernel,
+        functools.partial(distance_kernel, cap),
         in_specs=[vmem] * (len(blocks) + 1) + [pl.BlockSpec(memory_space=pl.ANY)],
         out_specs=[vmem] * 2,
         out_shape=[
@@ -687,14 +691,14 @@
     return jnp.where(used > 0.0, order - 1.0, -1.0), order[width - 1 : width, :]
 
 
-def signs_kernel(groups, width, cap, place_ref, after_ref, *refs):
+def signs_kernel(groups, width, slot_count, place_ref, after_ref, *refs):
     pairs, (signs_out, most_out) = refs[:-2], refs[-2:]
     sides = len(pairs)
     below = upto(width)
     number = lax.broadcasted_iota(jnp.int32, (width, 128), 0) + 1
     high = (number // 8).astype(F32).astype(BF16)
     low = (number % 8).astype(F32).astype(BF16)
-    slots = lax.broadcasted_iota(jnp.int32, (cap, width), 0).astype(F32)
+    slots = lax.broadcasted_iota(jnp.int32, (slot_count, width), 0).astype(F32)
     most = jnp.zeros((1, 128), F32)
     for s in range(groups):
         first = lax.rem(place_ref[0] + groups - s, groups) * width
@@ -712,7 +716,8 @@
                 one = (block[0:1, l : l + 128] == listed).astype(F32)
                 two = (block[1:2, l : l + 128] == listed).astype(F32)
                 at = pl.ds(pl.multiple_of(there + l, 128), 128)
-                signs_out[s * cap : (s + 1) * cap, at] = (one - two).astype(BF16)
+                rows = slice(s * slot_count, (s + 1) * slot_count)
+                signs_out[rows, at] = (one - two).astype(BF16)
     most_out[...] = most
 
 
@@ -720,12 +725,12 @@
     feats = len(pairs) * pairs[0].shape[1]
     vmem = pl.BlockSpec(memory_space=pltpu.VMEM)
     return pl.pallas_call(
-        functools.partial(signs_kernel, groups, width, cap),
+        functools.partial(signs_kernel, groups, width, slot_rows(cap)),
         in_specs=[pl.BlockSpec(memory_space=pltpu.SMEM), pl.BlockSpec(memory_space=pl.ANY)]
         + [vmem] * len(pairs),
         out_specs=[vmem] * 2,
         out_shape=[
-            jax.ShapeDtypeStruct((groups * cap, feats), BF16),
+            jax.ShapeDtypeStruct((groups * slot_rows(cap), feats), BF16),
             jax.ShapeDtypeStruct((1, 128), F32),
         ],
         compiler_params=params(),
@@ -748,13 +753,20 @@
     feats = cols * sides
     sizes = chunk_sizes(frames // sides)
 
-    chosen, traj_ids, pairs, later, picked = first_pick(
-        coords, traj_ids, pairs, cap, place, sizes, groups
+    far, near = shifts_of("atoms")[0], shifts_of("atoms")[1:]
+    chosen, traj_ids, pairs, rows, later, block = first_pick(
+        coords, traj_ids, pairs, cap, place, sizes, near, far
     )
-    arrived = [sent_around(picked)]
-    signs, most_used = pair_signs(pairs, picked[0], place, groups, width, cap)
-    picked = pick(later, chosen, most_used)
-    arrived.append(sent_around(picked))
+    order = near + [0]
+    picked = {far: block} | dict(zip(order, pick([rows], chosen, block)))
+    signs, most_used = pair_signs(pairs, block, place, groups, width, cap)
+    order = [far] + order
+    arrived = []
+    for j in range(2):
+        if j:
+            picked = dict(zip(order, pick([later], chosen, most_used)))
+        moved = {s: rotated(picked[s], "atoms", s) if s else picked[s] for s in order}
+        arrived.append([moved[s] for s in range(groups)])
 
     ids = jnp.concatenate([traj_ids[0], jnp.full((LAG,), -1, jnp.int32)])
     offset = atom_index * frames
@@ -764,13 +776,14 @@
 
     own_pieces, codes, after = [], [], arrived[-1][0]
     for j, blocks in enumerate(arrived):
-        block, code = distances(blocks, signs, after)
+        block, code = distances(blocks, signs, after, cap)
         after = block
         own_pieces.append(block)
         codes.append([rotated(code, "feat", s) for s in range(1, sides)])
         if j == 0:
             opening = passed_down(block[:HALO], "atoms")
     halo = lax.dynamic_slice_in_dim(opening, feat_index * cols, cols, 1)
+    opening = opening + 0.0 * own_pieces[-1][:HALO]
     for s in range(1, sides):
         there = lax.rem(feat_index + s, sides)
         sent = rotated(lax.dynamic_slice_in_dim(opening, there * cols, cols, 1), "feat", s)

time: 116 us -> 115 us (level)
  starting transfers between devices: 15.5 us -> 21.2 us
  waiting for transfers between devices: 67.1 us -> 62.1 us
    ppermute x15, starting transfers between devices: 13.3 us -> 19 us  [rotated(): lax.ppermute(block, axis, [(i, (i + shift) % size) for i in range(size)])]
    ppermute x15, waiting for transfers between devices: 67.1 us -> 62.1 us  [rotated(): lax.ppermute(block, axis, [(i, (i + shift) % size) for i in range(size)])]
    pallas_call x5 -> x6, Pallas kernels: 16.4 us -> 15.6 us  [the longest x1 5.83 us: pair_signs(): pl.pallas_call(functools.partial(signs_kernel, groups, width, slot_rows(c...]
  transfers between devices with their start and end apart: 16 -> 16, of which waited for: 9 -> 7; matrix products, arithmetic and copies ran while one was open for 0% -> 0% of each run, Pallas kernels for 17% -> 17%
where the time goes in v6:
time: 115 us
  waiting for transfers between devices  62.1 us (54%)
  Pallas kernels  29.5 us (26%)
  starting transfers between devices  21.2 us (18%)
    ppermute x15, waiting for transfers between devices, rotated(): lax.ppermute(block, axis, [(i, (i + shift) % size) for i in range(size)])  62.1 us
    ppermute x15, starting transfers between devices, rotated(): lax.ppermute(block, axis, [(i, (i + shift) % size) for i in range(size)])  19 us
    pallas_call x1, Pallas kernels, pair_signs(): pl.pallas_call(functools.partial(signs_kernel, groups, width, slot_rows(c...  5.83 us
    pallas_call x2, Pallas kernels, distances(): pl.pallas_call(functools.partial(distance_kernel, cap), in_specs=[vmem] *...  3.87 us
    pallas_call x1, Pallas kernels, first_pick(): pl.pallas_call(functools.partial(first_pick_kernel, len(pairs), near, far...  3.38 us
    pallas_call x1, Pallas kernels, late_moments(): pl.pallas_call(functools.partial(late_kernel, sizes, sides, groups, reps,...  3.31 us
    pallas_call x1, Pallas kernels, finish(): pl.pallas_call(functools.partial(finish_kernel, reps), in_specs=[pl.Block...  2.84 us
    pallas_call x1, Pallas kernels, early_moments(): pl.pallas_call(functools.partial(early_kernel, len(pieces), sides), in_sp...  2.8 us
  transfers between devices with their start and end apart: 16, of which 7 were waited for; matrix products, arithmetic and copies ran while one was open for 0% of the time, Pallas kernels for 17%

profile of v6, /device:TPU:9, one launch (start us, length us, event | category | flops | bytes accessed | tf_op | source)
XLA Modules:
  0.0 114.5 jit_solution(4757287888075474728)
XLA Ops:
  0.6 1.3 %collective-permute-start.15 = (s32[2,512]{1,0:T(2,128)}, s32[2,512]{1,0:T(2,128)S(1)}, u32[]{:S(2)}, u32[]{:S(2)}) collective-permute-start(s32[2,512]{1,0:T(2,128)} %refs_0_.1), channel_id=1, source_target_pairs={{0,2},{2,0},{1,3},{3,1},{4,6},{6,4},{5,7},{7,5},{8,10},{10,8},{9,1... | collective-permute-start | bytes 12296 | tf_op jit(solution)/shard_map/ppermute | solution.py:28
  1.9 0.1 pad_add_fusion.place_ref
  2.0 1.4 %collective-permute-done.15.refs_1_ = s32[2,512]{1,0:T(2,128)S(1)} collective-permute-done((s32[2,512]{1,0:T(2,128)}, s32[2,512]{1,0:T(2,128)S(1)}, u32[]{:S(2)}, u32[]{:S(2)}) %collective-permute-start.15) | collective-permute-done | bytes 4128 | tf_op jit(solution)/shard_map/ppermute | solution.py:28
  3.4 3.4 %first_pick.5 = (bf16[768,426]{1,0:T(8,128)(2,1)S(1)}, s32[1,2048]{1,0:T(1,128)S(1)}, s32[2,512]{1,0:T(2,128)S(1)}, s32[2,512]{1,0:T(2,128)S(1)}, bf16[3,3,160,7...) custom-call(s32[3]{0:T(128)S(1)} %pad_add_fusion.place_ref, ...), custom_call_target="tpu_custom_call" | custom-call | flops 1024 | bytes 1024 | tf_op jit(solution)/shard_map/first_pick/pallas_call | solution.py:107
  6.8 2.4 %collective-permute-start.17 = (bf16[160,1280]{1,0:T(8,128)(2,1)S(1)}, bf16[160,1280]{1,0:T(8,128)(2,1)S(1)}, u32[]{:S(2)}, u32[]{:S(2)}) collective-permute-start(bf16[160,1280]{1,0:T(8,128)(2,1)S(1)} %get-tuple-element.256.after_ref), channel_id=1, source_target_pairs={{0,8},{4,12},{8,0},{12,4},{1,9},{5,13},{9,1},{13,5},{2,10},{6,14},... | collective-permute-start | bytes 1228808 | tf_op jit(solution)/shard_map/ppermute | solution.py:28
  9.1 1.4 %pick.10 = (bf16[160,1280]{1,0:T(8,128)(2,1)S(1)}, bf16[160,1280]{1,0:T(8,128)(2,1)S(1)}, bf16[160,1280]{1,0:T(8,128)(2,1)S(1)}) custom-call(bf16[768,426]{1,0:T(8,128)(2,1)S(1)} %get-tuple-element.260.chosen_ref, bf16[160,1280]{1,0:T(8,128)(2,1)S(1)} %get-tuple-element.256.after_ref, bf16[3,3,160,768]{3,2,1,0:T(8,128)(2,1)S(1)} %get-tuple-element.261.refs_0_), custom_call_target="tpu_custom_call" | custom-call | flops 1024 | bytes 1024 | tf_op jit(solution)/shard_map/pick/pallas_call | solution.py:148
  10.5 0.1 collective-permute-start.16
  10.6 1.5 %collective-permute-start.18 = (bf16[160,1280]{1,0:T(8,128)(2,1)S(1)}, bf16[160,1280]{1,0:T(8,128)(2,1)S(1)}, u32[]{:S(2)}, u32[]{:S(2)}) collective-permute-start(bf16[160,1280]{1,0:T(8,128)(2,1)S(1)} %get-tuple-element.264), channel_id=1, source_target_pairs={{0,12},{4,0},{8,4},{12,8},{1,13},{5,1},{9,5},{13,9},{2,14},{6,2},{... | collective-permute-start | bytes 1228808 | tf_op jit(solution)/shard_map/ppermute | solution.py:28
  12.0 5.8 %pair_signs.5 = (bf16[1728,1024]{1,0:T(8,128)(2,1)S(1)}, f32[1,128]{1,0:T(1,128)S(1)}) custom-call(s32[3]{0:T(128)S(1)} %pad_add_fusion.place_ref, bf16[160,1280]{1,0:T(8,128)(2,1)S(1)} %get-tuple-element.256.after_ref, s32[2,512]{1,0:T(2,128)S(1)} %get-tuple-element.257.refs_0_, s32[2,512]{1,0:T(2,128)S(1)} %get-tuple-element.258.refs_1_), custom_call_target="tpu_custom_call" | custom-call | flops 99999997952 | bytes 1024 | tf_op jit(solution)/shard_map/pair_signs/pallas_call | solution.py:727
  17.9 0.0 copy-start
  17.9 1.2 %pick.11 = (bf16[96,1280]{1,0:T(8,128)(2,1)S(1)}, bf16[96,1280]{1,0:T(8,128)(2,1)S(1)}, bf16[96,1280]{1,0:T(8,128)(2,1)S(1)}, bf16[96,1280]{1,0:T(8,128)(2,1)S(1)}) custom-call(bf16[768,426]{1,0:T(8,128)(2,1)S(1)} %get-tuple-element.260.chosen_ref, f32[1,128]{1,0:T(1,128)S(1)} %get-tuple-element.259.after_ref, ...), custom_call_target="tpu_custom_call" | custom-call | flops 1024 | bytes 1024 | tf_op jit(solution)/shard_map/pick/pallas_call | solution.py:148
  19.1 0.1 collective-permute-start.20
  19.2 4.0 %collective-permute-start.21 = (bf16[96,1280]{1,0:T(8,128)(2,1)S(1)}, bf16[96,1280]{1,0:T(8,128)(2,1)S(1)}, u32[]{:S(2)}, u32[]{:S(2)}) collective-permute-start(bf16[96,1280]{1,0:T(8,128)(2,1)S(1)} %get-tuple-element.270), channel_id=1, source_target_pairs={{0,8},{4,12},{8,0},{12,4},{1,9},{5,13},{9,1},{13,5},{2,10},{6,14},... | collective-permute-start | bytes 737288 | tf_op jit(solution)/shard_map/ppermute | solution.py:28
  23.2 31.9 %collective-permute-done.16.refs_1_ = bf16[160,1280]{1,0:T(8,128)(2,1)S(1)} collective-permute-done((bf16[160,1280]{1,0:T(8,128)(2,1)S(1)}, bf16[160,1280]{1,0:T(8,128)(2,1)S(1)}, u32[]{:S(2)}, u32[]{:S(2)}) %collective-permute-start.16) | collective-permute-done | bytes 409632 | tf_op jit(solution)/shard_map/ppermute | solution.py:28
  55.1 0.0 collective-permute-start.22
  55.1 0.0 collective-permute-done.17.refs_2_
  55.1 0.0 collective-permute-done.18.refs_3_
  55.1 2.3 %distances.10 = (f32[160,1024]{1,0:T(8,128)S(1)}, s16[176,1024]{1,0:T(8,128)(2,1)S(1)}) custom-call(bf16[160,1280]{1,0:T(8,128)(2,1)S(1)} %get-tuple-element.262.refs_0_, bf16[160,1280]{1,0:T(8,128)(2,1)S(1)} %collective-permute-done.16.refs_1_, bf16[160,1280]{1,0:T(8,128)(2,1)S(1)} %collective-permute-done.17.refs_2_, ...), custom_call_target="tpu_custom_call" | custom-call | flops 99999997952 | bytes 1024 | tf_op jit(solution)/shard_map/distances/pallas_call | solution.py:210
  57.5 1.3 %collective-permute-start.19 = (s16[176,1024]{1,0:T(8,128)(2,1)S(1)}, s16[176,1024]{1,0:T(8,128)(2,1)S(1)}, u32[]{:S(2)}, u32[]{:S(2)}) collective-permute-start(s16[176,1024]{1,0:T(8,128)(2,1)S(1)} %get-tuple-element.268), channel_id=1, source_target_pairs={{0,2},{2,0},{1,3},{3,1},{4,6},{6,4},{5,7},{7,5},{8,10},{10,8},{9,1... | collective-permute-start | bytes 1081352 | tf_op jit(solution)/shard_map/ppermute | solution.py:28
  58.8 2.2 %collective-permute-start.24 = (f32[16,1024]{1,0:T(8,128)S(1)}, f32[16,1024]{1,0:T(8,128)S(1)}, u32[]{:S(2)}, u32[]{:S(2)}) collective-permute-start(f32[16,1024]{1,0:T(8,128)S(1)} %slice.22), channel_id=1, source_target_pairs={{4,0},{8,4},{12,8},{5,1},{9,5},{13,9},{6,2},{10,6},{14,10},{7,3},{... | collective-permute-start | bytes 196616 | tf_op jit(solution)/shard_map/ppermute | solution.py:37
  61.0 4.7 %collective-permute-done.21.refs_2_ = bf16[96,1280]{1,0:T(8,128)(2,1)S(1)} collective-permute-done((bf16[96,1280]{1,0:T(8,128)(2,1)S(1)}, bf16[96,1280]{1,0:T(8,128)(2,1)S(1)}, u32[]{:S(2)}, u32[]{:S(2)}) %collective-permute-start.21) | collective-permute-done | bytes 245792 | tf_op jit(solution)/shard_map/ppermute | solution.py:28
  65.7 0.0 collective-permute-done.22.refs_3_
  65.7 1.5 %distances.11 = (f32[96,1024]{1,0:T(8,128)S(1)}, s16[112,1024]{1,0:T(8,128)(2,1)S(1)}) custom-call(bf16[96,1280]{1,0:T(8,128)(2,1)S(1)} %get-tuple-element.267.refs_5_.refs_0_, bf16[96,1280]{1,0:T(8,128)(2,1)S(1)} %collective-permute-done.20.refs_1_, bf16[96,1280]{1,0:T(8,128)(2,1)S(1)} %collective-permute-done.21.refs_2_, ...), custom_call_target="tpu_custom_call" | custom-call | flops 99999997952 | bytes 1024 | tf_op jit(solution)/shard_map/distances/pallas_call | solution.py:210
  67.2 1.3 %collective-permute-start.23 = (s16[112,1024]{1,0:T(8,128)(2,1)S(1)}, s16[112,1024]{1,0:T(8,128)(2,1)S(1)}, u32[]{:S(2)}, u32[]{:S(2)}) collective-permute-start(s16[112,1024]{1,0:T(8,128)(2,1)S(1)} %get-tuple-element.273), channel_id=1, source_target_pairs={{0,2},{2,0},{1,3},{3,1},{4,6},{6,4},{5,7},{7,5},{8,10},{10,8},{9,1... | collective-permute-start | bytes 688136 | tf_op jit(solution)/shard_map/ppermute | solution.py:28
  68.5 0.0 collective-permute-done.24
  68.5 0.3 collective-permute-start.25
  68.8 0.1 fusion.3
  68.9 0.2 copy.8.refs_2_.refs_8_
  69.1 2.8 %early_moments.5 = (f32[1024,1024]{1,0:T(8,128)S(1)}, f32[256,512]{1,0:T(8,128)S(1)}, f32[1,1024]{1,0:T(1,128)S(1)}, f32[4,1024]{1,0:T(4,128)S(1)}, f32[16,1024]{1,0:T(8,128)S(1)}) custom-call(s32[3]{0:T(128)S(1)} %copy-done.3, f32[160,1024]{1,0:T(8,128)S(1)} %get-tuple-element.272.refs_5_.refs_0_, f32[96,1024]{1,0:T(8,128)S(1)} %get-tuple-element.274.refs_1_, ...), custom_call_target="tpu_custom_call" | custom-call | flops 1024 | bytes 1024 | tf_op jit(solution)/shard_map/early_moments/pallas_call | solution.py:289
  71.9 2.1 %collective-permute-done.25 = f32[16,512]{1,0:T(8,128)S(1)} collective-permute-done((f32[16,512]{1,0:T(8,128)S(1)}, f32[16,512]{1,0:T(8,128)S(1)}, u32[]{:S(2)}, u32[]{:S(2)}) %collective-permute-start.25) | collective-permute-done | bytes 32800 | tf_op jit(solution)/shard_map/ppermute | solution.py:28
  74.0 0.0 collective-permute-done.23.refs_1_
  74.0 3.3 %late_moments.5 = (f32[264,1024]{1,0:T(8,128)S(1)}, f32[264,1024]{1,0:T(8,128)S(1)}, f32[512,512]{1,0:T(8,128)S(1)}, bf16[1024,288]{1,0:T(8,128)(2,1)S(1)}, bf16...) custom-call(s32[3]{0:T(128)S(1)} %copy-done.3, ...), custom_call_target="tpu_custom_call" | custom-call | flops 1024 | bytes 1024 | tf_op jit(solution)/shard_map/late_moments/pallas_call | solution.py:422
  77.3 2.1 %collective-permute-start.26 = (f32[264,1024]{1,0:T(8,128)S(1)}, f32[264,1024]{1,0:T(8,128)S(1)}, u32[]{:S(2)}, u32[]{:S(2)}) collective-permute-start(f32[264,1024]{1,0:T(8,128)S(1)} %get-tuple-element.282), channel_id=1, source_target_pairs={{0,1},{1,0},{2,3},{3,2},{4,5},{5,4},{6,7},{7,6},{8,9},{9,8},{10,11... | collective-permute-start | bytes 3244040 | tf_op jit(solution)/shard_map/ppermute | solution.py:28
  79.4 2.3 %rest_moments.5 = (f32[256,1024]{1,0:T(8,128)S(1)}, f32[256,1024]{1,0:T(8,128)S(1)}) custom-call(s32[3]{0:T(128)S(1)} %copy-done.3, f32[1024,1024]{1,0:T(8,128)S(1)} %get-tuple-element.276.refs_2_.before_ref, bf16[1024,288]{1,0:T(8,128)(2,1)S(1)} %get-tuple-element.285.left_high, bf16[1024,288]{1,0:T(8,128)(2,1)S(1)} %get-tuple-element.286.left_low, ...), custom_call_target="tpu_custom_call" | custom-call | flops 1024 | bytes 1024 | tf_op jit(solution)/shard_map/rest_moments/pallas_call | solution.py:455
  81.7 0.1 collective-permute-start.27
  81.8 0.0 copy-start.1
  81.8 1.5 %first_share.5 = (s16[144,1024]{1,0:T(8,128)(2,1)S(1)}, s16[144,1024]{1,0:T(8,128)(2,1)S(1)}, s16[16,1024]{1,0:T(8,128)(2,1)S(1)}, f32[8,1024]{1,0:T(8,128)S(1)}) custom-call(s32[3]{0:T(128)S(1)} %copy-done.3, f32[264,1024]{1,0:T(8,128)S(1)} %get-tuple-element.281.refs_0_, f32[264,1024]{1,0:T(8,128)S(1)} %collective-permute-done.26.refs_1_), custom_call_target="tpu_custom_call" | custom-call | flops 1024 | bytes 1024 | tf_op jit(solution)/shard_map/first_share/pallas_call | solution.py:550
  83.3 3.2 %collective-permute-start.28 = (s16[144,1024]{1,0:T(8,128)(2,1)S(1)}, s16[144,1024]{1,0:T(8,128)(2,1)S(1)}, u32[]{:S(2)}, u32[]{:S(2)}) collective-permute-start(s16[144,1024]{1,0:T(8,128)(2,1)S(1)} %get-tuple-element.292), channel_id=1, source_target_pairs={{0,8},{4,12},{8,0},{12,4},{1,9},{5,13},{9,1},{13,5},{2,10},{6,14},... | collective-permute-start | bytes 884744 | tf_op jit(solution)/shard_map/ppermute | solution.py:28
  86.5 0.0 collective-permute-start.29
  86.5 1.1 rest_share.5
  87.6 0.0 copy-start.5
  87.6 0.0 copy-start.7
  87.6 1.5 %collective-permute-start.30 = (s16[144,1024]{1,0:T(8,128)(2,1)S(1)}, s16[144,1024]{1,0:T(8,128)(2,1)S(1)}, u32[]{:S(2)}, u32[]{:S(2)}) collective-permute-start(s16[144,1024]{1,0:T(8,128)(2,1)S(1)} %get-tuple-element.294), channel_id=1, source_target_pairs={{0,12},{4,0},{8,4},{12,8},{1,13},{5,1},{9,5},{13,9},{2,14},{6,2},{... | collective-permute-start | bytes 884744 | tf_op jit(solution)/shard_map/ppermute | solution.py:28
  89.2 8.7 %collective-permute-done.28.refs_0_ = s16[144,1024]{1,0:T(8,128)(2,1)S(1)} collective-permute-done((s16[144,1024]{1,0:T(8,128)(2,1)S(1)}, s16[144,1024]{1,0:T(8,128)(2,1)S(1)}, u32[]{:S(2)}, u32[]{:S(2)}) %collective-permute-start.28) | collective-permute-done | bytes 294944 | tf_op jit(solution)/shard_map/ppermute | solution.py:28
  97.9 12.3 %collective-permute-done.29.refs_1_ = s16[144,1024]{1,0:T(8,128)(2,1)S(1)} collective-permute-done((s16[144,1024]{1,0:T(8,128)(2,1)S(1)}, s16[144,1024]{1,0:T(8,128)(2,1)S(1)}, u32[]{:S(2)}, u32[]{:S(2)}) %collective-permute-start.29) | collective-permute-done | bytes 294944 | tf_op jit(solution)/shard_map/ppermute | solution.py:28
  110.2 1.0 collective-permute-done.30.refs_2_
  111.2 2.8 %finish.5 = (f32[128,512]{1,0:T(8,128)}, f32[128,512]{1,0:T(8,128)}, f32[512,512]{1,0:T(8,128)}) custom-call(s32[3]{0:T(128)S(1)} %copy-done.3, f32[128,1024]{1,0:T(8,128)S(1)} %get-tuple-element.291.kept_ref, s16[16,1024]{1,0:T(8,128)(2,1)S(1)} %get-tuple-element.284.codes_ref, s16[144,1024]{1,0:T(8,128)(2,1)S(1)} %collective-permute-done.28.refs_0_, ...), custom_call_target="tpu_custom_call" | custom-call | flops 1024 | bytes 1024 | tf_op jit(solution)/shard_map/finish/pallas_call | solution.py:661
  114.1 0.2 while.16
  (20 shorter events, 0.1 us)
Async XLA Ops:
  0.6 2.7 %collective-permute-start.15 = (s32[2,512]{1,0:T(2,128)}, s32[2,512]{1,0:T(2,128)S(1)}, u32[]{:S(2)}, u32[]{:S(2)}) collective-permute-start(s32[2,512]{1,0:T(2,128)} %refs_0_.1), channel_id=1, source_target_pairs={{0,2},{2,0},{1,3},{3,1},{4,6},{6,4},{5,7},{7,5},{8,10},{10,8},{9,1... | collective-permute-start | bytes 12296 | tf_op jit(solution)/shard_map/ppermute | solution.py:28
  2.0 10.1 %copy-start.2 = (s32[3]{0:T(128)}, s32[3]{0:T(128)S(1)}, u32[]{:S(2)}) copy-start(s32[3]{0:T(128)S(1)} %pad_add_fusion.place_ref) | copy-start | bytes 40
  3.4 3.4 %copy-start.9 = (s32[2,512]{1,0:T(2,128)}, s32[2,512]{1,0:T(2,128)S(1)}, u32[]{:S(2)}) copy-start(s32[2,512]{1,0:T(2,128)S(1)} %collective-permute-done.15.refs_1_) | copy-start | bytes 12292
  6.8 48.4 %collective-permute-start.17 = (bf16[160,1280]{1,0:T(8,128)(2,1)S(1)}, bf16[160,1280]{1,0:T(8,128)(2,1)S(1)}, u32[]{:S(2)}, u32[]{:S(2)}) collective-permute-start(bf16[160,1280]{1,0:T(8,128)(2,1)S(1)} %get-tuple-element.256.after_ref), channel_id=1, source_target_pairs={{0,8},{4,12},{8,0},{12,4},{1,9},{5,13},{9,1},{13,5},{2,10},{6,14},... | collective-permute-start | bytes 1228808 | tf_op jit(solution)/shard_map/ppermute | solution.py:28
  10.5 44.6 %collective-permute-start.16 = (bf16[160,1280]{1,0:T(8,128)(2,1)S(1)}, bf16[160,1280]{1,0:T(8,128)(2,1)S(1)}, u32[]{:S(2)}, u32[]{:S(2)}) collective-permute-start(bf16[160,1280]{1,0:T(8,128)(2,1)S(1)} %get-tuple-element.263), channel_id=1, source_target_pairs={{0,4},{4,8},{8,12},{12,0},{1,5},{5,9},{9,13},{13,1},{2,6},{6,10},{... | collective-permute-start | bytes 1228808 | tf_op jit(solution)/shard_map/ppermute | solution.py:28
  10.6 44.5 %collective-permute-start.18 = (bf16[160,1280]{1,0:T(8,128)(2,1)S(1)}, bf16[160,1280]{1,0:T(8,128)(2,1)S(1)}, u32[]{:S(2)}, u32[]{:S(2)}) collective-permute-start(bf16[160,1280]{1,0:T(8,128)(2,1)S(1)} %get-tuple-element.264), channel_id=1, source_target_pairs={{0,12},{4,0},{8,4},{12,8},{1,13},{5,1},{9,5},{13,9},{2,14},{6,2},{... | collective-permute-start | bytes 1228808 | tf_op jit(solution)/shard_map/ppermute | solution.py:28
  17.9 37.3 %copy-start = (f32[1,128]{1,0:T(1,128)}, f32[1,128]{1,0:T(1,128)S(1)}, u32[]{:S(2)}) copy-start(f32[1,128]{1,0:T(1,128)S(1)} %get-tuple-element.259.after_ref) | copy-start | bytes 1540
  19.1 41.9 %collective-permute-start.20 = (bf16[96,1280]{1,0:T(8,128)(2,1)S(1)}, bf16[96,1280]{1,0:T(8,128)(2,1)S(1)}, u32[]{:S(2)}, u32[]{:S(2)}) collective-permute-start(bf16[96,1280]{1,0:T(8,128)(2,1)S(1)} %get-tuple-element.269), channel_id=1, source_target_pairs={{0,4},{4,8},{8,12},{12,0},{1,5},{5,9},{9,13},{13,1},{2,6},{6,10},{... | collective-permute-start | bytes 737288 | tf_op jit(solution)/shard_map/ppermute | solution.py:28
  19.2 46.5 %collective-permute-start.21 = (bf16[96,1280]{1,0:T(8,128)(2,1)S(1)}, bf16[96,1280]{1,0:T(8,128)(2,1)S(1)}, u32[]{:S(2)}, u32[]{:S(2)}) collective-permute-start(bf16[96,1280]{1,0:T(8,128)(2,1)S(1)} %get-tuple-element.270), channel_id=1, source_target_pairs={{0,8},{4,12},{8,0},{12,4},{1,9},{5,13},{9,1},{13,5},{2,10},{6,14},... | collective-permute-start | bytes 737288 | tf_op jit(solution)/shard_map/ppermute | solution.py:28
  55.1 10.5 %collective-permute-start.22 = (bf16[96,1280]{1,0:T(8,128)(2,1)S(1)}, bf16[96,1280]{1,0:T(8,128)(2,1)S(1)}, u32[]{:S(2)}, u32[]{:S(2)}) collective-permute-start(bf16[96,1280]{1,0:T(8,128)(2,1)S(1)} %get-tuple-element.271), channel_id=1, source_target_pairs={{0,12},{4,0},{8,4},{12,8},{1,13},{5,1},{9,5},{13,9},{2,14},{6,2},{... | collective-permute-start | bytes 737288 | tf_op jit(solution)/shard_map/ppermute | solution.py:28
  57.5 16.5 %collective-permute-start.19 = (s16[176,1024]{1,0:T(8,128)(2,1)S(1)}, s16[176,1024]{1,0:T(8,128)(2,1)S(1)}, u32[]{:S(2)}, u32[]{:S(2)}) collective-permute-start(s16[176,1024]{1,0:T(8,128)(2,1)S(1)} %get-tuple-element.268), channel_id=1, source_target_pairs={{0,2},{2,0},{1,3},{3,1},{4,6},{6,4},{5,7},{7,5},{8,10},{10,8},{9,1... | collective-permute-start | bytes 1081352 | tf_op jit(solution)/shard_map/ppermute | solution.py:28
  58.8 10.3 %copy-start.3 = (s32[3]{0:T(128)S(1)}, s32[3]{0:T(128)}, u32[]{:S(2)}) copy-start(s32[3]{0:T(128)} %copy-done.2) | copy-start | bytes 40
  58.8 9.7 %collective-permute-start.24 = (f32[16,1024]{1,0:T(8,128)S(1)}, f32[16,1024]{1,0:T(8,128)S(1)}, u32[]{:S(2)}, u32[]{:S(2)}) collective-permute-start(f32[16,1024]{1,0:T(8,128)S(1)} %slice.22), channel_id=1, source_target_pairs={{4,0},{8,4},{12,8},{5,1},{9,5},{13,9},{6,2},{10,6},{14,10},{7,3},{... | collective-permute-start | bytes 196616 | tf_op jit(solution)/shard_map/ppermute | solution.py:37
  67.2 6.8 %collective-permute-start.23 = (s16[112,1024]{1,0:T(8,128)(2,1)S(1)}, s16[112,1024]{1,0:T(8,128)(2,1)S(1)}, u32[]{:S(2)}, u32[]{:S(2)}) collective-permute-start(s16[112,1024]{1,0:T(8,128)(2,1)S(1)} %get-tuple-element.273), channel_id=1, source_target_pairs={{0,2},{2,0},{1,3},{3,1},{4,6},{6,4},{5,7},{7,5},{8,10},{10,8},{9,1... | collective-permute-start | bytes 688136 | tf_op jit(solution)/shard_map/ppermute | solution.py:28
  68.5 5.5 %collective-permute-start.25 = (f32[16,512]{1,0:T(8,128)S(1)}, f32[16,512]{1,0:T(8,128)S(1)}, u32[]{:S(2)}, u32[]{:S(2)}) collective-permute-start(f32[16,512]{1,0:T(8,128)S(1)} %dynamic-slice_add_fusion.1), channel_id=1, source_target_pairs={{0,2},{2,0},{1,3},{3,1},{4,6},{6,4},{5,7},{7,5},{8,10},{10,8},{9,1... | collective-permute-start | bytes 98312 | tf_op jit(solution)/shard_map/ppermute | solution.py:28
  77.3 4.5 %collective-permute-start.26 = (f32[264,1024]{1,0:T(8,128)S(1)}, f32[264,1024]{1,0:T(8,128)S(1)}, u32[]{:S(2)}, u32[]{:S(2)}) collective-permute-start(f32[264,1024]{1,0:T(8,128)S(1)} %get-tuple-element.282), channel_id=1, source_target_pairs={{0,1},{1,0},{2,3},{3,2},{4,5},{5,4},{6,7},{7,6},{8,9},{9,8},{10,11... | collective-permute-start | bytes 3244040 | tf_op jit(solution)/shard_map/ppermute | solution.py:28
  81.7 4.7 %collective-permute-start.27 = (f32[256,1024]{1,0:T(8,128)S(1)}, f32[256,1024]{1,0:T(8,128)S(1)}, u32[]{:S(2)}, u32[]{:S(2)}) collective-permute-start(f32[256,1024]{1,0:T(8,128)S(1)} %get-tuple-element.290), channel_id=1, source_target_pairs={{0,1},{1,0},{2,3},{3,2},{4,5},{5,4},{6,7},{7,6},{8,9},{9,8},{10,11... | collective-permute-start | bytes 3145736 | tf_op jit(solution)/shard_map/ppermute | solution.py:28
  81.8 7.3 %copy-start.1 = (f32[1,128]{1,0:T(1,128)S(1)}, f32[1,128]{1,0:T(1,128)}, u32[]{:S(2)}) copy-start(f32[1,128]{1,0:T(1,128)} %copy-done) | copy-start | bytes 1540
  83.3 14.6 %collective-permute-start.28 = (s16[144,1024]{1,0:T(8,128)(2,1)S(1)}, s16[144,1024]{1,0:T(8,128)(2,1)S(1)}, u32[]{:S(2)}, u32[]{:S(2)}) collective-permute-start(s16[144,1024]{1,0:T(8,128)(2,1)S(1)} %get-tuple-element.292), channel_id=1, source_target_pairs={{0,8},{4,12},{8,0},{12,4},{1,9},{5,13},{9,1},{13,5},{2,10},{6,14},... | collective-permute-start | bytes 884744 | tf_op jit(solution)/shard_map/ppermute | solution.py:28
  86.5 23.8 %collective-permute-start.29 = (s16[144,1024]{1,0:T(8,128)(2,1)S(1)}, s16[144,1024]{1,0:T(8,128)(2,1)S(1)}, u32[]{:S(2)}, u32[]{:S(2)}) collective-permute-start(s16[144,1024]{1,0:T(8,128)(2,1)S(1)} %get-tuple-element.293), channel_id=1, source_target_pairs={{0,4},{4,8},{8,12},{12,0},{1,5},{5,9},{9,13},{13,1},{2,6},{6,10},{... | collective-permute-start | bytes 884744 | tf_op jit(solution)/shard_map/ppermute | solution.py:28
  87.6 26.5 %copy-start.5 = (s32[1,2048]{1,0:T(1,128)S(1)}, s32[1,2048]{1,0:T(1,128)}, u32[]{:S(2)}) copy-start(s32[1,2048]{1,0:T(1,128)} %ids_ref.1) | copy-start | bytes 24580
  87.6 26.5 %copy-start.7 = (s32[2,512]{1,0:T(2,128)S(1)}, s32[2,512]{1,0:T(2,128)}, u32[]{:S(2)}) copy-start(s32[2,512]{1,0:T(2,128)} %refs_0_.1) | copy-start | bytes 12292
  87.6 26.5 %copy-start.10 = (s32[2,512]{1,0:T(2,128)S(1)}, s32[2,512]{1,0:T(2,128)}, u32[]{:S(2)}) copy-start(s32[2,512]{1,0:T(2,128)} %copy-done.9) | copy-start | bytes 12292
  87.6 23.6 %collective-permute-start.30 = (s16[144,1024]{1,0:T(8,128)(2,1)S(1)}, s16[144,1024]{1,0:T(8,128)(2,1)S(1)}, u32[]{:S(2)}, u32[]{:S(2)}) collective-permute-start(s16[144,1024]{1,0:T(8,128)(2,1)S(1)} %get-tuple-element.294), channel_id=1, source_target_pairs={{0,12},{4,0},{8,4},{12,8},{1,13},{5,1},{9,5},{13,9},{2,14},{6,2},{... | collective-permute-start | bytes 884744 | tf_op jit(solution)/shard_map/ppermute | solution.py:28

commit v7 on v6

--- a/solution.py
+++ b/solution.py
@@ -16,10 +16,10 @@
 ROOT_STEP = 0.02
 TINY = 1e-30
 REACH = 1e-6
-VMEM_LIMIT = 20 * 1024 * 1024
+VMEM_LIMIT = 16 * 1024 * 1024
 F32 = jnp.float32
 BF16 = jnp.bfloat16
-LARGE = pl.CostEstimate(flops=10**11, bytes_accessed=1024, transcendentals=0)
+LARGE = pl.CostEstimate(flops=3*10**10, bytes_accessed=1024, transcendentals=0)
 SMALL = pl.CostEstimate(flops=1024, bytes_accessed=1024, transcendentals=0)
 
 

time: 115 us -> 115 us (level)
  no operation moved by 1% of the time
where the time goes in v7:
time: 115 us; the launch traced here: 114 us
  waiting for transfers between devices  62.2 us (54%)
  Pallas kernels  29.5 us (26%)
  starting transfers between devices  21.2 us (18%)
    ppermute x15, waiting for transfers between devices, rotated(): lax.ppermute(block, axis, [(i, (i + shift) % size) for i in range(size)])  62.2 us
    ppermute x15, starting transfers between devices, rotated(): lax.ppermute(block, axis, [(i, (i + shift) % size) for i in range(size)])  19 us
    pallas_call x1, Pallas kernels, pair_signs(): pl.pallas_call(functools.partial(signs_kernel, groups, width, slot_rows(c...  5.84 us
    pallas_call x2, Pallas kernels, distances(): pl.pallas_call(functools.partial(distance_kernel, cap), in_specs=[vmem] *...  3.88 us
    pallas_call x1, Pallas kernels, first_pick(): pl.pallas_call(functools.partial(first_pick_kernel, len(pairs), near, far...  3.38 us
    pallas_call x1, Pallas kernels, late_moments(): pl.pallas_call(functools.partial(late_kernel, sizes, sides, groups, reps,...  3.33 us
    pallas_call x1, Pallas kernels, finish(): pl.pallas_call(functools.partial(finish_kernel, reps), in_specs=[pl.Block...  2.83 us
    pallas_call x1, Pallas kernels, early_moments(): pl.pallas_call(functools.partial(early_kernel, len(pieces), sides), in_sp...  2.8 us
  transfers between devices with their start and end apart: 16, of which 7 were waited for; matrix products, arithmetic and copies ran while one was open for 0% of the time, Pallas kernels for 17%

profile of v7, /device:TPU:9, one launch (start us, length us, event | category | flops | bytes accessed | tf_op | source)
XLA Modules:
  0.0 114.1 jit_solution(4572359397649589205)
XLA Ops:
  0.6 1.3 %collective-permute-start.15 = (s32[2,512]{1,0:T(2,128)}, s32[2,512]{1,0:T(2,128)S(1)}, u32[]{:S(2)}, u32[]{:S(2)}) collective-permute-start(s32[2,512]{1,0:T(2,128)} %refs_0_.1), channel_id=1, source_target_pairs={{0,2},{2,0},{1,3},{3,1},{4,6},{6,4},{5,7},{7,5},{8,10},{10,8},{9,1... | collective-permute-start | bytes 12296 | tf_op jit(solution)/shard_map/ppermute | solution.py:28
  1.9 0.1 pad_add_fusion.place_ref
  2.0 1.4 %collective-permute-done.15.refs_1_ = s32[2,512]{1,0:T(2,128)S(1)} collective-permute-done((s32[2,512]{1,0:T(2,128)}, s32[2,512]{1,0:T(2,128)S(1)}, u32[]{:S(2)}, u32[]{:S(2)}) %collective-permute-start.15) | collective-permute-done | bytes 4128 | tf_op jit(solution)/shard_map/ppermute | solution.py:28
  3.4 3.4 %first_pick.5 = (bf16[768,426]{1,0:T(8,128)(2,1)S(1)}, s32[1,2048]{1,0:T(1,128)S(1)}, s32[2,512]{1,0:T(2,128)S(1)}, s32[2,512]{1,0:T(2,128)S(1)}, bf16[3,3,160,7...) custom-call(s32[3]{0:T(128)S(1)} %pad_add_fusion.place_ref, ...), custom_call_target="tpu_custom_call" | custom-call | flops 1024 | bytes 1024 | tf_op jit(solution)/shard_map/first_pick/pallas_call | solution.py:107
  6.7 2.4 %collective-permute-start.17 = (bf16[160,1280]{1,0:T(8,128)(2,1)S(1)}, bf16[160,1280]{1,0:T(8,128)(2,1)S(1)}, u32[]{:S(2)}, u32[]{:S(2)}) collective-permute-start(bf16[160,1280]{1,0:T(8,128)(2,1)S(1)} %get-tuple-element.256.after_ref), channel_id=1, source_target_pairs={{0,8},{4,12},{8,0},{12,4},{1,9},{5,13},{9,1},{13,5},{2,10},{6,14},... | collective-permute-start | bytes 1228808 | tf_op jit(solution)/shard_map/ppermute | solution.py:28
  9.1 1.4 %pick.10 = (bf16[160,1280]{1,0:T(8,128)(2,1)S(1)}, bf16[160,1280]{1,0:T(8,128)(2,1)S(1)}, bf16[160,1280]{1,0:T(8,128)(2,1)S(1)}) custom-call(bf16[768,426]{1,0:T(8,128)(2,1)S(1)} %get-tuple-element.260.chosen_ref, bf16[160,1280]{1,0:T(8,128)(2,1)S(1)} %get-tuple-element.256.after_ref, bf16[3,3,160,768]{3,2,1,0:T(8,128)(2,1)S(1)} %get-tuple-element.261.refs_0_), custom_call_target="tpu_custom_call" | custom-call | flops 1024 | bytes 1024 | tf_op jit(solution)/shard_map/pick/pallas_call | solution.py:148
  10.5 0.1 collective-permute-start.16
  10.6 1.5 %collective-permute-start.18 = (bf16[160,1280]{1,0:T(8,128)(2,1)S(1)}, bf16[160,1280]{1,0:T(8,128)(2,1)S(1)}, u32[]{:S(2)}, u32[]{:S(2)}) collective-permute-start(bf16[160,1280]{1,0:T(8,128)(2,1)S(1)} %get-tuple-element.264), channel_id=1, source_target_pairs={{0,12},{4,0},{8,4},{12,8},{1,13},{5,1},{9,5},{13,9},{2,14},{6,2},{... | collective-permute-start | bytes 1228808 | tf_op jit(solution)/shard_map/ppermute | solution.py:28
  12.0 5.8 %pair_signs.5 = (bf16[1728,1024]{1,0:T(8,128)(2,1)S(1)}, f32[1,128]{1,0:T(1,128)S(1)}) custom-call(s32[3]{0:T(128)S(1)} %pad_add_fusion.place_ref, bf16[160,1280]{1,0:T(8,128)(2,1)S(1)} %get-tuple-element.256.after_ref, s32[2,512]{1,0:T(2,128)S(1)} %get-tuple-element.257.refs_0_, s32[2,512]{1,0:T(2,128)S(1)} %get-tuple-element.258.refs_1_), custom_call_target="tpu_custom_call" | custom-call | flops 30000001024 | bytes 1024 | tf_op jit(solution)/shard_map/pair_signs/pallas_call | solution.py:727
  17.9 1.2 %pick.11 = (bf16[96,1280]{1,0:T(8,128)(2,1)S(1)}, bf16[96,1280]{1,0:T(8,128)(2,1)S(1)}, bf16[96,1280]{1,0:T(8,128)(2,1)S(1)}, bf16[96,1280]{1,0:T(8,128)(2,1)S(1)}) custom-call(bf16[768,426]{1,0:T(8,128)(2,1)S(1)} %get-tuple-element.260.chosen_ref, f32[1,128]{1,0:T(1,128)S(1)} %get-tuple-element.259.after_ref, ...), custom_call_target="tpu_custom_call" | custom-call | flops 1024 | bytes 1024 | tf_op jit(solution)/shard_map/pick/pallas_call | solution.py:148
  19.0 0.1 collective-permute-start.20
  19.2 4.0 %collective-permute-start.21 = (bf16[96,1280]{1,0:T(8,128)(2,1)S(1)}, bf16[96,1280]{1,0:T(8,128)(2,1)S(1)}, u32[]{:S(2)}, u32[]{:S(2)}) collective-permute-start(bf16[96,1280]{1,0:T(8,128)(2,1)S(1)} %get-tuple-element.270), channel_id=1, source_target_pairs={{0,8},{4,12},{8,0},{12,4},{1,9},{5,13},{9,1},{13,5},{2,10},{6,14},... | collective-permute-start | bytes 737288 | tf_op jit(solution)/shard_map/ppermute | solution.py:28
  23.1 32.0 %collective-permute-done.16.refs_1_ = bf16[160,1280]{1,0:T(8,128)(2,1)S(1)} collective-permute-done((bf16[160,1280]{1,0:T(8,128)(2,1)S(1)}, bf16[160,1280]{1,0:T(8,128)(2,1)S(1)}, u32[]{:S(2)}, u32[]{:S(2)}) %collective-permute-start.16) | collective-permute-done | bytes 409632 | tf_op jit(solution)/shard_map/ppermute | solution.py:28
  55.1 0.0 collective-permute-start.22
  55.1 0.0 collective-permute-done.17.refs_2_
  55.1 0.0 collective-permute-done.18.refs_3_
  55.1 2.4 %distances.10 = (f32[160,1024]{1,0:T(8,128)S(1)}, s16[176,1024]{1,0:T(8,128)(2,1)S(1)}) custom-call(bf16[160,1280]{1,0:T(8,128)(2,1)S(1)} %get-tuple-element.262.refs_0_, bf16[160,1280]{1,0:T(8,128)(2,1)S(1)} %collective-permute-done.16.refs_1_, bf16[160,1280]{1,0:T(8,128)(2,1)S(1)} %collective-permute-done.17.refs_2_, ...), custom_call_target="tpu_custom_call" | custom-call | flops 30000001024 | bytes 1024 | tf_op jit(solution)/shard_map/distances/pallas_call | solution.py:210
  57.5 1.3 %collective-permute-start.19 = (s16[176,1024]{1,0:T(8,128)(2,1)S(1)}, s16[176,1024]{1,0:T(8,128)(2,1)S(1)}, u32[]{:S(2)}, u32[]{:S(2)}) collective-permute-start(s16[176,1024]{1,0:T(8,128)(2,1)S(1)} %get-tuple-element.268), channel_id=1, source_target_pairs={{0,2},{2,0},{1,3},{3,1},{4,6},{6,4},{5,7},{7,5},{8,10},{10,8},{9,1... | collective-permute-start | bytes 1081352 | tf_op jit(solution)/shard_map/ppermute | solution.py:28
  58.8 2.2 %collective-permute-start.24 = (f32[16,1024]{1,0:T(8,128)S(1)}, f32[16,1024]{1,0:T(8,128)S(1)}, u32[]{:S(2)}, u32[]{:S(2)}) collective-permute-start(f32[16,1024]{1,0:T(8,128)S(1)} %slice.22), channel_id=1, source_target_pairs={{4,0},{8,4},{12,8},{5,1},{9,5},{13,9},{6,2},{10,6},{14,10},{7,3},{... | collective-permute-start | bytes 196616 | tf_op jit(solution)/shard_map/ppermute | solution.py:37
  61.0 0.0 collective-permute-done.20.refs_1_
  61.0 4.7 %collective-permute-done.21.refs_2_ = bf16[96,1280]{1,0:T(8,128)(2,1)S(1)} collective-permute-done((bf16[96,1280]{1,0:T(8,128)(2,1)S(1)}, bf16[96,1280]{1,0:T(8,128)(2,1)S(1)}, u32[]{:S(2)}, u32[]{:S(2)}) %collective-permute-start.21) | collective-permute-done | bytes 245792 | tf_op jit(solution)/shard_map/ppermute | solution.py:28
  65.6 0.0 collective-permute-done.22.refs_3_
  65.6 1.5 %distances.11 = (f32[96,1024]{1,0:T(8,128)S(1)}, s16[112,1024]{1,0:T(8,128)(2,1)S(1)}) custom-call(bf16[96,1280]{1,0:T(8,128)(2,1)S(1)} %get-tuple-element.267.refs_5_.refs_0_, bf16[96,1280]{1,0:T(8,128)(2,1)S(1)} %collective-permute-done.20.refs_1_, bf16[96,1280]{1,0:T(8,128)(2,1)S(1)} %collective-permute-done.21.refs_2_, ...), custom_call_target="tpu_custom_call" | custom-call | flops 30000001024 | bytes 1024 | tf_op jit(solution)/shard_map/distances/pallas_call | solution.py:210
  67.2 1.3 %collective-permute-start.23 = (s16[112,1024]{1,0:T(8,128)(2,1)S(1)}, s16[112,1024]{1,0:T(8,128)(2,1)S(1)}, u32[]{:S(2)}, u32[]{:S(2)}) collective-permute-start(s16[112,1024]{1,0:T(8,128)(2,1)S(1)} %get-tuple-element.273), channel_id=1, source_target_pairs={{0,2},{2,0},{1,3},{3,1},{4,6},{6,4},{5,7},{7,5},{8,10},{10,8},{9,1... | collective-permute-start | bytes 688136 | tf_op jit(solution)/shard_map/ppermute | solution.py:28
  68.5 0.0 collective-permute-done.24
  68.5 0.3 collective-permute-start.25
  68.8 0.1 fusion.3
  68.9 0.2 copy.8.refs_2_.refs_8_
  69.1 2.8 %early_moments.5 = (f32[1024,1024]{1,0:T(8,128)S(1)}, f32[256,512]{1,0:T(8,128)S(1)}, f32[1,1024]{1,0:T(1,128)S(1)}, f32[4,1024]{1,0:T(4,128)S(1)}, f32[16,1024]{1,0:T(8,128)S(1)}) custom-call(s32[3]{0:T(128)S(1)} %pad_add_fusion.place_ref, f32[160,1024]{1,0:T(8,128)S(1)} %get-tuple-element.272.refs_5_.refs_0_, f32[96,1024]{1,0:T(8,128)S(1)} %get-tuple-element.274.refs_1_, ...), custom_call_target="tpu_custom_call" | custom-call | flops 1024 | bytes 1024 | tf_op jit(solution)/shard_map/early_moments/pallas_call | solution.py:289
  71.9 2.1 %collective-permute-done.25 = f32[16,512]{1,0:T(8,128)S(1)} collective-permute-done((f32[16,512]{1,0:T(8,128)S(1)}, f32[16,512]{1,0:T(8,128)S(1)}, u32[]{:S(2)}, u32[]{:S(2)}) %collective-permute-start.25) | collective-permute-done | bytes 32800 | tf_op jit(solution)/shard_map/ppermute | solution.py:28
  74.0 0.0 collective-permute-done.23.refs_1_
  74.0 0.0 collective-permute-done.19.refs_0_
  74.0 3.3 %late_moments.5 = (f32[264,1024]{1,0:T(8,128)S(1)}, f32[264,1024]{1,0:T(8,128)S(1)}, f32[512,512]{1,0:T(8,128)S(1)}, bf16[1024,288]{1,0:T(8,128)(2,1)S(1)}, bf16...) custom-call(s32[3]{0:T(128)S(1)} %pad_add_fusion.place_ref, ...), custom_call_target="tpu_custom_call" | custom-call | flops 1024 | bytes 1024 | tf_op jit(solution)/shard_map/late_moments/pallas_call | solution.py:422
  77.4 2.1 %collective-permute-start.26 = (f32[264,1024]{1,0:T(8,128)S(1)}, f32[264,1024]{1,0:T(8,128)S(1)}, u32[]{:S(2)}, u32[]{:S(2)}) collective-permute-start(f32[264,1024]{1,0:T(8,128)S(1)} %get-tuple-element.282), channel_id=1, source_target_pairs={{0,1},{1,0},{2,3},{3,2},{4,5},{5,4},{6,7},{7,6},{8,9},{9,8},{10,11... | collective-permute-start | bytes 3244040 | tf_op jit(solution)/shard_map/ppermute | solution.py:28
  79.4 2.3 %rest_moments.5 = (f32[256,1024]{1,0:T(8,128)S(1)}, f32[256,1024]{1,0:T(8,128)S(1)}) custom-call(s32[3]{0:T(128)S(1)} %pad_add_fusion.place_ref, f32[1024,1024]{1,0:T(8,128)S(1)} %get-tuple-element.276.refs_2_.before_ref, bf16[1024,288]{1,0:T(8,128)(2,1)S(1)} %get-tuple-element.285.left_high, bf16[1024,288]{1,0:T(8,128)(2,1)S(1)} %get-tuple-element.286.left_low, ...), custom_call_target="tpu_custom_call" | custom-call | flops 1024 | bytes 1024 | tf_op jit(solution)/shard_map/rest_moments/pallas_call | solution.py:455
  81.8 0.1 collective-permute-start.27
  81.8 0.0 collective-permute-done.26.refs_1_
  81.8 1.5 %first_share.5 = (s16[144,1024]{1,0:T(8,128)(2,1)S(1)}, s16[144,1024]{1,0:T(8,128)(2,1)S(1)}, s16[16,1024]{1,0:T(8,128)(2,1)S(1)}, f32[8,1024]{1,0:T(8,128)S(1)}) custom-call(s32[3]{0:T(128)S(1)} %pad_add_fusion.place_ref, f32[264,1024]{1,0:T(8,128)S(1)} %get-tuple-element.281.refs_0_, f32[264,1024]{1,0:T(8,128)S(1)} %collective-permute-done.26.refs_1_), custom_call_target="tpu_custom_call" | custom-call | flops 1024 | bytes 1024 | tf_op jit(solution)/shard_map/first_share/pallas_call | solution.py:550
  83.3 3.2 %collective-permute-start.28 = (s16[144,1024]{1,0:T(8,128)(2,1)S(1)}, s16[144,1024]{1,0:T(8,128)(2,1)S(1)}, u32[]{:S(2)}, u32[]{:S(2)}) collective-permute-start(s16[144,1024]{1,0:T(8,128)(2,1)S(1)} %get-tuple-element.292), channel_id=1, source_target_pairs={{0,8},{4,12},{8,0},{12,4},{1,9},{5,13},{9,1},{13,5},{2,10},{6,14},... | collective-permute-start | bytes 884744 | tf_op jit(solution)/shard_map/ppermute | solution.py:28
  86.5 0.0 collective-permute-start.29
  86.5 1.1 rest_share.5
  87.6 0.0 copy-start
  87.6 0.0 copy-start.1
  87.6 1.5 %collective-permute-start.30 = (s16[144,1024]{1,0:T(8,128)(2,1)S(1)}, s16[144,1024]{1,0:T(8,128)(2,1)S(1)}, u32[]{:S(2)}, u32[]{:S(2)}) collective-permute-start(s16[144,1024]{1,0:T(8,128)(2,1)S(1)} %get-tuple-element.294), channel_id=1, source_target_pairs={{0,12},{4,0},{8,4},{12,8},{1,13},{5,1},{9,5},{13,9},{2,14},{6,2},{... | collective-permute-start | bytes 884744 | tf_op jit(solution)/shard_map/ppermute | solution.py:28
  89.2 8.8 %collective-permute-done.28.refs_0_ = s16[144,1024]{1,0:T(8,128)(2,1)S(1)} collective-permute-done((s16[144,1024]{1,0:T(8,128)(2,1)S(1)}, s16[144,1024]{1,0:T(8,128)(2,1)S(1)}, u32[]{:S(2)}, u32[]{:S(2)}) %collective-permute-start.28) | collective-permute-done | bytes 294944 | tf_op jit(solution)/shard_map/ppermute | solution.py:28
  97.9 12.3 %collective-permute-done.29.refs_1_ = s16[144,1024]{1,0:T(8,128)(2,1)S(1)} collective-permute-done((s16[144,1024]{1,0:T(8,128)(2,1)S(1)}, s16[144,1024]{1,0:T(8,128)(2,1)S(1)}, u32[]{:S(2)}, u32[]{:S(2)}) %collective-permute-start.29) | collective-permute-done | bytes 294944 | tf_op jit(solution)/shard_map/ppermute | solution.py:28
  110.2 1.0 collective-permute-done.30.refs_2_
  111.2 2.8 %finish.5 = (f32[128,512]{1,0:T(8,128)}, f32[128,512]{1,0:T(8,128)}, f32[512,512]{1,0:T(8,128)}) custom-call(s32[3]{0:T(128)S(1)} %pad_add_fusion.place_ref, f32[128,1024]{1,0:T(8,128)S(1)} %get-tuple-element.291.kept_ref, s16[16,1024]{1,0:T(8,128)(2,1)S(1)} %get-tuple-element.284.codes_ref, s16[144,1024]{1,0:T(8,128)(2,1)S(1)} %collective-permute-done.28.refs_0_, ...), custom_call_target="tpu_custom_call" | custom-call | flops 1024 | bytes 1024 | tf_op jit(solution)/shard_map/finish/pallas_call | solution.py:661
  (8 shorter events, 0.0 us)
Async XLA Ops:
  0.6 2.7 %collective-permute-start.15 = (s32[2,512]{1,0:T(2,128)}, s32[2,512]{1,0:T(2,128)S(1)}, u32[]{:S(2)}, u32[]{:S(2)}) collective-permute-start(s32[2,512]{1,0:T(2,128)} %refs_0_.1), channel_id=1, source_target_pairs={{0,2},{2,0},{1,3},{3,1},{4,6},{6,4},{5,7},{7,5},{8,10},{10,8},{9,1... | collective-permute-start | bytes 12296 | tf_op jit(solution)/shard_map/ppermute | solution.py:28
  6.7 48.4 %collective-permute-start.17 = (bf16[160,1280]{1,0:T(8,128)(2,1)S(1)}, bf16[160,1280]{1,0:T(8,128)(2,1)S(1)}, u32[]{:S(2)}, u32[]{:S(2)}) collective-permute-start(bf16[160,1280]{1,0:T(8,128)(2,1)S(1)} %get-tuple-element.256.after_ref), channel_id=1, source_target_pairs={{0,8},{4,12},{8,0},{12,4},{1,9},{5,13},{9,1},{13,5},{2,10},{6,14},... | collective-permute-start | bytes 1228808 | tf_op jit(solution)/shard_map/ppermute | solution.py:28
  10.5 44.6 %collective-permute-start.16 = (bf16[160,1280]{1,0:T(8,128)(2,1)S(1)}, bf16[160,1280]{1,0:T(8,128)(2,1)S(1)}, u32[]{:S(2)}, u32[]{:S(2)}) collective-permute-start(bf16[160,1280]{1,0:T(8,128)(2,1)S(1)} %get-tuple-element.263), channel_id=1, source_target_pairs={{0,4},{4,8},{8,12},{12,0},{1,5},{5,9},{9,13},{13,1},{2,6},{6,10},{... | collective-permute-start | bytes 1228808 | tf_op jit(solution)/shard_map/ppermute | solution.py:28
  10.6 44.5 %collective-permute-start.18 = (bf16[160,1280]{1,0:T(8,128)(2,1)S(1)}, bf16[160,1280]{1,0:T(8,128)(2,1)S(1)}, u32[]{:S(2)}, u32[]{:S(2)}) collective-permute-start(bf16[160,1280]{1,0:T(8,128)(2,1)S(1)} %get-tuple-element.264), channel_id=1, source_target_pairs={{0,12},{4,0},{8,4},{12,8},{1,13},{5,1},{9,5},{13,9},{2,14},{6,2},{... | collective-permute-start | bytes 1228808 | tf_op jit(solution)/shard_map/ppermute | solution.py:28
  19.0 41.9 %collective-permute-start.20 = (bf16[96,1280]{1,0:T(8,128)(2,1)S(1)}, bf16[96,1280]{1,0:T(8,128)(2,1)S(1)}, u32[]{:S(2)}, u32[]{:S(2)}) collective-permute-start(bf16[96,1280]{1,0:T(8,128)(2,1)S(1)} %get-tuple-element.269), channel_id=1, source_target_pairs={{0,4},{4,8},{8,12},{12,0},{1,5},{5,9},{9,13},{13,1},{2,6},{6,10},{... | collective-permute-start | bytes 737288 | tf_op jit(solution)/shard_map/ppermute | solution.py:28
  19.2 46.5 %collective-permute-start.21 = (bf16[96,1280]{1,0:T(8,128)(2,1)S(1)}, bf16[96,1280]{1,0:T(8,128)(2,1)S(1)}, u32[]{:S(2)}, u32[]{:S(2)}) collective-permute-start(bf16[96,1280]{1,0:T(8,128)(2,1)S(1)} %get-tuple-element.270), channel_id=1, source_target_pairs={{0,8},{4,12},{8,0},{12,4},{1,9},{5,13},{9,1},{13,5},{2,10},{6,14},... | collective-permute-start | bytes 737288 | tf_op jit(solution)/shard_map/ppermute | solution.py:28
  55.1 10.5 %collective-permute-start.22 = (bf16[96,1280]{1,0:T(8,128)(2,1)S(1)}, bf16[96,1280]{1,0:T(8,128)(2,1)S(1)}, u32[]{:S(2)}, u32[]{:S(2)}) collective-permute-start(bf16[96,1280]{1,0:T(8,128)(2,1)S(1)} %get-tuple-element.271), channel_id=1, source_target_pairs={{0,12},{4,0},{8,4},{12,8},{1,13},{5,1},{9,5},{13,9},{2,14},{6,2},{... | collective-permute-start | bytes 737288 | tf_op jit(solution)/shard_map/ppermute | solution.py:28
  57.5 16.5 %collective-permute-start.19 = (s16[176,1024]{1,0:T(8,128)(2,1)S(1)}, s16[176,1024]{1,0:T(8,128)(2,1)S(1)}, u32[]{:S(2)}, u32[]{:S(2)}) collective-permute-start(s16[176,1024]{1,0:T(8,128)(2,1)S(1)} %get-tuple-element.268), channel_id=1, source_target_pairs={{0,2},{2,0},{1,3},{3,1},{4,6},{6,4},{5,7},{7,5},{8,10},{10,8},{9,1... | collective-permute-start | bytes 1081352 | tf_op jit(solution)/shard_map/ppermute | solution.py:28
  58.8 9.7 %collective-permute-start.24 = (f32[16,1024]{1,0:T(8,128)S(1)}, f32[16,1024]{1,0:T(8,128)S(1)}, u32[]{:S(2)}, u32[]{:S(2)}) collective-permute-start(f32[16,1024]{1,0:T(8,128)S(1)} %slice.22), channel_id=1, source_target_pairs={{4,0},{8,4},{12,8},{5,1},{9,5},{13,9},{6,2},{10,6},{14,10},{7,3},{... | collective-permute-start | bytes 196616 | tf_op jit(solution)/shard_map/ppermute | solution.py:37
  67.2 6.8 %collective-permute-start.23 = (s16[112,1024]{1,0:T(8,128)(2,1)S(1)}, s16[112,1024]{1,0:T(8,128)(2,1)S(1)}, u32[]{:S(2)}, u32[]{:S(2)}) collective-permute-start(s16[112,1024]{1,0:T(8,128)(2,1)S(1)} %get-tuple-element.273), channel_id=1, source_target_pairs={{0,2},{2,0},{1,3},{3,1},{4,6},{6,4},{5,7},{7,5},{8,10},{10,8},{9,1... | collective-permute-start | bytes 688136 | tf_op jit(solution)/shard_map/ppermute | solution.py:28
  68.5 5.5 %collective-permute-start.25 = (f32[16,512]{1,0:T(8,128)S(1)}, f32[16,512]{1,0:T(8,128)S(1)}, u32[]{:S(2)}, u32[]{:S(2)}) collective-permute-start(f32[16,512]{1,0:T(8,128)S(1)} %dynamic-slice_add_fusion.1), channel_id=1, source_target_pairs={{0,2},{2,0},{1,3},{3,1},{4,6},{6,4},{5,7},{7,5},{8,10},{10,8},{9,1... | collective-permute-start | bytes 98312 | tf_op jit(solution)/shard_map/ppermute | solution.py:28
  77.4 4.5 %collective-permute-start.26 = (f32[264,1024]{1,0:T(8,128)S(1)}, f32[264,1024]{1,0:T(8,128)S(1)}, u32[]{:S(2)}, u32[]{:S(2)}) collective-permute-start(f32[264,1024]{1,0:T(8,128)S(1)} %get-tuple-element.282), channel_id=1, source_target_pairs={{0,1},{1,0},{2,3},{3,2},{4,5},{5,4},{6,7},{7,6},{8,9},{9,8},{10,11... | collective-permute-start | bytes 3244040 | tf_op jit(solution)/shard_map/ppermute | solution.py:28
  81.8 4.7 %collective-permute-start.27 = (f32[256,1024]{1,0:T(8,128)S(1)}, f32[256,1024]{1,0:T(8,128)S(1)}, u32[]{:S(2)}, u32[]{:S(2)}) collective-permute-start(f32[256,1024]{1,0:T(8,128)S(1)} %get-tuple-element.290), channel_id=1, source_target_pairs={{0,1},{1,0},{2,3},{3,2},{4,5},{5,4},{6,7},{7,6},{8,9},{9,8},{10,11... | collective-permute-start | bytes 3145736 | tf_op jit(solution)/shard_map/ppermute | solution.py:28
  83.3 14.6 %collective-permute-start.28 = (s16[144,1024]{1,0:T(8,128)(2,1)S(1)}, s16[144,1024]{1,0:T(8,128)(2,1)S(1)}, u32[]{:S(2)}, u32[]{:S(2)}) collective-permute-start(s16[144,1024]{1,0:T(8,128)(2,1)S(1)} %get-tuple-element.292), channel_id=1, source_target_pairs={{0,8},{4,12},{8,0},{12,4},{1,9},{5,13},{9,1},{13,5},{2,10},{6,14},... | collective-permute-start | bytes 884744 | tf_op jit(solution)/shard_map/ppermute | solution.py:28
  86.5 23.8 %collective-permute-start.29 = (s16[144,1024]{1,0:T(8,128)(2,1)S(1)}, s16[144,1024]{1,0:T(8,128)(2,1)S(1)}, u32[]{:S(2)}, u32[]{:S(2)}) collective-permute-start(s16[144,1024]{1,0:T(8,128)(2,1)S(1)} %get-tuple-element.293), channel_id=1, source_target_pairs={{0,4},{4,8},{8,12},{12,0},{1,5},{5,9},{9,13},{13,1},{2,6},{6,10},{... | collective-permute-start | bytes 884744 | tf_op jit(solution)/shard_map/ppermute | solution.py:28
  87.6 26.5 %copy-start = (s32[1,2048]{1,0:T(1,128)S(1)}, s32[1,2048]{1,0:T(1,128)}, u32[]{:S(2)}) copy-start(s32[1,2048]{1,0:T(1,128)} %ids_ref.1) | copy-start | bytes 24580
  87.6 26.5 %copy-start.1 = (s32[2,512]{1,0:T(2,128)S(1)}, s32[2,512]{1,0:T(2,128)}, u32[]{:S(2)}) copy-start(s32[2,512]{1,0:T(2,128)} %refs_0_.1) | copy-start | bytes 12292
  87.6 23.6 %collective-permute-start.30 = (s16[144,1024]{1,0:T(8,128)(2,1)S(1)}, s16[144,1024]{1,0:T(8,128)(2,1)S(1)}, u32[]{:S(2)}, u32[]{:S(2)}) collective-permute-start(s16[144,1024]{1,0:T(8,128)(2,1)S(1)} %get-tuple-element.294), channel_id=1, source_target_pairs={{0,12},{4,0},{8,4},{12,8},{1,13},{5,1},{9,5},{13,9},{2,14},{6,2},{... | collective-permute-start | bytes 884744 | tf_op jit(solution)/shard_map/ppermute | solution.py:28

commit v8 on v7

--- a/solution.py
+++ b/solution.py
@@ -30,7 +30,7 @@
 
 def shifts_of(axis):
     size = lax.axis_size(axis)
-    return sorted(range(1, size), key=lambda s: -min(s, size - s))
+    return sorted(range(1, size), key=lambda s: (-min(s, size - s), -s))
 
 
 def passed_down(block, axis):

time: 115 us -> 115 us (level)
  transfers between devices with their start and end apart: 16 -> 16, of which waited for: 7 -> 6; matrix products, arithmetic and copies ran while one was open for 0% -> 0% of each run, Pallas kernels for 17% -> 17%
where the time goes in v8:
time: 115 us; the launch traced here: 114 us
  waiting for transfers between devices  62.2 us (54%)
  Pallas kernels  29.5 us (26%)
  starting transfers between devices  21.2 us (18%)
    ppermute x15, waiting for transfers between devices, rotated(): lax.ppermute(block, axis, [(i, (i + shift) % size) for i in range(size)])  62.2 us
    ppermute x15, starting transfers between devices, rotated(): lax.ppermute(block, axis, [(i, (i + shift) % size) for i in range(size)])  19 us
    pallas_call x1, Pallas kernels, pair_signs(): pl.pallas_call(functools.partial(signs_kernel, groups, width, slot_rows(c...  5.84 us
    pallas_call x2, Pallas kernels, distances(): pl.pallas_call(functools.partial(distance_kernel, cap), in_specs=[vmem] *...  3.88 us
    pallas_call x1, Pallas kernels, first_pick(): pl.pallas_call(functools.partial(first_pick_kernel, len(pairs), near, far...  3.38 us
    pallas_call x1, Pallas kernels, late_moments(): pl.pallas_call(functools.partial(late_kernel, sizes, sides, groups, reps,...  3.33 us
    pallas_call x1, Pallas kernels, finish(): pl.pallas_call(functools.partial(finish_kernel, reps), in_specs=[pl.Block...  2.83 us
    pallas_call x1, Pallas kernels, early_moments(): pl.pallas_call(functools.partial(early_kernel, len(pieces), sides), in_sp...  2.8 us
  transfers between devices with their start and end apart: 16, of which 6 were waited for; matrix products, arithmetic and copies ran while one was open for 0% of the time, Pallas kernels for 17%

profile of v8, /device:TPU:9, one launch (start us, length us, event | category | flops | bytes accessed | tf_op | source)
XLA Modules:
  0.0 114.1 jit_solution(13470804008868615574)
XLA Ops:
  0.6 1.3 %collective-permute-start.15 = (s32[2,512]{1,0:T(2,128)}, s32[2,512]{1,0:T(2,128)S(1)}, u32[]{:S(2)}, u32[]{:S(2)}) collective-permute-start(s32[2,512]{1,0:T(2,128)} %refs_0_.1), channel_id=1, source_target_pairs={{0,2},{2,0},{1,3},{3,1},{4,6},{6,4},{5,7},{7,5},{8,10},{10,8},{9,1... | collective-permute-start | bytes 12296 | tf_op jit(solution)/shard_map/ppermute | solution.py:28
  1.9 0.1 pad_add_fusion.place_ref
  2.0 1.4 %collective-permute-done.15.refs_1_ = s32[2,512]{1,0:T(2,128)S(1)} collective-permute-done((s32[2,512]{1,0:T(2,128)}, s32[2,512]{1,0:T(2,128)S(1)}, u32[]{:S(2)}, u32[]{:S(2)}) %collective-permute-start.15) | collective-permute-done | bytes 4128 | tf_op jit(solution)/shard_map/ppermute | solution.py:28
  3.4 3.4 %first_pick.5 = (bf16[768,426]{1,0:T(8,128)(2,1)S(1)}, s32[1,2048]{1,0:T(1,128)S(1)}, s32[2,512]{1,0:T(2,128)S(1)}, s32[2,512]{1,0:T(2,128)S(1)}, bf16[3,3,160,7...) custom-call(s32[3]{0:T(128)S(1)} %pad_add_fusion.place_ref, ...), custom_call_target="tpu_custom_call" | custom-call | flops 1024 | bytes 1024 | tf_op jit(solution)/shard_map/first_pick/pallas_call | solution.py:107
  6.7 2.4 %collective-permute-start.17 = (bf16[160,1280]{1,0:T(8,128)(2,1)S(1)}, bf16[160,1280]{1,0:T(8,128)(2,1)S(1)}, u32[]{:S(2)}, u32[]{:S(2)}) collective-permute-start(bf16[160,1280]{1,0:T(8,128)(2,1)S(1)} %get-tuple-element.256.after_ref), channel_id=1, source_target_pairs={{0,8},{4,12},{8,0},{12,4},{1,9},{5,13},{9,1},{13,5},{2,10},{6,14},... | collective-permute-start | bytes 1228808 | tf_op jit(solution)/shard_map/ppermute | solution.py:28
  9.1 1.4 %pick.10 = (bf16[160,1280]{1,0:T(8,128)(2,1)S(1)}, bf16[160,1280]{1,0:T(8,128)(2,1)S(1)}, bf16[160,1280]{1,0:T(8,128)(2,1)S(1)}) custom-call(bf16[768,426]{1,0:T(8,128)(2,1)S(1)} %get-tuple-element.260.chosen_ref, bf16[160,1280]{1,0:T(8,128)(2,1)S(1)} %get-tuple-element.256.after_ref, bf16[3,3,160,768]{3,2,1,0:T(8,128)(2,1)S(1)} %get-tuple-element.261.refs_0_), custom_call_target="tpu_custom_call" | custom-call | flops 1024 | bytes 1024 | tf_op jit(solution)/shard_map/pick/pallas_call | solution.py:148
  10.5 0.1 collective-permute-start.16
  10.6 1.5 %collective-permute-start.18 = (bf16[160,1280]{1,0:T(8,128)(2,1)S(1)}, bf16[160,1280]{1,0:T(8,128)(2,1)S(1)}, u32[]{:S(2)}, u32[]{:S(2)}) collective-permute-start(bf16[160,1280]{1,0:T(8,128)(2,1)S(1)} %get-tuple-element.264), channel_id=1, source_target_pairs={{0,12},{4,0},{8,4},{12,8},{1,13},{5,1},{9,5},{13,9},{2,14},{6,2},{... | collective-permute-start | bytes 1228808 | tf_op jit(solution)/shard_map/ppermute | solution.py:28
  12.0 5.8 %pair_signs.5 = (bf16[1728,1024]{1,0:T(8,128)(2,1)S(1)}, f32[1,128]{1,0:T(1,128)S(1)}) custom-call(s32[3]{0:T(128)S(1)} %pad_add_fusion.place_ref, bf16[160,1280]{1,0:T(8,128)(2,1)S(1)} %get-tuple-element.256.after_ref, s32[2,512]{1,0:T(2,128)S(1)} %get-tuple-element.257.refs_0_, s32[2,512]{1,0:T(2,128)S(1)} %get-tuple-element.258.refs_1_), custom_call_target="tpu_custom_call" | custom-call | flops 30000001024 | bytes 1024 | tf_op jit(solution)/shard_map/pair_signs/pallas_call | solution.py:727
  17.9 1.2 %pick.11 = (bf16[96,1280]{1,0:T(8,128)(2,1)S(1)}, bf16[96,1280]{1,0:T(8,128)(2,1)S(1)}, bf16[96,1280]{1,0:T(8,128)(2,1)S(1)}, bf16[96,1280]{1,0:T(8,128)(2,1)S(1)}) custom-call(bf16[768,426]{1,0:T(8,128)(2,1)S(1)} %get-tuple-element.260.chosen_ref, f32[1,128]{1,0:T(1,128)S(1)} %get-tuple-element.259.after_ref, ...), custom_call_target="tpu_custom_call" | custom-call | flops 1024 | bytes 1024 | tf_op jit(solution)/shard_map/pick/pallas_call | solution.py:148
  19.0 0.1 collective-permute-start.20
  19.2 4.0 %collective-permute-start.21 = (bf16[96,1280]{1,0:T(8,128)(2,1)S(1)}, bf16[96,1280]{1,0:T(8,128)(2,1)S(1)}, u32[]{:S(2)}, u32[]{:S(2)}) collective-permute-start(bf16[96,1280]{1,0:T(8,128)(2,1)S(1)} %get-tuple-element.270), channel_id=1, source_target_pairs={{0,8},{4,12},{8,0},{12,4},{1,9},{5,13},{9,1},{13,5},{2,10},{6,14},... | collective-permute-start | bytes 737288 | tf_op jit(solution)/shard_map/ppermute | solution.py:28
  23.1 32.0 %collective-permute-done.16.refs_1_ = bf16[160,1280]{1,0:T(8,128)(2,1)S(1)} collective-permute-done((bf16[160,1280]{1,0:T(8,128)(2,1)S(1)}, bf16[160,1280]{1,0:T(8,128)(2,1)S(1)}, u32[]{:S(2)}, u32[]{:S(2)}) %collective-permute-start.16) | collective-permute-done | bytes 409632 | tf_op jit(solution)/shard_map/ppermute | solution.py:28
  55.1 0.0 collective-permute-start.22
  55.1 0.0 collective-permute-done.17.refs_2_
  55.1 0.0 collective-permute-done.18.refs_3_
  55.1 2.4 %distances.10 = (f32[160,1024]{1,0:T(8,128)S(1)}, s16[176,1024]{1,0:T(8,128)(2,1)S(1)}) custom-call(bf16[160,1280]{1,0:T(8,128)(2,1)S(1)} %get-tuple-element.262.refs_0_, bf16[160,1280]{1,0:T(8,128)(2,1)S(1)} %collective-permute-done.16.refs_1_, bf16[160,1280]{1,0:T(8,128)(2,1)S(1)} %collective-permute-done.17.refs_2_, ...), custom_call_target="tpu_custom_call" | custom-call | flops 30000001024 | bytes 1024 | tf_op jit(solution)/shard_map/distances/pallas_call | solution.py:210
  57.5 1.3 %collective-permute-start.19 = (s16[176,1024]{1,0:T(8,128)(2,1)S(1)}, s16[176,1024]{1,0:T(8,128)(2,1)S(1)}, u32[]{:S(2)}, u32[]{:S(2)}) collective-permute-start(s16[176,1024]{1,0:T(8,128)(2,1)S(1)} %get-tuple-element.268), channel_id=1, source_target_pairs={{0,2},{2,0},{1,3},{3,1},{4,6},{6,4},{5,7},{7,5},{8,10},{10,8},{9,1... | collective-permute-start | bytes 1081352 | tf_op jit(solution)/shard_map/ppermute | solution.py:28
  58.8 2.2 %collective-permute-start.24 = (f32[16,1024]{1,0:T(8,128)S(1)}, f32[16,1024]{1,0:T(8,128)S(1)}, u32[]{:S(2)}, u32[]{:S(2)}) collective-permute-start(f32[16,1024]{1,0:T(8,128)S(1)} %slice.22), channel_id=1, source_target_pairs={{4,0},{8,4},{12,8},{5,1},{9,5},{13,9},{6,2},{10,6},{14,10},{7,3},{... | collective-permute-start | bytes 196616 | tf_op jit(solution)/shard_map/ppermute | solution.py:37
  61.0 0.0 collective-permute-done.20.refs_1_
  61.0 4.7 %collective-permute-done.21.refs_2_ = bf16[96,1280]{1,0:T(8,128)(2,1)S(1)} collective-permute-done((bf16[96,1280]{1,0:T(8,128)(2,1)S(1)}, bf16[96,1280]{1,0:T(8,128)(2,1)S(1)}, u32[]{:S(2)}, u32[]{:S(2)}) %collective-permute-start.21) | collective-permute-done | bytes 245792 | tf_op jit(solution)/shard_map/ppermute | solution.py:28
  65.6 0.0 collective-permute-done.22.refs_3_
  65.6 1.5 %distances.11 = (f32[96,1024]{1,0:T(8,128)S(1)}, s16[112,1024]{1,0:T(8,128)(2,1)S(1)}) custom-call(bf16[96,1280]{1,0:T(8,128)(2,1)S(1)} %get-tuple-element.267.refs_5_.refs_0_, bf16[96,1280]{1,0:T(8,128)(2,1)S(1)} %collective-permute-done.20.refs_1_, bf16[96,1280]{1,0:T(8,128)(2,1)S(1)} %collective-permute-done.21.refs_2_, ...), custom_call_target="tpu_custom_call" | custom-call | flops 30000001024 | bytes 1024 | tf_op jit(solution)/shard_map/distances/pallas_call | solution.py:210
  67.2 1.3 %collective-permute-start.23 = (s16[112,1024]{1,0:T(8,128)(2,1)S(1)}, s16[112,1024]{1,0:T(8,128)(2,1)S(1)}, u32[]{:S(2)}, u32[]{:S(2)}) collective-permute-start(s16[112,1024]{1,0:T(8,128)(2,1)S(1)} %get-tuple-element.273), channel_id=1, source_target_pairs={{0,2},{2,0},{1,3},{3,1},{4,6},{6,4},{5,7},{7,5},{8,10},{10,8},{9,1... | collective-permute-start | bytes 688136 | tf_op jit(solution)/shard_map/ppermute | solution.py:28
  68.5 0.0 collective-permute-done.24
  68.5 0.3 collective-permute-start.25
  68.8 0.1 fusion.3
  68.9 0.2 copy.8.refs_2_.refs_8_
  69.1 2.8 %early_moments.5 = (f32[1024,1024]{1,0:T(8,128)S(1)}, f32[256,512]{1,0:T(8,128)S(1)}, f32[1,1024]{1,0:T(1,128)S(1)}, f32[4,1024]{1,0:T(4,128)S(1)}, f32[16,1024]{1,0:T(8,128)S(1)}) custom-call(s32[3]{0:T(128)S(1)} %pad_add_fusion.place_ref, f32[160,1024]{1,0:T(8,128)S(1)} %get-tuple-element.272.refs_5_.refs_0_, f32[96,1024]{1,0:T(8,128)S(1)} %get-tuple-element.274.refs_1_, ...), custom_call_target="tpu_custom_call" | custom-call | flops 1024 | bytes 1024 | tf_op jit(solution)/shard_map/early_moments/pallas_call | solution.py:289
  71.9 2.1 %collective-permute-done.25 = f32[16,512]{1,0:T(8,128)S(1)} collective-permute-done((f32[16,512]{1,0:T(8,128)S(1)}, f32[16,512]{1,0:T(8,128)S(1)}, u32[]{:S(2)}, u32[]{:S(2)}) %collective-permute-start.25) | collective-permute-done | bytes 32800 | tf_op jit(solution)/shard_map/ppermute | solution.py:28
  74.0 0.0 collective-permute-done.23.refs_1_
  74.0 0.0 collective-permute-done.19.refs_0_
  74.0 3.3 %late_moments.5 = (f32[264,1024]{1,0:T(8,128)S(1)}, f32[264,1024]{1,0:T(8,128)S(1)}, f32[512,512]{1,0:T(8,128)S(1)}, bf16[1024,288]{1,0:T(8,128)(2,1)S(1)}, bf16...) custom-call(s32[3]{0:T(128)S(1)} %pad_add_fusion.place_ref, ...), custom_call_target="tpu_custom_call" | custom-call | flops 1024 | bytes 1024 | tf_op jit(solution)/shard_map/late_moments/pallas_call | solution.py:422
  77.4 2.1 %collective-permute-start.26 = (f32[264,1024]{1,0:T(8,128)S(1)}, f32[264,1024]{1,0:T(8,128)S(1)}, u32[]{:S(2)}, u32[]{:S(2)}) collective-permute-start(f32[264,1024]{1,0:T(8,128)S(1)} %get-tuple-element.282), channel_id=1, source_target_pairs={{0,1},{1,0},{2,3},{3,2},{4,5},{5,4},{6,7},{7,6},{8,9},{9,8},{10,11... | collective-permute-start | bytes 3244040 | tf_op jit(solution)/shard_map/ppermute | solution.py:28
  79.4 2.3 %rest_moments.5 = (f32[256,1024]{1,0:T(8,128)S(1)}, f32[256,1024]{1,0:T(8,128)S(1)}) custom-call(s32[3]{0:T(128)S(1)} %pad_add_fusion.place_ref, f32[1024,1024]{1,0:T(8,128)S(1)} %get-tuple-element.276.refs_2_.before_ref, bf16[1024,288]{1,0:T(8,128)(2,1)S(1)} %get-tuple-element.285.left_high, bf16[1024,288]{1,0:T(8,128)(2,1)S(1)} %get-tuple-element.286.left_low, ...), custom_call_target="tpu_custom_call" | custom-call | flops 1024 | bytes 1024 | tf_op jit(solution)/shard_map/rest_moments/pallas_call | solution.py:455
  81.8 0.1 collective-permute-start.27
  81.8 0.0 collective-permute-done.26.refs_1_
  81.8 1.5 %first_share.5 = (s16[144,1024]{1,0:T(8,128)(2,1)S(1)}, s16[144,1024]{1,0:T(8,128)(2,1)S(1)}, s16[16,1024]{1,0:T(8,128)(2,1)S(1)}, f32[8,1024]{1,0:T(8,128)S(1)}) custom-call(s32[3]{0:T(128)S(1)} %pad_add_fusion.place_ref, f32[264,1024]{1,0:T(8,128)S(1)} %get-tuple-element.281.refs_0_, f32[264,1024]{1,0:T(8,128)S(1)} %collective-permute-done.26.refs_1_), custom_call_target="tpu_custom_call" | custom-call | flops 1024 | bytes 1024 | tf_op jit(solution)/shard_map/first_share/pallas_call | solution.py:550
  83.3 3.2 %collective-permute-start.28 = (s16[144,1024]{1,0:T(8,128)(2,1)S(1)}, s16[144,1024]{1,0:T(8,128)(2,1)S(1)}, u32[]{:S(2)}, u32[]{:S(2)}) collective-permute-start(s16[144,1024]{1,0:T(8,128)(2,1)S(1)} %get-tuple-element.292), channel_id=1, source_target_pairs={{0,8},{4,12},{8,0},{12,4},{1,9},{5,13},{9,1},{13,5},{2,10},{6,14},... | collective-permute-start | bytes 884744 | tf_op jit(solution)/shard_map/ppermute | solution.py:28
  86.5 0.0 collective-permute-start.29
  86.5 0.0 collective-permute-done.27.refs_1_
  86.5 1.1 rest_share.5
  87.6 0.0 copy-start
  87.6 0.0 copy-start.1
  87.6 1.5 %collective-permute-start.30 = (s16[144,1024]{1,0:T(8,128)(2,1)S(1)}, s16[144,1024]{1,0:T(8,128)(2,1)S(1)}, u32[]{:S(2)}, u32[]{:S(2)}) collective-permute-start(s16[144,1024]{1,0:T(8,128)(2,1)S(1)} %get-tuple-element.294), channel_id=1, source_target_pairs={{0,4},{4,8},{8,12},{12,0},{1,5},{5,9},{9,13},{13,1},{2,6},{6,10},{... | collective-permute-start | bytes 884744 | tf_op jit(solution)/shard_map/ppermute | solution.py:28
  89.2 14.7 %collective-permute-done.28.refs_0_ = s16[144,1024]{1,0:T(8,128)(2,1)S(1)} collective-permute-done((s16[144,1024]{1,0:T(8,128)(2,1)S(1)}, s16[144,1024]{1,0:T(8,128)(2,1)S(1)}, u32[]{:S(2)}, u32[]{:S(2)}) %collective-permute-start.28) | collective-permute-done | bytes 294944 | tf_op jit(solution)/shard_map/ppermute | solution.py:28
  103.9 7.3 %collective-permute-done.29.refs_1_ = s16[144,1024]{1,0:T(8,128)(2,1)S(1)} collective-permute-done((s16[144,1024]{1,0:T(8,128)(2,1)S(1)}, s16[144,1024]{1,0:T(8,128)(2,1)S(1)}, u32[]{:S(2)}, u32[]{:S(2)}) %collective-permute-start.29) | collective-permute-done | bytes 294944 | tf_op jit(solution)/shard_map/ppermute | solution.py:28
  111.2 2.8 %finish.5 = (f32[128,512]{1,0:T(8,128)}, f32[128,512]{1,0:T(8,128)}, f32[512,512]{1,0:T(8,128)}) custom-call(s32[3]{0:T(128)S(1)} %pad_add_fusion.place_ref, f32[128,1024]{1,0:T(8,128)S(1)} %get-tuple-element.291.kept_ref, s16[16,1024]{1,0:T(8,128)(2,1)S(1)} %get-tuple-element.284.codes_ref, s16[144,1024]{1,0:T(8,128)(2,1)S(1)} %collective-permute-done.28.refs_0_, ...), custom_call_target="tpu_custom_call" | custom-call | flops 1024 | bytes 1024 | tf_op jit(solution)/shard_map/finish/pallas_call | solution.py:661
  (8 shorter events, 0.0 us)
Async XLA Ops:
  0.6 2.7 %collective-permute-start.15 = (s32[2,512]{1,0:T(2,128)}, s32[2,512]{1,0:T(2,128)S(1)}, u32[]{:S(2)}, u32[]{:S(2)}) collective-permute-start(s32[2,512]{1,0:T(2,128)} %refs_0_.1), channel_id=1, source_target_pairs={{0,2},{2,0},{1,3},{3,1},{4,6},{6,4},{5,7},{7,5},{8,10},{10,8},{9,1... | collective-permute-start | bytes 12296 | tf_op jit(solution)/shard_map/ppermute | solution.py:28
  6.7 48.4 %collective-permute-start.17 = (bf16[160,1280]{1,0:T(8,128)(2,1)S(1)}, bf16[160,1280]{1,0:T(8,128)(2,1)S(1)}, u32[]{:S(2)}, u32[]{:S(2)}) collective-permute-start(bf16[160,1280]{1,0:T(8,128)(2,1)S(1)} %get-tuple-element.256.after_ref), channel_id=1, source_target_pairs={{0,8},{4,12},{8,0},{12,4},{1,9},{5,13},{9,1},{13,5},{2,10},{6,14},... | collective-permute-start | bytes 1228808 | tf_op jit(solution)/shard_map/ppermute | solution.py:28
  10.5 44.6 %collective-permute-start.16 = (bf16[160,1280]{1,0:T(8,128)(2,1)S(1)}, bf16[160,1280]{1,0:T(8,128)(2,1)S(1)}, u32[]{:S(2)}, u32[]{:S(2)}) collective-permute-start(bf16[160,1280]{1,0:T(8,128)(2,1)S(1)} %get-tuple-element.263), channel_id=1, source_target_pairs={{0,4},{4,8},{8,12},{12,0},{1,5},{5,9},{9,13},{13,1},{2,6},{6,10},{... | collective-permute-start | bytes 1228808 | tf_op jit(solution)/shard_map/ppermute | solution.py:28
  10.6 44.5 %collective-permute-start.18 = (bf16[160,1280]{1,0:T(8,128)(2,1)S(1)}, bf16[160,1280]{1,0:T(8,128)(2,1)S(1)}, u32[]{:S(2)}, u32[]{:S(2)}) collective-permute-start(bf16[160,1280]{1,0:T(8,128)(2,1)S(1)} %get-tuple-element.264), channel_id=1, source_target_pairs={{0,12},{4,0},{8,4},{12,8},{1,13},{5,1},{9,5},{13,9},{2,14},{6,2},{... | collective-permute-start | bytes 1228808 | tf_op jit(solution)/shard_map/ppermute | solution.py:28
  19.0 41.9 %collective-permute-start.20 = (bf16[96,1280]{1,0:T(8,128)(2,1)S(1)}, bf16[96,1280]{1,0:T(8,128)(2,1)S(1)}, u32[]{:S(2)}, u32[]{:S(2)}) collective-permute-start(bf16[96,1280]{1,0:T(8,128)(2,1)S(1)} %get-tuple-element.269), channel_id=1, source_target_pairs={{0,4},{4,8},{8,12},{12,0},{1,5},{5,9},{9,13},{13,1},{2,6},{6,10},{... | collective-permute-start | bytes 737288 | tf_op jit(solution)/shard_map/ppermute | solution.py:28
  19.2 46.5 %collective-permute-start.21 = (bf16[96,1280]{1,0:T(8,128)(2,1)S(1)}, bf16[96,1280]{1,0:T(8,128)(2,1)S(1)}, u32[]{:S(2)}, u32[]{:S(2)}) collective-permute-start(bf16[96,1280]{1,0:T(8,128)(2,1)S(1)} %get-tuple-element.270), channel_id=1, source_target_pairs={{0,8},{4,12},{8,0},{12,4},{1,9},{5,13},{9,1},{13,5},{2,10},{6,14},... | collective-permute-start | bytes 737288 | tf_op jit(solution)/shard_map/ppermute | solution.py:28
  55.1 10.5 %collective-permute-start.22 = (bf16[96,1280]{1,0:T(8,128)(2,1)S(1)}, bf16[96,1280]{1,0:T(8,128)(2,1)S(1)}, u32[]{:S(2)}, u32[]{:S(2)}) collective-permute-start(bf16[96,1280]{1,0:T(8,128)(2,1)S(1)} %get-tuple-element.271), channel_id=1, source_target_pairs={{0,12},{4,0},{8,4},{12,8},{1,13},{5,1},{9,5},{13,9},{2,14},{6,2},{... | collective-permute-start | bytes 737288 | tf_op jit(solution)/shard_map/ppermute | solution.py:28
  57.5 16.5 %collective-permute-start.19 = (s16[176,1024]{1,0:T(8,128)(2,1)S(1)}, s16[176,1024]{1,0:T(8,128)(2,1)S(1)}, u32[]{:S(2)}, u32[]{:S(2)}) collective-permute-start(s16[176,1024]{1,0:T(8,128)(2,1)S(1)} %get-tuple-element.268), channel_id=1, source_target_pairs={{0,2},{2,0},{1,3},{3,1},{4,6},{6,4},{5,7},{7,5},{8,10},{10,8},{9,1... | collective-permute-start | bytes 1081352 | tf_op jit(solution)/shard_map/ppermute | solution.py:28
  58.8 9.7 %collective-permute-start.24 = (f32[16,1024]{1,0:T(8,128)S(1)}, f32[16,1024]{1,0:T(8,128)S(1)}, u32[]{:S(2)}, u32[]{:S(2)}) collective-permute-start(f32[16,1024]{1,0:T(8,128)S(1)} %slice.22), channel_id=1, source_target_pairs={{4,0},{8,4},{12,8},{5,1},{9,5},{13,9},{6,2},{10,6},{14,10},{7,3},{... | collective-permute-start | bytes 196616 | tf_op jit(solution)/shard_map/ppermute | solution.py:37
  67.2 6.8 %collective-permute-start.23 = (s16[112,1024]{1,0:T(8,128)(2,1)S(1)}, s16[112,1024]{1,0:T(8,128)(2,1)S(1)}, u32[]{:S(2)}, u32[]{:S(2)}) collective-permute-start(s16[112,1024]{1,0:T(8,128)(2,1)S(1)} %get-tuple-element.273), channel_id=1, source_target_pairs={{0,2},{2,0},{1,3},{3,1},{4,6},{6,4},{5,7},{7,5},{8,10},{10,8},{9,1... | collective-permute-start | bytes 688136 | tf_op jit(solution)/shard_map/ppermute | solution.py:28
  68.5 5.5 %collective-permute-start.25 = (f32[16,512]{1,0:T(8,128)S(1)}, f32[16,512]{1,0:T(8,128)S(1)}, u32[]{:S(2)}, u32[]{:S(2)}) collective-permute-start(f32[16,512]{1,0:T(8,128)S(1)} %dynamic-slice_add_fusion.1), channel_id=1, source_target_pairs={{0,2},{2,0},{1,3},{3,1},{4,6},{6,4},{5,7},{7,5},{8,10},{10,8},{9,1... | collective-permute-start | bytes 98312 | tf_op jit(solution)/shard_map/ppermute | solution.py:28
  77.4 4.5 %collective-permute-start.26 = (f32[264,1024]{1,0:T(8,128)S(1)}, f32[264,1024]{1,0:T(8,128)S(1)}, u32[]{:S(2)}, u32[]{:S(2)}) collective-permute-start(f32[264,1024]{1,0:T(8,128)S(1)} %get-tuple-element.282), channel_id=1, source_target_pairs={{0,1},{1,0},{2,3},{3,2},{4,5},{5,4},{6,7},{7,6},{8,9},{9,8},{10,11... | collective-permute-start | bytes 3244040 | tf_op jit(solution)/shard_map/ppermute | solution.py:28
  81.8 4.7 %collective-permute-start.27 = (f32[256,1024]{1,0:T(8,128)S(1)}, f32[256,1024]{1,0:T(8,128)S(1)}, u32[]{:S(2)}, u32[]{:S(2)}) collective-permute-start(f32[256,1024]{1,0:T(8,128)S(1)} %get-tuple-element.290), channel_id=1, source_target_pairs={{0,1},{1,0},{2,3},{3,2},{4,5},{5,4},{6,7},{7,6},{8,9},{9,8},{10,11... | collective-permute-start | bytes 3145736 | tf_op jit(solution)/shard_map/ppermute | solution.py:28
  83.3 20.6 %collective-permute-start.28 = (s16[144,1024]{1,0:T(8,128)(2,1)S(1)}, s16[144,1024]{1,0:T(8,128)(2,1)S(1)}, u32[]{:S(2)}, u32[]{:S(2)}) collective-permute-start(s16[144,1024]{1,0:T(8,128)(2,1)S(1)} %get-tuple-element.292), channel_id=1, source_target_pairs={{0,8},{4,12},{8,0},{12,4},{1,9},{5,13},{9,1},{13,5},{2,10},{6,14},... | collective-permute-start | bytes 884744 | tf_op jit(solution)/shard_map/ppermute | solution.py:28
  86.5 24.8 %collective-permute-start.29 = (s16[144,1024]{1,0:T(8,128)(2,1)S(1)}, s16[144,1024]{1,0:T(8,128)(2,1)S(1)}, u32[]{:S(2)}, u32[]{:S(2)}) collective-permute-start(s16[144,1024]{1,0:T(8,128)(2,1)S(1)} %get-tuple-element.293), channel_id=1, source_target_pairs={{0,12},{4,0},{8,4},{12,8},{1,13},{5,1},{9,5},{13,9},{2,14},{6,2},{... | collective-permute-start | bytes 884744 | tf_op jit(solution)/shard_map/ppermute | solution.py:28
  87.6 26.5 %copy-start = (s32[1,2048]{1,0:T(1,128)S(1)}, s32[1,2048]{1,0:T(1,128)}, u32[]{:S(2)}) copy-start(s32[1,2048]{1,0:T(1,128)} %ids_ref.1) | copy-start | bytes 24580
  87.6 26.5 %copy-start.1 = (s32[2,512]{1,0:T(2,128)S(1)}, s32[2,512]{1,0:T(2,128)}, u32[]{:S(2)}) copy-start(s32[2,512]{1,0:T(2,128)} %refs_0_.1) | copy-start | bytes 12292
  87.6 23.6 %collective-permute-start.30 = (s16[144,1024]{1,0:T(8,128)(2,1)S(1)}, s16[144,1024]{1,0:T(8,128)(2,1)S(1)}, u32[]{:S(2)}, u32[]{:S(2)}) collective-permute-start(s16[144,1024]{1,0:T(8,128)(2,1)S(1)} %get-tuple-element.294), channel_id=1, source_target_pairs={{0,4},{4,8},{8,12},{12,0},{1,5},{5,9},{9,13},{13,1},{2,6},{6,10},{... | collective-permute-start | bytes 884744 | tf_op jit(solution)/shard_map/ppermute | solution.py:28
